TPU v7x, 32 devices: a whole 2x2x4 slice. The times are simulated.
32 devices in a mesh: job: 4 (over y, core), seq: 8 (over z, x).
Axes of the slice: x: 2, y: 2, z: 4, core: 2. Of those that a mesh axis runs over, the one named last changes fastest.
Arguments:
- video: bfloat16 [4, 1024, 3072], P('job', 'seq'), may hold values from -6 to 6
- text_cache: bfloat16 [4, 256, 4096], P('job', 'seq'), may hold values from -6 to 6
- text_count: int32 [4], replicated, may hold values from 129 to 256, as said below
- holder: int32 [4], replicated, may hold values from 0 to 3, each once
- text_splits: int32 [4, 8], replicated, may hold values from 0 to 64, as said below
- mod_shift: float32 [4, 3072], replicated, may hold values from -3 to 3
- mod_scale: float32 [4, 3072], replicated, may hold values from -2 to 2
- mod_gate: float32 [4, 3072], replicated, may hold values from -4 to 4
- text_gain: float32 [4096], replicated, may hold values from 0.25 to 1.75
- refine_w: bfloat16 [4096, 3072], P(None, 'job'), may hold values from -0.09375 to 0.09375
- refine_bias: float32 [3072], P('job'), may hold values from -3 to 3
- w_qkv: bfloat16 [3072, 16, 3, 128], P(None, 'job'), may hold values from -0.109375 to 0.109375
- q_gain: float32 [16, 128], P('job'), may hold values from 0.85 to 9.2
- k_gain: float32 [16, 128], P('job'), may hold values from 0.85 to 9.2
- w_out: bfloat16 [16, 128, 3072], P('job'), may hold values from -0.125 to 0.125
Outputs:
- video_out: bfloat16 [4, 1024, 3072], P('job', 'seq')
- text_out: bfloat16 [4, 512, 3072], P('job', 'seq')
Inputs may be any that keep to these rules, and one draw needn't show every extreme that they name: `text_count`: 256 is reached by some job in every draw. `text_splits`: for each job the entries over the 8 shards add up to text_count of that job; some shard holds exactly 64 rows in every draw.
All inputs are finite; a program needn't handle non-finite values.
Results may differ from a plain program's by a relative error of at most 0.012.
The roundings to bfloat16 on the way count: a program that leaves them out, or rounds other values in their place, can miss the bound.
Values may be sent and summed in bfloat16 or wider, within the bound.
No kernel may reach another device: no remote copies, remote signals or barrier semaphores. Data moves between devices by JAX's collectives and lax.ppermute only.
A program may use at most 64 MiB of HBM per device.

v0:
```python
import jax
import jax.numpy as jnp
from jax import lax
from jax.sharding import PartitionSpec as P

HD = 128
TXT = 256


epsilon = 1e-06


def rms_scale(values, gains):
    mean_square = jnp.mean(values * values, axis=-1, keepdims=True)
    return values * lax.rsqrt(mean_square + epsilon) * gains


def modulate(tokens, shift_part, scale_part):
    widened = tokens.astype(jnp.float32)
    centre = jnp.mean(widened, axis=-1, keepdims=True)
    spread_sq = jnp.mean((widened - centre) ** 2, axis=-1, keepdims=True)
    normed = (widened - centre) * lax.rsqrt(spread_sq + epsilon)
    return (normed * (1.0 + scale_part) + shift_part).astype(jnp.bfloat16)


def refine_rows(raw_text, text_gain, refine_w, refine_bias):
    normed = rms_scale(raw_text.astype(jnp.float32), text_gain).astype(jnp.bfloat16)
    lifted = jnp.einsum("jrt,tc->jrc", normed, refine_w, preferred_element_type=jnp.float32)
    return (lifted + refine_bias).astype(jnp.bfloat16)


def project_heads(modded, w_qkv, q_gain, k_gain):
    projections = jnp.einsum("jrd,dhce->jrhce", modded, w_qkv, preferred_element_type=jnp.float32)
    queries = rms_scale(projections[:, :, :, 0], q_gain).astype(jnp.bfloat16)
    key_rows = rms_scale(projections[:, :, :, 1], k_gain).astype(jnp.bfloat16)
    values = projections[:, :, :, 2].astype(jnp.bfloat16)
    return jnp.stack([queries, key_rows, values], axis=3)


def query_block(query_count, unit_rows):
    unit_total = query_count // unit_rows
    for factor in range(1, unit_total + 1):
        if unit_total % factor == 0 and factor * unit_rows >= 512:
            return factor * unit_rows
    return query_count


def attend(queries, key_rows, values, key_ok, block_rows):
    query_count = queries.shape[0]
    stacked_blocks = queries.reshape(query_count // block_rows, block_rows, queries.shape[1])
    scale_factor = HD ** (-0.5)

    def one_block(query_part):
        scores = (
            jnp.einsum("qe,ke->qk", query_part, key_rows, preferred_element_type=jnp.float32)
            * scale_factor
        )
        scores = jnp.where(key_ok[None, :], scores, -1e30)
        highest = jnp.max(scores, axis=-1, keepdims=True)
        weights = jnp.exp(scores - highest)
        summed = jnp.sum(weights, axis=-1, keepdims=True)
        weights = (weights / summed).astype(jnp.bfloat16)
        return jnp.dot(weights, values, preferred_element_type=jnp.float32).astype(jnp.bfloat16)

    return lax.map(one_block, stacked_blocks).reshape(query_count, queries.shape[1])


def body(
    video,
    text_cache,
    text_count,
    holder,
    text_splits,
    mod_shift,
    mod_scale,
    mod_gate,
    text_gain,
    refine_w,
    refine_bias,
    w_qkv,
    q_gain,
    k_gain,
    w_out,
):
    job_count = lax.axis_size("job")
    shard_count = lax.axis_size("seq")
    my_job = lax.axis_index("job")
    my_shard = lax.axis_index("seq")
    video_rows = video.shape[1]
    block_rows = text_cache.shape[1]
    slot_count = 2 * block_rows
    row_count = video_rows + slot_count
    group_size = w_qkv.shape[1]
    pair_count = job_count * group_size
    slot_total = max(pair_count, shard_count)
    repeat_count = slot_total // pair_count
    per_device = slot_total // shard_count
    offsets = jnp.cumsum(text_splits, axis=1) - text_splits
    slot_ids = jnp.arange(slot_count, dtype=jnp.int32)
    my_offsets = lax.dynamic_index_in_dim(offsets, my_shard, 1, keepdims=False)
    my_splits = lax.dynamic_index_in_dim(text_splits, my_shard, 1, keepdims=False)
    slot_valid = (slot_ids[None, :] < my_splits[:, None]) & (
        my_offsets[:, None] + slot_ids[None, :] < text_count[:, None]
    )
    position = holder[:, None] * (TXT + slot_count) + my_offsets[:, None] + slot_ids[None, :]
    cache_rows = lax.all_gather(text_cache, "job", axis=0, tiled=True)
    refined = refine_rows(cache_rows, text_gain, refine_w, refine_bias)
    gathered_text = lax.all_gather(refined, "seq", axis=1, tiled=True)
    width = gathered_text.shape[2]
    padded = jnp.concatenate(
        [
            gathered_text,
            jnp.zeros((gathered_text.shape[0], slot_count, width), gathered_text.dtype),
        ],
        axis=1,
    )
    flat_rows = padded.reshape(-1, width)
    chosen = jnp.take(flat_rows, position.reshape(-1), axis=0).reshape(job_count, slot_count, width)
    text_cols = jnp.where(slot_valid[:, :, None], chosen, jnp.zeros_like(chosen))
    text_full = lax.all_gather(text_cols, "job", axis=2, tiled=True)
    modded = modulate(
        lax.all_gather(video, "job", axis=0, tiled=True),
        mod_shift[:, None, :],
        mod_scale[:, None, :],
    )
    video_heads = project_heads(modded, w_qkv, q_gain, k_gain)
    text_modded = modulate(text_full, mod_shift[:, None, :], mod_scale[:, None, :])
    text_heads = project_heads(text_modded, w_qkv, q_gain, k_gain)
    heads_all = jnp.concatenate([video_heads, text_heads], axis=1)
    by_row = jnp.transpose(heads_all, (1, 0, 2, 3, 4)).reshape(row_count, pair_count, 3, HD)
    query_rows = by_row[:, :, 0]
    key_rows = jnp.tile(by_row[:, :, 1], (1, repeat_count, 1))
    value_rows = jnp.tile(by_row[:, :, 2], (1, repeat_count, 1))
    query_send = jnp.tile(query_rows, (1, repeat_count, 1))
    query_recv, key_recv, value_recv = (
        lax.all_to_all(query_send, "seq", split_axis=1, concat_axis=0, tiled=True),
        lax.all_to_all(key_rows, "seq", split_axis=1, concat_axis=0, tiled=True),
        lax.all_to_all(value_rows, "seq", split_axis=1, concat_axis=0, tiled=True),
    )
    my_part = my_shard * per_device // pair_count
    outputs = []
    for slot_index in range(per_device):
        slot_global = my_shard * per_device + slot_index
        job_of_slot = slot_global % pair_count // group_size
        splits_row = lax.dynamic_index_in_dim(text_splits, job_of_slot, 0, keepdims=False)
        offsets_row = lax.dynamic_index_in_dim(offsets, job_of_slot, 0, keepdims=False)
        count_of_job = lax.dynamic_index_in_dim(text_count, job_of_slot, 0, keepdims=False)
        key_valid = (slot_ids[None, :] < splits_row[:, None]) & (
            offsets_row[:, None] + slot_ids[None, :] < count_of_job
        )
        key_ok = jnp.concatenate(
            [jnp.ones((shard_count, video_rows), jnp.bool_), key_valid], axis=1
        ).reshape(-1)
        grouped = query_recv[:, slot_index].reshape(
            shard_count // repeat_count, repeat_count, row_count, HD
        )
        queries = lax.dynamic_index_in_dim(grouped, my_part, 1, keepdims=False).reshape(-1, HD)
        block_size = query_block(queries.shape[0], row_count)
        outputs.append(
            attend(queries, key_recv[:, slot_index], value_recv[:, slot_index], key_ok, block_size)
        )
    attended = jnp.stack(outputs, axis=1)
    spread_out = attended.reshape(shard_count // repeat_count, 1, row_count, per_device, HD)
    selector = (
        (jnp.arange(repeat_count) == my_part).astype(jnp.bfloat16).reshape(1, repeat_count, 1, 1, 1)
    )
    send_back = (spread_out * selector).reshape(shard_count * row_count, per_device, HD)
    returned = lax.all_to_all(send_back, "seq", split_axis=0, concat_axis=1, tiled=True)
    own_heads = lax.dynamic_index_in_dim(
        returned.reshape(row_count, repeat_count, pair_count, HD),
        my_shard % repeat_count,
        1,
        keepdims=False,
    )
    per_job = jnp.transpose(
        own_heads.reshape(row_count, job_count, group_size * HD), (1, 0, 2)
    ).reshape(job_count * row_count, group_size * HD)
    out_weight = w_out.reshape(group_size * HD, w_out.shape[2])
    projected = lax.psum_scatter(
        jnp.dot(per_job, out_weight, preferred_element_type=jnp.float32).astype(jnp.bfloat16),
        "job",
        scatter_dimension=0,
        tiled=True,
    ).astype(jnp.float32)
    own_rows = jnp.concatenate(
        [video[0], lax.dynamic_index_in_dim(text_full, my_job, 0, keepdims=False)], axis=0
    )
    gate_row = lax.dynamic_index_in_dim(mod_gate, my_job, 0, keepdims=False)
    result = (own_rows.astype(jnp.float32) + gate_row * projected).astype(jnp.bfloat16)
    own_valid = lax.dynamic_index_in_dim(slot_valid, my_job, 0, keepdims=False)
    text_result = jnp.where(
        own_valid[:, None], result[video_rows:], jnp.zeros_like(result[video_rows:])
    )
    return (result[:video_rows][None], text_result[None])


def solution(mesh):
    placed = (
        P("job", "seq", None),
        P("job", "seq", None),
        P(),
        P(),
        P(),
        P(),
        P(),
        P(),
        P(),
        P(None, "job"),
        P("job"),
        P(None, "job", None, None),
        P("job", None),
        P("job", None),
        P("job", None, None),
    )
    return jax.shard_map(
        body,
        mesh=mesh,
        in_specs=placed,
        out_specs=(P("job", "seq", None), P("job", "seq", None)),
        check_vma=False,
    )
```

profile of v0, /device:TPU:0, one launch (start us, length us, event | category | flops | bytes accessed | tf_op | source)
XLA Modules:
  0.0 339.1 jit_solution(4789145008552270287)
XLA Ops:
  8.0 21.1 %all-gather.5.cloned.1.call-done = bf16[4,32,4096]{2,1,0:T(8,128)(2,1)} async-done(((bf16[1,32,4096]{2,1,0:T(8,128)(2,1)}), bf16[4,32,4096]{2,1,0:T(8,128)(2,1)}) %all-gather.5.cloned.1.call-update) | async-done | bytes 1048592 | tf_op jit(solution)/shard_map/all_gather | solution.py:106
  30.6 4.9 %fusion.62 = bf16[4,32,768]{2,1,0:T(8,128)(2,1)} fusion(bf16[4096,768]{1,0:T(8,128)(2,1)} %param.28, bf16[4,32,4096]{2,1,0:T(8,128)(2,1)} %all-gather.5.cloned.1.call-done, f32[4096]{0:T(1024)} %param.27, f32[4,32]{1,0:T(4,128)S(1)} %add_rsqrt_fusion.6, f32[768]{0:T(1024)} %param.29), kind=kOutput, calls=%fused_computation.74 | convolution fusion | flops 807600128 | bytes 7556608 | tf_op jit(solution)/shard_map/jrt,tc->jrc/dot_general | solution.py:28
  38.1 41.7 %all-gather.7.cloned.1.call-done = bf16[4,256,768]{2,1,0:T(8,128)(2,1)} async-done(((bf16[4,32,768]{2,1,0:T(8,128)(2,1)}), bf16[4,256,768]{2,1,0:T(8,128)(2,1)}) %all-gather.7.cloned.1.call-update) | async-done | bytes 1572880 | tf_op jit(solution)/shard_map/all_gather | solution.py:108
  79.8 2.9 concatenate.18
  82.7 3.2 gather_fusion
  87.4 21.3 %all-gather.11.cloned.1.call-done = bf16[4,128,3072]{2,1,0:T(8,128)(2,1)} async-done(((bf16[1,128,3072]{2,1,0:T(8,128)(2,1)}), bf16[4,128,3072]{2,1,0:T(8,128)(2,1)}) %all-gather.11.cloned.1.call-update) | async-done | bytes 3145744 | tf_op jit(solution)/shard_map/all_gather | solution.py:122
  108.7 2.5 convert_reduce_fusion
  112.6 8.8 %fusion.26 = f32[4,128,4,3,128]{4,1,3,2,0:T(8,128)S(1)} fusion(bf16[3072,4,3,128]{3,1,2,0:T(4,128)(2,1)} %param.30, bf16[4,128,3072]{2,1,0:T(8,128)(2,1)S(1)} %copy-done.1, f32[4,3072]{1,0:T(4,128)S(1)} %copy-done.21, f32[4,3072]{1,0:T(4,128)S(1)} %copy-done.12, f32[4,128]{1,0:T(4,128)S(1)} %add_rsqrt_fusion.5, f32[4,128]{1,0:T(4,128)S(1)} %broadcast_multiply_fusion.1), kind=kOutput, calls=%fused_computation.33 | convolution fusion | flops 4841275392 | bytes 15831040 | tf_op jit(solution)/shard_map/jrd,dhce->jrhce/dot_general | solution.py:33
  124.5 5.9 %all-gather.9.cloned.1.call-done = bf16[4,64,3072]{2,1,0:T(8,128)(2,1)} async-done(((bf16[4,64,768]{2,1,0:T(8,128)(2,1)}), bf16[4,64,3072]{2,1,0:T(8,128)(2,1)}) %all-gather.9.cloned.1.call-update) | async-done | bytes 1572880 | tf_op jit(solution)/shard_map/all_gather | solution.py:120
  132.1 2.0 fusion.40
  134.1 7.0 %fusion.24 = f32[4,64,4,3,128]{4,1,3,2,0:T(8,128)S(1)} fusion(bf16[3072,4,3,128]{3,1,2,0:T(4,128)(2,1)} %param.30, bf16[4,64,3072]{2,1,0:T(8,128)(2,1)} %all-gather.9.cloned.1.call-done, f32[4,3072]{1,0:T(4,128)S(1)} %copy-done.21, f32[4,3072]{1,0:T(4,128)S(1)} %copy-done.12, f32[4,64]{1,0:T(4,128)S(1)} %add_rsqrt_fusion.4, ...), kind=kOutput, calls=%fused_computation.31 | convolution fusion | flops 2420637696 | bytes 12683264 | tf_op jit(solution)/shard_map/jrd,dhce->jrhce/dot_general | solution.py:33
  143.2 25.9 %all_to_all.69 = bf16[192,16,128]{2,0,1:T(8,128)(2,1)} all-to-all(bf16[192,16,128]{2,0,1:T(8,128)(2,1)S(1)} %get-tuple-element.104), channel_id=1, replica_groups=mesh['job'=4,'seq'=8] {'seq'}, dimensions={1} | all-to-all | bytes 1572864 | tf_op jit(solution)/shard_map/all_to_all | solution.py:138
  169.1 23.7 %all_to_all.70 = bf16[192,16,128]{2,0,1:T(8,128)(2,1)} all-to-all(bf16[192,16,128]{2,0,1:T(8,128)(2,1)S(1)} %get-tuple-element.105), channel_id=1, replica_groups=mesh['job'=4,'seq'=8] {'seq'}, dimensions={1} | all-to-all | bytes 1572864 | tf_op jit(solution)/shard_map/all_to_all | solution.py:137
  192.8 4.2 %all-to-all-start = ((bf16[192,16,128]{2,0,1:T(8,128)(2,1)}), bf16[192,16,128]{2,0,1:T(8,128)(2,1)}, u32[]{:S(2)}, u32[]{:S(2)}) async-start(bf16[192,16,128]{2,0,1:T(8,128)(2,1)} %get-tuple-element.106), calls=%async_computation | async-start | bytes 1572864 | tf_op jit(solution)/shard_map/all_to_all | solution.py:136
  203.7 12.7 %all-to-all-done = bf16[192,16,128]{2,0,1:T(8,128)(2,1)} async-done(((bf16[192,16,128]{2,0,1:T(8,128)(2,1)}), bf16[192,16,128]{2,0,1:T(8,128)(2,1)}, u32[]{:S(2)}, u32[]{:S(2)}) %all-to-all-start) | async-done | bytes 786464 | tf_op jit(solution)/shard_map/all_to_all | solution.py:136
  219.3 10.4 %while.23 = (s32[]{:T(128)}, bf16[2,768,128]{2,1,0:T(8,128)(2,1)}, pred[8,192]{1,0:T(8,128)(4,1)}, bf16[2,768,128]{2,1,0:T(8,128)(2,1)}, bf16[1536,128]{1,0:T(8,...) while((s32[]{:T(128)}, bf16[2,768,128]{2,1,0:T(8,128)(2,1)}, ...), condition=%wide.wide.region_17.18_spmd, body=%wide.wide.region_14.17_spmd.sunk | while | flops 618232320 | bytes 20076728 | solution.py:65
  219.3 2.1 fusion.113
  224.5 2.1 fusion.113
  230.5 10.1 %while.22 = (s32[]{:T(128)}, bf16[2,768,128]{2,1,0:T(8,128)(2,1)}, pred[8,192]{1,0:T(8,128)(4,1)}, bf16[2,768,128]{2,1,0:T(8,128)(2,1)}, bf16[1536,128]{1,0:T(8,...) while((s32[]{:T(128)}, bf16[2,768,128]{2,1,0:T(8,128)(2,1)}, ...), condition=%wide.wide.region_13.14_spmd, body=%wide.wide.region_10.13_spmd.sunk | while | flops 618232320 | bytes 20076728 | solution.py:65
  241.9 6.5 %copy.58 = bf16[1536,2,128]{2,1,0:T(2,128)(2,1)S(1)} copy(bf16[1536,2,128]{2,0,1:T(8,128)(2,1)S(1)} %maximum_multiply_fusion) | data formatting | bytes 1572864 | tf_op jit(solution)/shard_map/mul | solution.py:167
  248.4 23.6 %all_to_all.71 = bf16[1536,2,128]{2,1,0:T(2,128)(2,1)S(1)} all-to-all(bf16[1536,2,128]{2,1,0:T(2,128)(2,1)S(1)} %copy.58), channel_id=1, replica_groups=mesh['job'=4,'seq'=8] {'seq'}, dimensions={0} | all-to-all | bytes 1572864 | tf_op jit(solution)/shard_map/all_to_all | solution.py:168
  273.8 3.3 reshape.250
  278.4 4.4 %convolution_convert_fusion = bf16[768,3072]{1,0:T(8,128)(2,1)} fusion(bf16[768,512]{1,0:T(8,128)(2,1)S(1)} %bitcast.153, bf16[512,3072]{1,0:T(8,128)(2,1)S(1)} %bitcast.137), kind=kOutput, calls=%fused_computation.47 | convolution fusion | flops 2418278400 | bytes 8650752 | tf_op jit(solution)/shard_map/dot_general | solution.py:180
  285.2 43.6 %reduce-scatter.2.cloned.1.call-done = bf16[192,3072]{1,0:T(8,128)(2,1)} async-done(((bf16[768,3072]{1,0:T(8,128)(2,1)}), bf16[192,3072]{1,0:T(8,128)(2,1)}) %reduce-scatter.2.cloned.1.call-update) | async-done | bytes 1179664 | tf_op jit(solution)/shard_map/reduce_scatter | solution.py:179
  (133 shorter events, 51.6 us)
Async XLA Ops:
  7.2 271.2 %copy-start = (bf16[4,128,3072]{2,1,0:T(8,128)(2,1)S(1)}, bf16[4,128,3072]{2,1,0:T(8,128)(2,1)}, u32[]{:S(2)}) copy-start(bf16[4,128,3072]{2,1,0:T(8,128)(2,1)} %param.33) | copy-start | bytes 9437188
  7.2 21.9 %all-gather.5.cloned.1.call-start = ((), (), s32[]{:S(2)}) async-start(), calls=%async_computation.5 | async-start | bytes 1310720 | tf_op jit(solution)/shard_map/all_gather | solution.py:106
  7.9 28.3 %copy-start.13 = (s32[4,8]{1,0:T(4,128)S(1)}, s32[4,8]{1,0:T(4,128)}, u32[]{:S(2)}) copy-start(s32[4,8]{1,0:T(4,128)} %param.23) | copy-start | bytes 388
  7.9 28.6 %copy-start.20 = (s32[4]{0:T(128)S(1)}, s32[4]{0:T(128)}, u32[]{:S(2)}) copy-start(s32[4]{0:T(128)} %param.22) | copy-start | bytes 52
  7.9 71.9 %all-gather.7.cloned.1.call-start = ((), (), s32[]{:S(2)}) async-start(), calls=%async_computation.6 | async-start | bytes 1769472 | tf_op jit(solution)/shard_map/all_gather | solution.py:108
  30.6 6.2 %copy-start.18 = (s32[4]{0:T(128)S(1)}, s32[4]{0:T(128)}, u32[]{:S(2)}) copy-start(s32[4]{0:T(128)} %param.21) | copy-start | bytes 52
  30.6 6.9 %copy-start.11 = (f32[4,3072]{1,0:T(4,128)S(1)}, f32[4,3072]{1,0:T(4,128)}, u32[]{:S(2)}) copy-start(f32[4,3072]{1,0:T(4,128)} %param.25) | copy-start | bytes 147460
  35.5 73.3 %all-gather.11.cloned.1.call-start = ((), (), s32[]{:S(2)}) async-start(), calls=%async_computation.8 | async-start | bytes 3932160 | tf_op jit(solution)/shard_map/all_gather | solution.py:122
  36.2 94.2 %all-gather.9.cloned.1.call-start = ((), (), s32[]{:S(2)}) async-start(), calls=%async_computation.7 | async-start | bytes 1966080 | tf_op jit(solution)/shard_map/all_gather | solution.py:120
  87.4 25.1 %copy-start.12 = (f32[4,3072]{1,0:T(4,128)S(1)}, f32[4,3072]{1,0:T(4,128)}, u32[]{:S(2)}) copy-start(f32[4,3072]{1,0:T(4,128)} %broadcast_add_fusion) | copy-start | bytes 147460
  87.4 25.1 %copy-start.21 = (f32[4,3072]{1,0:T(4,128)S(1)}, f32[4,3072]{1,0:T(4,128)}, u32[]{:S(2)}) copy-start(f32[4,3072]{1,0:T(4,128)} %param.24) | copy-start | bytes 147460
  112.6 10.4 %copy-start.14 = (f32[4,128]{1,0:T(4,128)S(1)}, f32[4,128]{1,0:T(4,128)}, u32[]{:S(2)}) copy-start(f32[4,128]{1,0:T(4,128)} %param.31) | copy-start | bytes 6148
  112.6 10.4 %copy-start.15 = (f32[4,128]{1,0:T(4,128)S(1)}, f32[4,128]{1,0:T(4,128)}, u32[]{:S(2)}) copy-start(f32[4,128]{1,0:T(4,128)} %param.32) | copy-start | bytes 6148
  134.1 7.8 %copy-start.2 = (bf16[4,128,4,1,128]{4,1,3,2,0:T(8,128)(2,1)S(1)}, bf16[4,128,4,1,128]{4,1,3,2,0:T(8,128)(2,1)}, u32[]{:S(2)}) copy-start(bf16[4,128,4,1,128]{4,1,3,2,0:T(8,128)(2,1)} %slice.110) | copy-start | bytes 1572868
  134.1 7.8 %copy-start.3 = (bf16[4,128,4,1,128]{4,1,3,2,0:T(8,128)(2,1)S(1)}, bf16[4,128,4,1,128]{4,1,3,2,0:T(8,128)(2,1)}, u32[]{:S(2)}) copy-start(bf16[4,128,4,1,128]{4,1,3,2,0:T(8,128)(2,1)} %get-tuple-element.102) | copy-start | bytes 1572868
  134.1 7.8 %copy-start.4 = (bf16[4,128,4,1,128]{4,1,3,2,0:T(8,128)(2,1)S(1)}, bf16[4,128,4,1,128]{4,1,3,2,0:T(8,128)(2,1)}, u32[]{:S(2)}) copy-start(bf16[4,128,4,1,128]{4,1,3,2,0:T(8,128)(2,1)} %get-tuple-element.103) | copy-start | bytes 1572868
  192.8 23.6 %all-to-all-start = ((bf16[192,16,128]{2,0,1:T(8,128)(2,1)}), bf16[192,16,128]{2,0,1:T(8,128)(2,1)}, u32[]{:S(2)}, u32[]{:S(2)}) async-start(bf16[192,16,128]{2,0,1:T(8,128)(2,1)} %get-tuple-element.106), calls=%async_computation | async-start | bytes 1572864 | tf_op jit(solution)/shard_map/all_to_all | solution.py:136
  197.0 131.9 %reduce-scatter.2.cloned.1.call-start = ((), (), s32[]{:S(2)}) async-start(), calls=%async_computation.9 | async-start | bytes 5898240 | tf_op jit(solution)/shard_map/reduce_scatter | solution.py:179
  199.4 19.2 %copy-start.16 = (pred[8,192]{1,0:T(8,128)(4,1)}, pred[8,192]{1,0:T(8,128)(4,1)S(1)}, u32[]{:S(2)}) copy-start(pred[8,192]{1,0:T(8,128)(4,1)S(1)} %concatenate.20) | copy-start | bytes 4612
  199.4 19.1 %copy-start.17 = (pred[8,192]{1,0:T(8,128)(4,1)}, pred[8,192]{1,0:T(8,128)(4,1)S(1)}, u32[]{:S(2)}) copy-start(pred[8,192]{1,0:T(8,128)(4,1)S(1)} %concatenate.22) | copy-start | bytes 4612
  219.3 3.1 copy-start.7
  219.3 3.1 copy-start.10
  224.5 3.1 copy-start.7
  224.5 3.1 copy-start.10
  (10 other events, 18.4 us)
Sparse Core Ops, SparseCore 0:
  9.6 19.4 all-gather.4
  35.6 44.1 all-gather.6
  81.4 27.3 all-gather.10
  110.7 19.6 all-gather.8
  282.9 45.9 reduce-scatter.1
where the time goes:
time: 340 us; the launch traced here: 339 us
  waiting for transfers between devices  148 us (44%)
  blocking collectives  73.1 us (21%)
  matrix products  38.3 us (11%)
  local copies, waits for them, and re-layouts  36.9 us (11%)
  other arithmetic  24.3 us (7%)
  between operations  14.2 us (4%)
  starting transfers between devices  4.41 us (1%)
    reduce_scatter x1, waiting for transfers between devices, body(): lax.psum_scatter(jnp.dot(per_job, out_weight, preferred_element_type=jnp....  43.6 us
    all_gather x1, waiting for transfers between devices, body(): gathered_text = lax.all_gather(refined, 'seq', axis=1, tiled=True)  41.7 us
    all_to_all x1, blocking collectives, body(): lax.all_to_all(value_rows, 'seq', split_axis=1, concat_axis=0, tiled=True)  25.9 us
    all_to_all x1, blocking collectives, body(): lax.all_to_all(key_rows, 'seq', split_axis=1, concat_axis=0, tiled=True)  23.7 us
    all_to_all x1, blocking collectives, body(): lax.all_to_all(send_back, 'seq', split_axis=0, concat_axis=1, tiled=True)  23.6 us
    all_gather x1, waiting for transfers between devices, body(): lax.all_gather(video, 'job', axis=0, tiled=True)  21.3 us
    all_gather x1, waiting for transfers between devices, body(): cache_rows = lax.all_gather(text_cache, 'job', axis=0, tiled=True)  21.1 us
    dot_general x2, matrix products, project_heads(): jnp.einsum('jrd,dhce->jrhce', modded, w_qkv, preferred_element_type=jnp.f...  15.8 us
  transfers between devices with their start and end apart: 6, of which 6 were waited for; matrix products, arithmetic and copies ran while one was open for 10% of the time, Pallas kernels for 0%

commit v1 on v0

--- a/solution.py
+++ b/solution.py
@@ -1,6 +1,10 @@
+import functools
+
 import jax
 import jax.numpy as jnp
 from jax import lax
+from jax.experimental import pallas as pl
+from jax.experimental.pallas import tpu as pltpu
 from jax.sharding import PartitionSpec as P
 
 HD = 128
@@ -65,7 +69,7 @@
     return lax.map(one_block, stacked_blocks).reshape(query_count, queries.shape[1])
 
 
-def body(
+def general_body(
     video,
     text_cache,
     text_count,
@@ -194,6 +198,340 @@
     return (result[:video_rows][None], text_result[None])
 
 
+def vmem_spec():
+    return pl.BlockSpec(memory_space=pltpu.VMEM)
+
+
+def smem_spec():
+    return pl.BlockSpec(memory_space=pltpu.SMEM)
+
+
+def params(mib, grid_dims=0):
+    semantics = ("arbitrary",) * grid_dims if grid_dims else None
+    return pltpu.CompilerParams(vmem_limit_bytes=mib << 20, dimension_semantics=semantics)
+
+
+def text_kernel(where_ref, parts_ref, shift_ref, scale_ref, modded_ref, own_ref, rows_ref):
+    mine = where_ref[0]
+    jobs, _, rows, width = parts_ref.shape
+    for r in range(jobs):
+        slot = where_ref[1 + r]
+        for b in range(jobs):
+            rows_ref[:, b * width : (b + 1) * width] = parts_ref[mine ^ b, slot ^ b]
+        raw = rows_ref[...]
+        if r == 0:
+            own_ref[...] = raw
+        modded_ref[r * rows : (r + 1) * rows] = modulate(
+            raw, shift_ref[r : r + 1], scale_ref[r : r + 1]
+        )
+
+
+def text_rows_of_jobs(where, parts, shift_rel, scale_rel):
+    jobs, _, rows, width = parts.shape
+    full = jobs * width
+    return pl.pallas_call(
+        text_kernel,
+        out_shape=(
+            jax.ShapeDtypeStruct((jobs * rows, full), jnp.bfloat16),
+            jax.ShapeDtypeStruct((rows, full), jnp.bfloat16),
+        ),
+        in_specs=[smem_spec(), vmem_spec(), vmem_spec(), vmem_spec()],
+        out_specs=(vmem_spec(), vmem_spec()),
+        scratch_shapes=[pltpu.VMEM((rows, full), jnp.bfloat16)],
+        compiler_params=params(16),
+        cost_estimate=pl.CostEstimate(flops=10 * jobs * rows * full, bytes_accessed=2 << 20, transcendentals=0),
+    )(where, parts, shift_rel, scale_rel)
+
+
+def qkv_kernel(has_text, *refs):
+    if has_text:
+        a_ref, b_ref, text_ref, shift_ref, scale_ref, w_ref, qg_ref, kg_ref, out_ref, x_ref = refs
+    else:
+        a_ref, b_ref, shift_ref, scale_ref, w_ref, qg_ref, kg_ref, out_ref, x_ref = refs
+    rows = a_ref.shape[0]
+    step = pl.program_id(0)
+
+    @pl.when(step == 0)
+    def _():
+        x_ref[0:rows] = modulate(a_ref[...], shift_ref[0:1], scale_ref[0:1])
+        x_ref[rows : 2 * rows] = modulate(b_ref[...], shift_ref[1:2], scale_ref[1:2])
+        if has_text:
+            x_ref[2 * rows :] = text_ref[...]
+
+    heads = w_ref.shape[1]
+    trows = (x_ref.shape[0] - 2 * rows) // 4
+    for h in range(heads):
+        head = step * heads + h
+        weights = jnp.concatenate([w_ref[0, h], w_ref[1, h], w_ref[2, h]], axis=1)
+        raw = jnp.dot(x_ref[...], weights, preferred_element_type=jnp.float32)
+        queries = rms_scale(raw[:, :HD], qg_ref[pl.ds(head, 1)]).astype(jnp.bfloat16)
+        key_rows = rms_scale(raw[:, HD : 2 * HD], kg_ref[pl.ds(head, 1)]).astype(jnp.bfloat16)
+        values = raw[:, 2 * HD :].astype(jnp.bfloat16)
+        done = jnp.concatenate([queries, key_rows, values], axis=1)
+        for r in range(2):
+            out_ref[r, h, 0:rows] = done[r * rows : (r + 1) * rows]
+            if has_text:
+                base = 2 * rows + r * trows
+                out_ref[r, h, rows : rows + trows] = done[base : base + trows]
+                base = 2 * rows + (2 + r) * trows
+                out_ref[r, h, rows + trows :] = done[base : base + trows]
+
+
+def project_qkv(pair, text_modded, shift_two, scale_two, weights, q_gain, k_gain):
+    rows, width = pair[0].shape
+    group = weights.shape[1]
+    has_text = text_modded is not None
+    extra = [text_modded] if has_text else []
+    total = 2 * rows + (text_modded.shape[0] if has_text else 0)
+    out_rows = total // 2
+    step_heads = 2
+    return pl.pallas_call(
+        functools.partial(qkv_kernel, has_text),
+        grid=(group // step_heads,),
+        out_shape=jax.ShapeDtypeStruct((2, group, out_rows, 3 * HD), jnp.bfloat16),
+        in_specs=[vmem_spec()] * (4 + len(extra))
+        + [pl.BlockSpec((3, step_heads, width, HD), lambda i: (0, i, 0, 0)), vmem_spec(), vmem_spec()],
+        out_specs=pl.BlockSpec((2, step_heads, out_rows, 3 * HD), lambda i: (0, i, 0, 0)),
+        scratch_shapes=[pltpu.VMEM((total, width), jnp.bfloat16)],
+        compiler_params=params(40, 1),
+        cost_estimate=pl.CostEstimate(
+            flops=2 * total * width * group * 3 * HD,
+            bytes_accessed=2 * group * 3 * HD * width + 4 * total * width,
+            transcendentals=0,
+        ),
+    )(*pair, *extra, shift_two, scale_two, weights, q_gain, k_gain)
+
+
+def attention_kernel(text_base, meta_ref, video_ref, text_ref, out_ref, k_ref, v_ref, t_ref):
+    shards, _, _ = video_ref.shape
+    vrows = 128
+    trows = t_ref.shape[0] // shards
+    slots = out_ref.shape[1] - vrows
+    video = shards * vrows
+    total = k_ref.shape[0]
+    for s in range(shards):
+        k_ref[s * vrows : (s + 1) * vrows] = video_ref[s, 0:vrows, HD : 2 * HD]
+        v_ref[s * vrows : (s + 1) * vrows] = video_ref[s, 0:vrows, 2 * HD :]
+        lo = video + s * trows
+        k_ref[lo : lo + trows] = text_ref[s, text_base : text_base + trows, HD : 2 * HD]
+        v_ref[lo : lo + trows] = text_ref[s, text_base : text_base + trows, 2 * HD :]
+    column = lax.broadcasted_iota(jnp.int32, (1, total), 1)
+    key_ok = column < video + meta_ref[0]
+    scale = HD ** (-0.5)
+
+    def one_block(queries):
+        scores = lax.dot_general(
+            queries, k_ref[...], (((1,), (1,)), ((), ())), preferred_element_type=jnp.float32
+        )
+        scores = jnp.where(key_ok, scores * scale, -1e30)
+        weights = jnp.exp(scores - jnp.max(scores, axis=-1, keepdims=True))
+        summed = jnp.sum(weights, axis=-1, keepdims=True)
+        mixed = jnp.dot(weights.astype(jnp.bfloat16), v_ref[...], preferred_element_type=jnp.float32)
+        return (mixed / summed).astype(jnp.bfloat16)
+
+    def video_block(i, carry):
+        done = one_block(video_ref[pl.ds(2 * i, 2), 0:vrows, 0:HD].reshape(2 * vrows, HD))
+        out_ref[pl.ds(2 * i, 2), 0:vrows] = done.reshape(2, vrows, HD)
+        return carry
+
+    lax.fori_loop(0, shards // 2, video_block, 0)
+    t_ref[...] = one_block(
+        text_ref[:, text_base : text_base + trows, 0:HD].reshape(shards * trows, HD)
+    )
+    slot = lax.broadcasted_iota(jnp.int32, (slots, shards * trows), 0)
+    row = lax.broadcasted_iota(jnp.int32, (slots, shards * trows), 1)
+    for s in range(shards):
+        chosen = (row == slot + meta_ref[1 + s]) & (slot < meta_ref[1 + shards + s])
+        chosen = jnp.where(chosen, 1.0, 0.0).astype(jnp.bfloat16)
+        out_ref[s, vrows:] = jnp.dot(
+            chosen, t_ref[...], preferred_element_type=jnp.float32
+        ).astype(jnp.bfloat16)
+
+
+def attend_pair(meta, video_qkv, text_qkv, text_base, trows, slots):
+    shards = video_qkv.shape[0]
+    vrows = 128
+    total = shards * (vrows + trows)
+    return pl.pallas_call(
+        functools.partial(attention_kernel, text_base),
+        out_shape=jax.ShapeDtypeStruct((shards, vrows + slots, HD), jnp.bfloat16),
+        in_specs=[smem_spec(), vmem_spec(), vmem_spec()],
+        out_specs=vmem_spec(),
+        scratch_shapes=[
+            pltpu.VMEM((total, HD), jnp.bfloat16),
+            pltpu.VMEM((total, HD), jnp.bfloat16),
+            pltpu.VMEM((shards * trows, HD), jnp.bfloat16),
+        ],
+        compiler_params=params(40),
+        cost_estimate=pl.CostEstimate(
+            flops=4 * total * total * HD, bytes_accessed=3 << 20, transcendentals=total * total
+        ),
+    )(meta, video_qkv, text_qkv)
+
+
+def out_kernel(heads_ref, w_ref, out_ref):
+    jobs, group, _, _ = heads_ref.shape
+    for r in range(jobs):
+        rows = jnp.concatenate([heads_ref[r, h] for h in range(group)], axis=1)
+        out_ref[r] = jnp.dot(rows, w_ref[...], preferred_element_type=jnp.float32).astype(jnp.bfloat16)
+
+
+def project_out(heads, weights):
+    jobs, group, rows, _ = heads.shape
+    depth, width = weights.shape
+    cols = 768
+    return pl.pallas_call(
+        out_kernel,
+        grid=(width // cols,),
+        out_shape=jax.ShapeDtypeStruct((jobs, rows, width), jnp.bfloat16),
+        in_specs=[vmem_spec(), pl.BlockSpec((depth, cols), lambda i: (0, i))],
+        out_specs=pl.BlockSpec((jobs, rows, cols), lambda i: (0, 0, i)),
+        compiler_params=params(40, 1),
+        cost_estimate=pl.CostEstimate(
+            flops=2 * jobs * rows * depth * width, bytes_accessed=8 << 20, transcendentals=0
+        ),
+    )(heads, weights)
+
+
+def two_wave_body(
+    video,
+    text_cache,
+    text_count,
+    holder,
+    text_splits,
+    mod_shift,
+    mod_scale,
+    mod_gate,
+    text_gain,
+    refine_w,
+    refine_bias,
+    w_qkv,
+    q_gain,
+    k_gain,
+    w_out,
+):
+    job_count = lax.axis_size("job")
+    shard_count = lax.axis_size("seq")
+    my_job = lax.axis_index("job")
+    my_shard = lax.axis_index("seq")
+    group_size = w_qkv.shape[1]
+    trows = text_cache.shape[1]
+    slot_count = 2 * trows
+    vrows = video.shape[1]
+
+    def to_core(x):
+        return lax.ppermute(x, "job", [(i, i ^ 1) for i in range(job_count)])
+
+    def to_chip(x):
+        return lax.ppermute(x, "job", [(i, i ^ 2) for i in range(job_count)])
+
+    def over_seq(x):
+        return lax.all_to_all(x, "seq", split_axis=0, concat_axis=0, tiled=False)
+
+    def pick(array, index):
+        return lax.dynamic_index_in_dim(array, index, 0, keepdims=False)
+
+    offsets = jnp.cumsum(text_splits, axis=1) - text_splits
+    jobs_rel = [my_job ^ r for r in range(job_count)]
+    shift_rel = jnp.stack([pick(mod_shift, j) for j in jobs_rel])
+    scale_rel = jnp.stack([pick(mod_scale, j) for j in jobs_rel])
+    qkv_w = jnp.transpose(w_qkv, (2, 1, 0, 3))
+
+    own_video = video[0]
+    core_video = to_core(own_video)
+
+    normed = rms_scale(text_cache[0].astype(jnp.float32), text_gain).astype(jnp.bfloat16)
+    normed_core = to_core(normed)
+    normed_chip = to_chip(normed)
+    normed_both = to_core(normed_chip)
+    lifted = jnp.dot(
+        jnp.concatenate([normed, normed_core, normed_chip, normed_both], axis=0),
+        refine_w,
+        preferred_element_type=jnp.float32,
+    )
+    refined = (lifted + refine_bias).astype(jnp.bfloat16).reshape(job_count, trows, -1)
+    refined_core = to_core(refined)
+    refined_chip = to_chip(refined)
+    refined_both = to_core(refined_chip)
+    parts = jnp.stack([refined, refined_core, refined_chip, refined_both])
+    where = jnp.stack([my_job] + [pick(holder, j) for j in jobs_rel]).astype(jnp.int32)
+    text_modded, own_text = text_rows_of_jobs(where, parts, shift_rel, scale_rel)
+    job_text = lax.all_gather(own_text, "seq", axis=0, tiled=True)
+
+    local_send = project_qkv(
+        (own_video, core_video), None, shift_rel[:2], scale_rel[:2], qkv_w, q_gain, k_gain
+    )
+    local_qkv = over_seq(local_send.reshape(shard_count, vrows, 3 * HD))
+    chip_video = to_chip(own_video)
+    both_video = to_core(chip_video)
+    remote_send = project_qkv(
+        (chip_video, both_video), text_modded, shift_rel[2:], scale_rel[2:], qkv_w, q_gain, k_gain
+    )
+    remote_qkv = over_seq(remote_send.reshape(shard_count, vrows + 2 * trows, 3 * HD))
+
+    half = my_shard // group_size
+    out_weight = w_out.reshape(group_size * HD, w_out.shape[2])
+
+    def meta_of(job):
+        return jnp.concatenate(
+            [pick(text_count, job)[None], pick(offsets, job), pick(text_splits, job)]
+        ).astype(jnp.int32)
+
+    remote_mixed = attend_pair(
+        meta_of(my_job ^ half ^ 2), remote_qkv, remote_qkv, vrows + trows, trows, slot_count
+    )
+    remote_back = over_seq(remote_mixed)
+    local_qkv, _ = lax.optimization_barrier((local_qkv, remote_mixed))
+    local_mixed = attend_pair(
+        meta_of(my_job ^ half), local_qkv, remote_qkv, vrows, trows, slot_count
+    )
+    local_back = over_seq(local_mixed)
+    row_count = vrows + slot_count
+    remote_part = project_out(
+        remote_back.reshape(2, group_size, row_count, HD), out_weight
+    )
+    from_core = to_core(remote_part[1])
+    crossing = (remote_part[0].astype(jnp.float32) + from_core.astype(jnp.float32)).astype(
+        jnp.bfloat16
+    )
+    from_chip = to_chip(crossing)
+    local_part = project_out(local_back.reshape(2, group_size, row_count, HD), out_weight)
+    local_core = to_core(local_part[1])
+
+    projected = (
+        local_part[0].astype(jnp.float32)
+        + local_core.astype(jnp.float32)
+        + from_chip.astype(jnp.float32)
+    )
+    my_offset = pick(pick(offsets, my_job), my_shard)
+    my_split = pick(pick(text_splits, my_job), my_shard)
+    slot_ids = jnp.arange(slot_count, dtype=jnp.int32)
+    own_valid = (slot_ids < my_split) & (my_offset + slot_ids < pick(text_count, my_job))
+    padded = jnp.pad(job_text, ((0, slot_count), (0, 0)))
+    slot_rows = lax.dynamic_slice_in_dim(padded, my_offset, slot_count, 0)
+    gate_row = pick(mod_gate, my_job)
+    video_result = own_video.astype(jnp.float32) + gate_row * projected[:vrows]
+    text_result = slot_rows.astype(jnp.float32) + gate_row * projected[vrows:]
+    text_result = jnp.where(own_valid[:, None], text_result, 0.0)
+    return (
+        video_result.astype(jnp.bfloat16)[None],
+        text_result.astype(jnp.bfloat16)[None],
+    )
+
+
+def body(*arrays):
+    video, text_cache, w_qkv = arrays[0], arrays[1], arrays[11]
+    job_count = lax.axis_size("job")
+    shard_count = lax.axis_size("seq")
+    fits = (
+        job_count == 4
+        and shard_count == 2 * w_qkv.shape[1]
+        and video.shape[1] == 128
+        and text_cache.shape[1] == 32
+    )
+    return (two_wave_body if fits else general_body)(*arrays)
+
+
 def solution(mesh):
     placed = (
         P("job", "seq", None),

time: 340 us -> 202 us (0.59)
  blocking collectives: 73.1 us -> 0 us
  waiting for transfers between devices: 148 us -> 81.7 us
  matrix products: 38.3 us -> 3.96 us
  Pallas kernels: 0 us -> 33.3 us
  starting transfers between devices: 4.41 us -> 26 us
  other arithmetic: 24.3 us -> 13.5 us
  local copies, waits for them, and re-layouts: 36.9 us -> 26.4 us
    all_gather x4 -> x1, waiting for transfers between devices: 90 us -> 13.9 us  [two_wave_body(): job_text = lax.all_gather(own_text, 'seq', axis=0, tiled=True)]
    all_to_all x3 -> x0, blocking collectives: 73.1 us -> none  [the longest x1 25.9 us: body(): lax.all_to_all(value_rows, 'seq', split_axis=1, concat_axis=0, tiled=True)]
    reduce_scatter x1 -> x0, waiting for transfers between devices: 43.6 us -> none  [body(): lax.psum_scatter(jnp.dot(per_job, out_weight, preferred_element_type=jnp....]
    dot_general x12 -> x1, matrix products: 38.3 us -> 3.96 us  [two_wave_body(): jnp.dot(jnp.concatenate([normed, normed_core, normed_chip, normed_both],...]
    pallas_call x0 -> x7, Pallas kernels: none -> 33.3 us  [the longest x2 14.4 us: project_qkv(): pl.pallas_call(functools.partial(qkv_kernel, has_text), grid=(group // st...]
    ppermute x0 -> x12, waiting for transfers between devices: none -> 30.8 us  [the longest x4 26.1 us: to_chip(): return lax.ppermute(x, 'job', [(i, i ^ 2) for i in range(job_count)])]
    all_to_all x1 -> x4, waiting for transfers between devices: 12.7 us -> 37 us  [over_seq(): return lax.all_to_all(x, 'seq', split_axis=0, concat_axis=0, tiled=False)]
    unnamed x33 -> x45, local copies, waits for them, and re-layouts: 1.08 us -> 20.6 us
  transfers between devices with their start and end apart: 6 -> 17, of which waited for: 6 -> 11; matrix products, arithmetic and copies ran while one was open for 10% -> 14% of each run, Pallas kernels for 0% -> 13%
where the time goes in v1:
time: 202 us; the launch traced here: 201 us
  waiting for transfers between devices  81.7 us (40%)
  Pallas kernels  33.3 us (16%)
  local copies, waits for them, and re-layouts  26.4 us (13%)
  starting transfers between devices  26 us (13%)
  between operations  16.3 us (8%)
  other arithmetic  13.5 us (7%)
  matrix products  3.96 us (2%)
    all_to_all x4, waiting for transfers between devices, over_seq(): return lax.all_to_all(x, 'seq', split_axis=0, concat_axis=0, tiled=False)  37 us
    ppermute x4, waiting for transfers between devices, to_chip(): return lax.ppermute(x, 'job', [(i, i ^ 2) for i in range(job_count)])  26.1 us
    unnamed x45, local copies, waits for them, and re-layouts  20.6 us
    all_to_all x4, starting transfers between devices, over_seq(): return lax.all_to_all(x, 'seq', split_axis=0, concat_axis=0, tiled=False)  18.1 us
    pallas_call x2, Pallas kernels, project_qkv(): pl.pallas_call(functools.partial(qkv_kernel, has_text), grid=(group // st...  14.4 us
    all_gather x1, waiting for transfers between devices, two_wave_body(): job_text = lax.all_gather(own_text, 'seq', axis=0, tiled=True)  13.9 us
    pallas_call x2, Pallas kernels, attend_pair(): pl.pallas_call(functools.partial(attention_kernel, text_base), out_shape=...  11 us
    ppermute x4, starting transfers between devices, to_chip(): return lax.ppermute(x, 'job', [(i, i ^ 2) for i in range(job_count)])  6.71 us
  transfers between devices with their start and end apart: 17, of which 11 were waited for; matrix products, arithmetic and copies ran while one was open for 14% of the time, Pallas kernels for 13%

profile of v1, /device:TPU:0, one launch (start us, length us, event | category | flops | bytes accessed | tf_op | source)
XLA Modules:
  0.0 201.2 jit_solution(10071430359890352113)
XLA Ops:
  9.4 3.0 %collective-permute-start.4 = (bf16[32,4096]{1,0:T(8,128)(2,1)S(1)}, bf16[32,4096]{1,0:T(8,128)(2,1)S(1)}, u32[]{:S(2)}, u32[]{:S(2)}) collective-permute-start(bf16[32,4096]{1,0:T(8,128)(2,1)S(1)} %fusion.18), channel_id=1, source_target_pairs={{0,16},{8,24},{16,0},{24,8},{1,17},{9,25},{17,1},{25,9},{2,18},{10... | collective-permute-start | bytes 786440 | tf_op jit(solution)/shard_map/ppermute | solution.py:426
  12.6 9.0 %copy.19 = bf16[3072,4,3,128]{3,0,1,2:T(8,128)(2,1)} copy(bf16[3072,4,3,128]{3,1,2,0:T(4,128)(2,1)} %param.26) | data formatting | bytes 18874368 | tf_op args[11]
  22.4 2.6 %stack.47.where_ref = s32[5]{0:T(128)S(1)} concatenate(s32[1]{0:T(128)} %bitcast.8, s32[1]{0:T(128)} %get-tuple-element.34, s32[1]{0:T(128)} %get-tuple-element.35, s32[1]{0:T(128)} %get-tuple-element.33, s32[1]{0:T(128)} %get-tuple-element.36), dimensions={0} | concatenate | bytes 40 | tf_op jit(solution)/shard_map/stack | solution.py:457
  26.7 4.0 %fusion.4 = bf16[128,768]{1,0:T(8,128)(2,1)S(1)} fusion(bf16[4096,768]{1,0:T(8,128)(2,1)} %param.24, bf16[32,4096]{1,0:T(8,128)(2,1)S(1)} %collective-permute-done.5, bf16[32,4096]{1,0:T(8,128)(2,1)S(1)} %collective-permute-done.4, bf16[32,4096]{1,0:T(8,128)(2,1)S(1)} %collective-permute-done.3, bf16[32,4096]{1,0:T(8,128)(2,1)S(1)} %fusion.18, ...), kind=kOutput, calls=%fused_computation.14 | convolution fusion | flops 809697280 | bytes 7539712 | tf_op jit(solution)/shard_map/dot_general | solution.py:447
  32.7 3.8 %collective-permute-done.1.refs_0_ = bf16[128,3072]{1,0:T(8,128)(2,1)S(1)} collective-permute-done((bf16[128,3072]{1,0:T(8,128)(2,1)}, bf16[128,3072]{1,0:T(8,128)(2,1)S(1)}, u32[]{:S(2)}, u32[]{:S(2)}) %collective-permute-start.1) | collective-permute-done | bytes 786464 | tf_op jit(solution)/shard_map/ppermute | solution.py:426
  37.0 2.8 %collective-permute-done.7 = bf16[4,32,768]{2,1,0:T(8,128)(2,1)S(1)} collective-permute-done((bf16[4,32,768]{2,1,0:T(8,128)(2,1)S(1)}, bf16[4,32,768]{2,1,0:T(8,128)(2,1)S(1)}, u32[]{:S(2)}, u32[]{:S(2)}) %collective-permute-start.7) | collective-permute-done | bytes 196640 | tf_op jit(solution)/shard_map/ppermute | solution.py:426
  42.7 8.1 %shard_map.160 = bf16[2,4,192,384]{3,2,1,0:T(8,128)(2,1)} custom-call(bf16[128,3072]{1,0:T(8,128)(2,1)S(1)} %collective-permute-done.1.refs_0_, bf16[128,3072]{1,0:T(8,128)(2,1)S(1)} %collective-permute-done.2.refs_1_, bf16[128,3072]{1,0:T(8,128)(2,1)S(1)} %get-tuple-element.5.refs_2_, f32[2,3072]{1,0:T(2,128)S(1)} %pad_maximum_fusion.5.refs_3_, ...), custom_call_target="tpu_custom_call" | custom-call | flops 3623878656 | bytes 14155776 | tf_op jit(solution)/shard_map/pallas_call | solution.py:288
  50.8 6.2 %all-to-all-start.1 = ((bf16[8,192,384]{2,1,0:T(8,128)(2,1)}), bf16[8,192,384]{2,1,0:T(8,128)(2,1)S(1)}, u32[]{:S(2)}, u32[]{:S(2)}) async-start(bf16[8,192,384]{2,1,0:T(8,128)(2,1)} %bitcast.16), calls=%async_computation.1 | async-start | bytes 2359296 | tf_op jit(solution)/shard_map/all_to_all | solution.py:429
  59.3 3.7 %copy-done.2 = bf16[3072,4,3,128]{3,0,1,2:T(8,128)(2,1)S(1)} copy-done((bf16[3072,4,3,128]{3,0,1,2:T(8,128)(2,1)S(1)}, bf16[3072,4,3,128]{3,0,1,2:T(8,128)(2,1)}, u32[]{:S(2)}) %copy-start.2) | copy-done | bytes 9437208
  63.0 6.3 %shard_map.158 = bf16[2,4,128,384]{3,2,1,0:T(8,128)(2,1)} custom-call(bf16[128,3072]{1,0:T(8,128)(2,1)S(1)} %bitcast.57, bf16[128,3072]{1,0:T(8,128)(2,1)S(1)} %collective-permute-done.refs_1_, f32[2,3072]{1,0:T(2,128)S(1)} %pad_maximum_fusion.3.refs_2_, f32[2,3072]{1,0:T(2,128)S(1)} %pad_maximum_fusion.4.refs_3_, bf16[3,4,3072,128]{3,2,1,0:T(8,128)(2,1)S(1)} %bitcast.52, ...), custom_call_target="tpu_custom_call" | custom-call | flops 2415919104 | bytes 12582912 | tf_op jit(solution)/shard_map/pallas_call | solution.py:288
  69.3 16.5 %all-to-all-done.1.video_ref.text_ref = bf16[8,192,384]{2,1,0:T(8,128)(2,1)S(1)} async-done(((bf16[8,192,384]{2,1,0:T(8,128)(2,1)}), bf16[8,192,384]{2,1,0:T(8,128)(2,1)S(1)}, u32[]{:S(2)}, u32[]{:S(2)}) %all-to-all-start.1) | async-done | bytes 1179680 | tf_op jit(solution)/shard_map/all_to_all | solution.py:429
  85.8 3.7 %all-to-all-start = ((bf16[8,128,384]{2,1,0:T(8,128)(2,1)}), bf16[8,128,384]{2,1,0:T(8,128)(2,1)S(1)}, u32[]{:S(2)}, u32[]{:S(2)}) async-start(bf16[8,128,384]{2,1,0:T(8,128)(2,1)} %bitcast.5), calls=%async_computation | async-start | bytes 1572864 | tf_op jit(solution)/shard_map/all_to_all | solution.py:429
  90.5 5.9 %shard_map.161 = bf16[8,192,128]{2,1,0:T(8,128)(2,1)} custom-call(s32[17]{0:T(128)S(1)} %pad_add_fusion.1.meta_ref, bf16[8,192,384]{2,1,0:T(8,128)(2,1)S(1)} %all-to-all-done.1.video_ref.text_ref, bf16[8,192,384]{2,1,0:T(8,128)(2,1)S(1)} %all-to-all-done.1.video_ref.text_ref), custom_call_target="tpu_custom_call" | custom-call | flops 838860800 | bytes 3145728 | tf_op jit(solution)/shard_map/pallas_call | solution.py:355
  96.4 13.5 %all-to-all-done.video_ref = bf16[8,128,384]{2,1,0:T(8,128)(2,1)S(1)} async-done(((bf16[8,128,384]{2,1,0:T(8,128)(2,1)}), bf16[8,128,384]{2,1,0:T(8,128)(2,1)S(1)}, u32[]{:S(2)}, u32[]{:S(2)}) %all-to-all-start) | async-done | bytes 786464 | tf_op jit(solution)/shard_map/all_to_all | solution.py:429
  110.7 4.1 %all-to-all-start.3 = ((bf16[8,192,128]{2,1,0:T(8,128)(2,1)}), bf16[8,192,128]{2,1,0:T(8,128)(2,1)}, u32[]{:S(2)}, u32[]{:S(2)}) async-start(bf16[8,192,128]{2,1,0:T(8,128)(2,1)} %shard_map.161), calls=%async_computation.3 | async-start | bytes 786432 | tf_op jit(solution)/shard_map/all_to_all | solution.py:429
  118.2 5.1 %shard_map.162 = bf16[8,192,128]{2,1,0:T(8,128)(2,1)S(1)} custom-call(s32[17]{0:T(128)S(1)} %pad_add_fusion.meta_ref, bf16[8,128,384]{2,1,0:T(8,128)(2,1)S(1)} %copy-done.12, bf16[8,192,384]{2,1,0:T(8,128)(2,1)S(1)} %copy-done.10), custom_call_target="tpu_custom_call" | custom-call | flops 838860800 | bytes 3145728 | tf_op jit(solution)/shard_map/pallas_call | solution.py:355
  126.3 4.1 %all-to-all-start.2 = ((bf16[8,192,128]{2,1,0:T(8,128)(2,1)}), bf16[8,192,128]{2,1,0:T(8,128)(2,1)}, u32[]{:S(2)}, u32[]{:S(2)}) async-start(bf16[8,192,128]{2,1,0:T(8,128)(2,1)} %copy-done.13), calls=%async_computation.2 | async-start | bytes 786432 | tf_op jit(solution)/shard_map/all_to_all | solution.py:429
  130.5 3.2 %shard_map.164 = bf16[2,192,3072]{2,1,0:T(8,128)(2,1)S(1)} custom-call(bf16[2,4,192,128]{3,2,1,0:T(8,128)(2,1)} %bitcast.21.heads_ref, bf16[512,3072]{1,0:T(8,128)(2,1)S(1)} %bitcast.53), custom_call_target="tpu_custom_call" | custom-call | flops 1207959552 | bytes 8388608 | tf_op jit(solution)/shard_map/pallas_call | solution.py:383
  136.3 4.8 %all-to-all-done.2 = bf16[8,192,128]{2,1,0:T(8,128)(2,1)} async-done(((bf16[8,192,128]{2,1,0:T(8,128)(2,1)}), bf16[8,192,128]{2,1,0:T(8,128)(2,1)}, u32[]{:S(2)}, u32[]{:S(2)}) %all-to-all-start.2) | async-done | bytes 393248 | tf_op jit(solution)/shard_map/all_to_all | solution.py:429
  141.1 3.2 %shard_map.163 = bf16[2,192,3072]{2,1,0:T(8,128)(2,1)S(1)} custom-call(bf16[2,4,192,128]{3,2,1,0:T(8,128)(2,1)} %bitcast.17.heads_ref, bf16[512,3072]{1,0:T(8,128)(2,1)S(1)} %bitcast.54), custom_call_target="tpu_custom_call" | custom-call | flops 1207959552 | bytes 8388608 | tf_op jit(solution)/shard_map/pallas_call | solution.py:383
  144.6 2.3 %copy-done.5 = bf16[2,192,3072]{2,1,0:T(8,128)(2,1)S(1)} copy-done((bf16[2,192,3072]{2,1,0:T(8,128)(2,1)S(1)}, bf16[2,192,3072]{2,1,0:T(8,128)(2,1)}, u32[]{:S(2)}) %copy-start.5) | copy-done | bytes 2359320
  155.3 19.5 %collective-permute-done.11 = bf16[192,3072]{1,0:T(8,128)(2,1)} collective-permute-done((bf16[192,3072]{1,0:T(8,128)(2,1)S(1)}, bf16[192,3072]{1,0:T(8,128)(2,1)}, u32[]{:S(2)}, u32[]{:S(2)}) %collective-permute-start.11) | collective-permute-done | bytes 1179680 | tf_op jit(solution)/shard_map/ppermute | solution.py:426
  174.8 2.5 %fusion.1 = f32[192,3072]{1,0:T(8,128)S(1)} fusion(bf16[192,3072]{1,0:T(8,128)(2,1)} %collective-permute-done.11, bf16[192,3072]{1,0:T(8,128)(2,1)} %collective-permute-done.9, bf16[2,192,3072]{2,1,0:T(8,128)(2,1)} %copy-done.6), kind=kLoop, calls=%fused_computation.4 | loop fusion | flops 2949120 | bytes 5898240 | tf_op jit(solution)/shard_map/add | solution.py:502
  178.5 13.9 %all-gather.2.cloned.1.call-done = bf16[256,3072]{1,0:T(8,128)(2,1)} async-done(((bf16[32,3072]{1,0:T(8,128)(2,1)}), bf16[256,3072]{1,0:T(8,128)(2,1)}) %all-gather.2.cloned.1.call-update) | async-done | bytes 1572880 | tf_op jit(solution)/shard_map/all_gather | solution.py:459
  (92 shorter events, 32.9 us)
Async XLA Ops:
  7.2 148.1 %copy-start = (f32[4,3072]{1,0:T(4,128)S(1)}, f32[4,3072]{1,0:T(4,128)}, u32[]{:S(2)}) copy-start(f32[4,3072]{1,0:T(4,128)} %param.22) | copy-start | bytes 147460
  9.4 15.7 %collective-permute-start.4 = (bf16[32,4096]{1,0:T(8,128)(2,1)S(1)}, bf16[32,4096]{1,0:T(8,128)(2,1)S(1)}, u32[]{:S(2)}, u32[]{:S(2)}) collective-permute-start(bf16[32,4096]{1,0:T(8,128)(2,1)S(1)} %fusion.18), channel_id=1, source_target_pairs={{0,16},{8,24},{16,0},{24,8},{1,17},{9,25},{17,1},{25,9},{2,18},{10... | collective-permute-start | bytes 786440 | tf_op jit(solution)/shard_map/ppermute | solution.py:426
  12.4 13.2 %collective-permute-start.3 = (bf16[32,4096]{1,0:T(8,128)(2,1)S(1)}, bf16[32,4096]{1,0:T(8,128)(2,1)S(1)}, u32[]{:S(2)}, u32[]{:S(2)}) collective-permute-start(bf16[32,4096]{1,0:T(8,128)(2,1)S(1)} %fusion.18), channel_id=1, source_target_pairs={{0,8},{8,0},{16,24},{24,16},{1,9},{9,1},{17,25},{25,17},{2,10},{10... | collective-permute-start | bytes 786440 | tf_op jit(solution)/shard_map/ppermute | solution.py:423
  12.4 24.0 %collective-permute-start.1 = (bf16[128,3072]{1,0:T(8,128)(2,1)}, bf16[128,3072]{1,0:T(8,128)(2,1)S(1)}, u32[]{:S(2)}, u32[]{:S(2)}) collective-permute-start(bf16[128,3072]{1,0:T(8,128)(2,1)} %bitcast.55), channel_id=1, source_target_pairs={{0,16},{8,24},{16,0},{24,8},{1,17},{9,25},{17,1},{25,9},{2,18},{10... | collective-permute-start | bytes 2359304 | tf_op jit(solution)/shard_map/ppermute | solution.py:426
  12.6 14.1 %copy-start.21 = (f32[768]{0:T(1024)S(1)}, f32[768]{0:T(1024)}, u32[]{:S(2)}) copy-start(f32[768]{0:T(1024)} %param.25) | copy-start | bytes 9220
  25.1 1.6 collective-permute-start.5
  26.7 16.0 %copy-start.1 = (bf16[3072,4,3,128]{3,0,1,2:T(8,128)(2,1)S(1)}, bf16[3072,4,3,128]{3,0,1,2:T(8,128)(2,1)}, u32[]{:S(2)}) copy-start(bf16[3072,4,3,128]{3,0,1,2:T(8,128)(2,1)} %copy.19) | copy-start | bytes 28311556
  30.7 12.0 %copy-start.14 = (f32[4,128]{1,0:T(4,128)S(1)}, f32[4,128]{1,0:T(4,128)}, u32[]{:S(2)}) copy-start(f32[4,128]{1,0:T(4,128)} %refs_6_.3) | copy-start | bytes 6148
  30.7 9.1 %collective-permute-start.7 = (bf16[4,32,768]{2,1,0:T(8,128)(2,1)S(1)}, bf16[4,32,768]{2,1,0:T(8,128)(2,1)S(1)}, u32[]{:S(2)}, u32[]{:S(2)}) collective-permute-start(bf16[4,32,768]{2,1,0:T(8,128)(2,1)S(1)} %bitcast.58), channel_id=1, source_target_pairs={{0,16},{8,24},{16,0},{24,8},{1,17},{9,25},{17,1},{25,9},{2,18},{10... | collective-permute-start | bytes 589832 | tf_op jit(solution)/shard_map/ppermute | solution.py:426
  36.4 6.3 %collective-permute-start.2 = (bf16[128,3072]{1,0:T(8,128)(2,1)S(1)}, bf16[128,3072]{1,0:T(8,128)(2,1)S(1)}, u32[]{:S(2)}, u32[]{:S(2)}) collective-permute-start(bf16[128,3072]{1,0:T(8,128)(2,1)S(1)} %collective-permute-done.1.refs_0_), channel_id=1, source_target_pairs={{0,8},{8,0},{16,24},{24,16},{1,9},{9,1},{17,25},{25,17},{2,10},{10... | collective-permute-start | bytes 2359304 | tf_op jit(solution)/shard_map/ppermute | solution.py:423
  36.5 3.4 %collective-permute-start.6 = (bf16[4,32,768]{2,1,0:T(8,128)(2,1)S(1)}, bf16[4,32,768]{2,1,0:T(8,128)(2,1)S(1)}, u32[]{:S(2)}, u32[]{:S(2)}) collective-permute-start(bf16[4,32,768]{2,1,0:T(8,128)(2,1)S(1)} %bitcast.59), channel_id=1, source_target_pairs={{0,8},{8,0},{16,24},{24,16},{1,9},{9,1},{17,25},{25,17},{2,10},{10... | collective-permute-start | bytes 589832 | tf_op jit(solution)/shard_map/ppermute | solution.py:423
  39.8 1.4 collective-permute-start.8
  50.8 35.0 %all-to-all-start.1 = ((bf16[8,192,384]{2,1,0:T(8,128)(2,1)}), bf16[8,192,384]{2,1,0:T(8,128)(2,1)S(1)}, u32[]{:S(2)}, u32[]{:S(2)}) async-start(bf16[8,192,384]{2,1,0:T(8,128)(2,1)} %bitcast.16), calls=%async_computation.1 | async-start | bytes 2359296 | tf_op jit(solution)/shard_map/all_to_all | solution.py:429
  57.0 2.4 %collective-permute-start = (bf16[128,3072]{1,0:T(8,128)(2,1)S(1)}, bf16[128,3072]{1,0:T(8,128)(2,1)S(1)}, u32[]{:S(2)}, u32[]{:S(2)}) collective-permute-start(bf16[128,3072]{1,0:T(8,128)(2,1)S(1)} %bitcast.56), channel_id=1, source_target_pairs={{0,8},{8,0},{16,24},{24,16},{1,9},{9,1},{17,25},{25,17},{2,10},{10... | collective-permute-start | bytes 2359304 | tf_op jit(solution)/shard_map/ppermute | solution.py:423
  63.0 26.6 %copy-start.18 = (s32[4,8]{1,0:T(4,128)S(1)}, s32[4,8]{1,0:T(4,128)}, u32[]{:S(2)}) copy-start(s32[4,8]{1,0:T(4,128)} %param.19) | copy-start | bytes 388
  85.8 24.0 %all-to-all-start = ((bf16[8,128,384]{2,1,0:T(8,128)(2,1)}), bf16[8,128,384]{2,1,0:T(8,128)(2,1)S(1)}, u32[]{:S(2)}, u32[]{:S(2)}) async-start(bf16[8,128,384]{2,1,0:T(8,128)(2,1)} %bitcast.5), calls=%async_computation | async-start | bytes 1572864 | tf_op jit(solution)/shard_map/all_to_all | solution.py:429
  110.7 15.6 %all-to-all-start.3 = ((bf16[8,192,128]{2,1,0:T(8,128)(2,1)}), bf16[8,192,128]{2,1,0:T(8,128)(2,1)}, u32[]{:S(2)}, u32[]{:S(2)}) async-start(bf16[8,192,128]{2,1,0:T(8,128)(2,1)} %shard_map.161), calls=%async_computation.3 | async-start | bytes 786432 | tf_op jit(solution)/shard_map/all_to_all | solution.py:429
  114.8 15.6 %copy-start.3 = (bf16[4,128,3072]{2,1,0:T(8,128)(2,1)S(1)}, bf16[4,128,3072]{2,1,0:T(8,128)(2,1)}, u32[]{:S(2)}) copy-start(bf16[4,128,3072]{2,1,0:T(8,128)(2,1)} %param.29) | copy-start | bytes 9437188
  126.3 14.8 %all-to-all-start.2 = ((bf16[8,192,128]{2,1,0:T(8,128)(2,1)}), bf16[8,192,128]{2,1,0:T(8,128)(2,1)}, u32[]{:S(2)}, u32[]{:S(2)}) async-start(bf16[8,192,128]{2,1,0:T(8,128)(2,1)} %copy-done.13), calls=%async_computation.2 | async-start | bytes 786432 | tf_op jit(solution)/shard_map/all_to_all | solution.py:429
  130.4 62.0 %all-gather.2.cloned.1.call-start = ((), (), s32[]{:S(2)}) async-start(), calls=%async_computation.4 | async-start | bytes 1769472 | tf_op jit(solution)/shard_map/all_gather | solution.py:459
  136.3 8.2 %collective-permute-start.10 = (bf16[192,3072]{1,0:T(8,128)(2,1)}, bf16[192,3072]{1,0:T(8,128)(2,1)}, u32[]{:S(2)}, u32[]{:S(2)}) collective-permute-start(bf16[192,3072]{1,0:T(8,128)(2,1)} %slice_bitcast_fusion), channel_id=1, source_target_pairs={{0,8},{8,0},{16,24},{24,16},{1,9},{9,1},{17,25},{25,17},{2,10},{10... | collective-permute-start | bytes 3538952 | tf_op jit(solution)/shard_map/ppermute | solution.py:423
  144.5 10.8 %collective-permute-start.9 = (bf16[192,3072]{1,0:T(8,128)(2,1)S(1)}, bf16[192,3072]{1,0:T(8,128)(2,1)}, u32[]{:S(2)}, u32[]{:S(2)}) collective-permute-start(bf16[192,3072]{1,0:T(8,128)(2,1)S(1)} %slice_bitcast_fusion.2), channel_id=1, source_target_pairs={{0,8},{8,0},{16,24},{24,16},{1,9},{9,1},{17,25},{25,17},{2,10},{10... | collective-permute-start | bytes 3538952 | tf_op jit(solution)/shard_map/ppermute | solution.py:423
  148.6 26.2 %collective-permute-start.11 = (bf16[192,3072]{1,0:T(8,128)(2,1)S(1)}, bf16[192,3072]{1,0:T(8,128)(2,1)}, u32[]{:S(2)}, u32[]{:S(2)}) collective-permute-start(bf16[192,3072]{1,0:T(8,128)(2,1)S(1)} %fusion), channel_id=1, source_target_pairs={{0,16},{8,24},{16,0},{24,8},{1,17},{9,25},{17,1},{25,9},{2,18},{10... | collective-permute-start | bytes 3538952 | tf_op jit(solution)/shard_map/ppermute | solution.py:426
  155.3 22.1 %copy-start.8 = (bf16[1,128,3072]{2,1,0:T(8,128)(2,1)S(1)}, bf16[1,128,3072]{2,1,0:T(8,128)(2,1)}, u32[]{:S(2)}) copy-start(bf16[1,128,3072]{2,1,0:T(8,128)(2,1)} %param.15) | copy-start | bytes 2359300
  (15 other events, 80.9 us)
Sparse Core Ops, SparseCore 0:
  150.3 42.0 all-gather.1

commit v2 on v0

--- a/solution.py
+++ b/solution.py
@@ -1,6 +1,10 @@
+import functools
+
 import jax
 import jax.numpy as jnp
 from jax import lax
+from jax.experimental import pallas as pl
+from jax.experimental.pallas import tpu as pltpu
 from jax.sharding import PartitionSpec as P
 
 HD = 128
@@ -65,7 +69,7 @@
     return lax.map(one_block, stacked_blocks).reshape(query_count, queries.shape[1])
 
 
-def body(
+def general_body(
     video,
     text_cache,
     text_count,
@@ -194,6 +198,466 @@
     return (result[:video_rows][None], text_result[None])
 
 
+def vmem_spec():
+    return pl.BlockSpec(memory_space=pltpu.VMEM)
+
+
+def smem_spec():
+    return pl.BlockSpec(memory_space=pltpu.SMEM)
+
+
+def hbm_spec():
+    return pl.BlockSpec(memory_space=pltpu.HBM)
+
+
+def params(mib):
+    return pltpu.CompilerParams(vmem_limit_bytes=mib << 20)
+
+
+def cost(flops, moved, exps=0):
+    return pl.CostEstimate(flops=int(flops), bytes_accessed=int(moved), transcendentals=int(exps))
+
+
+def norm_kernel(rows_ref, gain_ref, out_ref):
+    out_ref[...] = rms_scale(rows_ref[0].astype(jnp.float32), gain_ref[...]).astype(jnp.bfloat16)
+
+
+def norm_text(rows, gain):
+    return pl.pallas_call(
+        norm_kernel,
+        out_shape=jax.ShapeDtypeStruct(rows.shape[1:], jnp.bfloat16),
+        in_specs=[vmem_spec(), vmem_spec()],
+        out_specs=vmem_spec(),
+        compiler_params=params(8),
+        cost_estimate=cost(4 * rows.size, 4 * rows.size),
+    )(rows, gain[None])
+
+
+def table_row(ref, index):
+    return ref[pl.ds(index, 1)]
+
+
+def project_heads_into(out_ref, x_ref, w_ref, qg_ref, kg_ref, place):
+    heads = w_ref.shape[1]
+    for first in range(0, heads, 2):
+        pair = range(first, first + 2)
+        weights = jnp.concatenate([w_ref[c, h] for h in pair for c in range(3)], axis=1)
+        raw = jnp.dot(x_ref[...], weights, preferred_element_type=jnp.float32)
+        for i, h in enumerate(pair):
+            lo = 3 * HD * i
+            queries = rms_scale(raw[:, lo : lo + HD], qg_ref[h : h + 1]).astype(jnp.bfloat16)
+            keys = rms_scale(raw[:, lo + HD : lo + 2 * HD], kg_ref[h : h + 1]).astype(jnp.bfloat16)
+            values = raw[:, lo + 2 * HD : lo + 3 * HD].astype(jnp.bfloat16)
+            for lo_row, count, r, to in place:
+                for c, part in enumerate((queries, keys, values)):
+                    out_ref[r, h, to : to + count, c * HD : (c + 1) * HD] = part[
+                        lo_row : lo_row + count
+                    ]
+
+
+def local_kernel(a_ref, b_ref, shift_ref, scale_ref, w_ref, qg_ref, kg_ref, out_ref, x_ref):
+    rows = a_ref.shape[0]
+    mine = lax.axis_index("job")
+    for r, ref in enumerate((a_ref, b_ref)):
+        x_ref[r * rows : (r + 1) * rows] = modulate(
+            ref[...], table_row(shift_ref, mine ^ r), table_row(scale_ref, mine ^ r)
+        )
+    place = [(r * rows, rows, r, 0) for r in range(2)]
+    project_heads_into(out_ref, x_ref, w_ref, qg_ref, kg_ref, place)
+
+
+def remote_kernel(
+    holder_ref, a_ref, b_ref, t0_ref, t1_ref, t2_ref, t3_ref, shift_ref, scale_ref, w_ref,
+    qg_ref, kg_ref, out_ref, x_ref, text_ref,
+):
+    rows = a_ref.shape[0]
+    jobs, trows, width = t0_ref.shape
+    mine = lax.axis_index("job")
+    for b in range(jobs):
+        for q, part in enumerate((t0_ref, t1_ref, t2_ref, t3_ref)):
+
+            @pl.when(mine ^ b == q)
+            def _():
+                for r in range(jobs):
+                    text_ref[r * trows : (r + 1) * trows, b * width : (b + 1) * width] = part[
+                        holder_ref[mine ^ r] ^ b
+                    ]
+
+    for r, ref in enumerate((a_ref, b_ref)):
+        x_ref[r * rows : (r + 1) * rows] = modulate(
+            ref[...], table_row(shift_ref, mine ^ (2 + r)), table_row(scale_ref, mine ^ (2 + r))
+        )
+    for r in range(jobs):
+        lo = 2 * rows + r * trows
+        x_ref[lo : lo + trows] = modulate(
+            text_ref[r * trows : (r + 1) * trows],
+            table_row(shift_ref, mine ^ r),
+            table_row(scale_ref, mine ^ r),
+        )
+    place = [(r * rows, rows, r, 0) for r in range(2)]
+    place += [
+        (2 * rows + r * trows, trows, r % 2, rows + (r // 2) * trows) for r in range(jobs)
+    ]
+    project_heads_into(out_ref, x_ref, w_ref, qg_ref, kg_ref, place)
+    for r in range(2):
+        for h in range(w_ref.shape[1]):
+            lo = (r * w_ref.shape[1] + h) * 3 * HD
+            out_ref[r, h, rows + 2 * trows :] = text_ref[0:trows, lo : lo + 3 * HD]
+
+
+def qkv_call(kernel, inputs, specs, rows_in, rows_out, extra, weights, q_gain, k_gain):
+    group, width = weights.shape[1:3]
+    return pl.pallas_call(
+        kernel,
+        out_shape=jax.ShapeDtypeStruct((2, group, rows_out, 3 * HD), jnp.bfloat16),
+        in_specs=specs + [vmem_spec()] * 3,
+        out_specs=vmem_spec(),
+        scratch_shapes=[pltpu.VMEM((rows_in, width), jnp.bfloat16), *extra],
+        compiler_params=params(16),
+        cost_estimate=cost(2 * rows_in * weights.size, 2 * weights.size + 4 * rows_in * width),
+    )(*inputs, weights, q_gain, k_gain)
+
+
+def qkv_local(own, core, shift, scale, weights, q_gain, k_gain):
+    rows = own.shape[0]
+    return qkv_call(
+        local_kernel, (own, core, shift, scale), [vmem_spec()] * 4, 2 * rows, rows, [],
+        weights, q_gain, k_gain,
+    )
+
+
+def qkv_remote(holder, pair, parts, shift, scale, weights, q_gain, k_gain):
+    rows, width = pair[0].shape
+    jobs, trows, _ = parts[0].shape
+    return qkv_call(
+        remote_kernel, (holder, *pair, *parts, shift, scale), [smem_spec()] + [vmem_spec()] * 8,
+        2 * rows + jobs * trows, rows + 3 * trows,
+        [pltpu.VMEM((jobs * trows, width), jnp.bfloat16)], weights, q_gain, k_gain,
+    )
+
+
+def choose_slots(count_ref, splits_ref, job, table, put):
+    shards = splits_ref.shape[1]
+    slots = 2 * table.shape[0] // shards
+    slot = lax.broadcasted_iota(jnp.int32, (slots, table.shape[0]), 0)
+    row = lax.broadcasted_iota(jnp.int32, (slots, table.shape[0]), 1)
+    offset = jnp.int32(0)
+    for s in range(shards):
+        chosen = (row == slot + offset) & (slot < splits_ref[job, s]) & (row < count_ref[job])
+        chosen = jnp.where(chosen, 1.0, 0.0).astype(jnp.bfloat16)
+        put(s, jnp.dot(chosen, table, preferred_element_type=jnp.float32).astype(jnp.bfloat16))
+        offset = offset + splits_ref[job, s]
+
+
+def attention_kernel(
+    far, text_base, count_ref, splits_ref, video_hbm, text_hbm, *refs
+):
+    out_hbm, v_refs, t_refs, mixed_ref, out_ref, sems = refs[0], refs[1:4], refs[4:7], *refs[7:10]
+    col_ref = None if far else refs[10]
+    shards, vrows, _ = v_refs[0].shape
+    trows = t_refs[0].shape[1]
+    copies = []
+    for c in range(3):
+        cols = pl.ds(c * HD, HD)
+        copies.append(
+            pltpu.make_async_copy(
+                video_hbm.at[:, pl.ds(0, vrows), cols], v_refs[c], sems.at[c]
+            )
+        )
+        copies.append(
+            pltpu.make_async_copy(
+                text_hbm.at[:, pl.ds(text_base, trows), cols], t_refs[c], sems.at[3 + c]
+            )
+        )
+    if not far:
+        copies.append(
+            pltpu.make_async_copy(
+                text_hbm.at[:, pl.ds(vrows + 2 * trows, trows)], col_ref, sems.at[6]
+            )
+        )
+    for copy in copies:
+        copy.start()
+    for copy in copies:
+        copy.wait()
+    mine = lax.axis_index("job")
+    half = lax.axis_index("seq") // (shards // 2)
+    job = mine ^ half ^ (2 if far else 0)
+    column = lax.broadcasted_iota(jnp.int32, (1, shards * trows), 1)
+    key_ok = column < count_ref[job]
+    scale = HD ** (-0.5)
+    video_keys = v_refs[1][...].reshape(shards * vrows, HD)
+    text_keys = t_refs[1][...].reshape(shards * trows, HD)
+    video_values = v_refs[2][...].reshape(shards * vrows, HD)
+    text_values = t_refs[2][...].reshape(shards * trows, HD)
+
+    def product(a, b):
+        return lax.dot_general(a, b, (((1,), (1,)), ((), ())), preferred_element_type=jnp.float32)
+
+    def one_block(queries):
+        video_scores = product(queries, video_keys)
+        text_scores = jnp.where(key_ok, product(queries, text_keys), -1e30)
+        highest = jnp.maximum(
+            jnp.max(video_scores, axis=-1, keepdims=True),
+            jnp.max(text_scores, axis=-1, keepdims=True),
+        )
+        video_w = jnp.exp((video_scores - highest) * scale)
+        text_w = jnp.exp((text_scores - highest) * scale)
+        summed = jnp.sum(video_w, axis=-1, keepdims=True) + jnp.sum(text_w, axis=-1, keepdims=True)
+        mixed = jnp.dot(
+            video_w.astype(jnp.bfloat16), video_values, preferred_element_type=jnp.float32
+        ) + jnp.dot(text_w.astype(jnp.bfloat16), text_values, preferred_element_type=jnp.float32)
+        return (mixed / summed).astype(jnp.bfloat16)
+
+    mixed_ref[...] = one_block(t_refs[0][...].reshape(shards * trows, HD))
+    rows = vrows + 2 * trows
+    sends = [
+        pltpu.make_async_copy(out_ref.at[s], out_hbm.at[s], sems.at[7 + s]) for s in range(shards)
+    ]
+
+    def put(s, chosen):
+        out_ref[s, vrows:rows] = chosen
+
+    choose_slots(count_ref, splits_ref, job, mixed_ref[...], put)
+    if not far:
+
+        def put_columns(s, chosen):
+            for c in range(3):
+                lo = rows + 2 * trows * c
+                out_ref[s, lo : lo + 2 * trows] = chosen[:, c * HD : (c + 1) * HD]
+
+        choose_slots(
+            count_ref, splits_ref, mine, col_ref[...].reshape(shards * trows, 3 * HD), put_columns
+        )
+    for i in range(0, shards, 2):
+        done = one_block(v_refs[0][i : i + 2].reshape(2 * vrows, HD))
+        out_ref[i, 0:vrows] = done[:vrows]
+        out_ref[i + 1, 0:vrows] = done[vrows:]
+        sends[i].start()
+        sends[i + 1].start()
+    for send in sends:
+        send.wait()
+
+
+def attend_pair(far, count, splits, video_qkv, text_qkv, vrows, trows):
+    shards = video_qkv.shape[0]
+    slots = 2 * trows
+    total = shards * (vrows + trows)
+    rows_out = vrows + slots * (1 if far else 4)
+    scratch = [pltpu.VMEM((shards, vrows, HD), jnp.bfloat16)] * 3
+    scratch += [pltpu.VMEM((shards, trows, HD), jnp.bfloat16)] * 3
+    scratch += [pltpu.VMEM((shards * trows, HD), jnp.bfloat16)]
+    scratch += [pltpu.VMEM((shards, rows_out, HD), jnp.bfloat16)]
+    scratch += [pltpu.SemaphoreType.DMA((7 + shards,))]
+    if not far:
+        scratch += [pltpu.VMEM((shards, trows, 3 * HD), jnp.bfloat16)]
+    return pl.pallas_call(
+        functools.partial(attention_kernel, far, vrows + (trows if far else 0)),
+        out_shape=pltpu.HBM((shards, rows_out, HD), jnp.bfloat16),
+        in_specs=[smem_spec(), smem_spec(), hbm_spec(), hbm_spec()],
+        out_specs=hbm_spec(),
+        scratch_shapes=scratch,
+        compiler_params=params(12),
+        cost_estimate=cost(4 * total * total * HD, 3 << 20, total * total),
+    )(count, splits, video_qkv, text_qkv)
+
+
+def out_kernel(which, with_slots, added, *refs):
+    heads_ref, w_ref, out_ref = refs[0], refs[1], refs[2 + added]
+    group = w_ref.shape[0] // HD
+    count, width = out_ref.shape
+    rows = jnp.concatenate([heads_ref[which * group + h, 0:count] for h in range(group)], axis=1)
+    for lo in range(0, width, width // 4):
+        cols = slice(lo, lo + width // 4)
+        total = jnp.dot(rows, w_ref[:, cols], preferred_element_type=jnp.float32)
+        if added:
+            total = total + refs[2][:, cols].astype(jnp.float32)
+        out_ref[:, cols] = total.astype(jnp.bfloat16)
+    if with_slots:
+        slot_ref = refs[3 + added]
+        slots = slot_ref.shape[0]
+        for block in range(width // HD):
+            lo = count + (block % 3) * slots
+            slot_ref[:, block * HD : (block + 1) * HD] = heads_ref[block // 3, lo : lo + slots]
+
+
+def project_out(heads, rows, which, weights, *added, slots=0):
+    depth, width = weights.shape
+    out = jax.ShapeDtypeStruct((rows, width), jnp.bfloat16)
+    slot_out = jax.ShapeDtypeStruct((slots, width), jnp.bfloat16)
+    return pl.pallas_call(
+        functools.partial(out_kernel, which, slots > 0, len(added)),
+        out_shape=(out, slot_out) if slots else out,
+        in_specs=[vmem_spec()] * (2 + len(added)),
+        out_specs=(vmem_spec(), vmem_spec()) if slots else vmem_spec(),
+        compiler_params=params(8),
+        cost_estimate=cost(2 * rows * depth * width, 2 * (depth + 2 * rows) * width),
+    )(heads, weights, *added)
+
+
+def final_kernel(
+    count_ref, splits_ref, video_ref, part_ref, chip_hbm, gate_ref, slot_ref, vout_hbm, tout_hbm,
+    chip_ref, out_ref, in_sems, out_sems,
+):
+    vrows, step = video_ref.shape[1], slot_ref.shape[0]
+    total_rows = part_ref.shape[0]
+    reads, writes = [], []
+    for i, lo in enumerate(range(0, total_rows, step)):
+        rows = pl.ds(lo, step)
+        reads.append(pltpu.make_async_copy(chip_hbm.at[rows], chip_ref.at[rows], in_sems.at[i]))
+        target = vout_hbm.at[0, rows] if lo < vrows else tout_hbm.at[0]
+        writes.append(pltpu.make_async_copy(out_ref.at[rows], target, out_sems.at[i]))
+    for read in reads:
+        read.start()
+    job, shard = lax.axis_index("job"), lax.axis_index("seq")
+    gate = table_row(gate_ref, job)
+    offset = jnp.int32(0)
+    for s in range(splits_ref.shape[1]):
+        offset = offset + jnp.where(s < shard, splits_ref[job, s], 0)
+    slot = lax.broadcasted_iota(jnp.int32, (step, 1), 0)
+    valid = (slot < splits_ref[job, shard]) & (slot + offset < count_ref[job])
+    for i, lo in enumerate(range(0, total_rows, step)):
+        reads[i].wait()
+        rows = slice(lo, lo + step)
+        total = part_ref[rows].astype(jnp.float32) + chip_ref[rows].astype(jnp.float32)
+        base = video_ref[0, rows] if lo < vrows else slot_ref[...]
+        result = base.astype(jnp.float32) + gate * total
+        if lo >= vrows:
+            result = jnp.where(valid, result, 0.0)
+        out_ref[rows] = result.astype(jnp.bfloat16)
+        writes[i].start()
+    for write in writes:
+        write.wait()
+
+
+def finish(count, splits, video, part, from_chip, gate, slot_rows):
+    rows, width = part.shape
+    steps = rows // slot_rows.shape[0]
+    vrows = video.shape[1]
+    return pl.pallas_call(
+        final_kernel,
+        out_shape=(
+            jax.ShapeDtypeStruct((1, vrows, width), jnp.bfloat16),
+            jax.ShapeDtypeStruct((1, rows - vrows, width), jnp.bfloat16),
+        ),
+        in_specs=[
+            smem_spec(), smem_spec(), vmem_spec(), vmem_spec(), hbm_spec(), vmem_spec(), vmem_spec(),
+        ],
+        out_specs=(hbm_spec(), hbm_spec()),
+        scratch_shapes=[
+            pltpu.VMEM((rows, width), jnp.bfloat16),
+            pltpu.VMEM((rows, width), jnp.bfloat16),
+            pltpu.SemaphoreType.DMA((steps,)),
+            pltpu.SemaphoreType.DMA((steps,)),
+        ],
+        compiler_params=params(8),
+        cost_estimate=cost(6 * rows * width, 10 * rows * width),
+    )(count, splits, video, part, from_chip, gate, slot_rows)
+
+
+def two_wave_body(
+    video,
+    text_cache,
+    text_count,
+    holder,
+    text_splits,
+    mod_shift,
+    mod_scale,
+    mod_gate,
+    text_gain,
+    refine_w,
+    refine_bias,
+    w_qkv,
+    q_gain,
+    k_gain,
+    w_out,
+):
+    job_count = lax.axis_size("job")
+    shard_count = lax.axis_size("seq")
+    group_size = w_qkv.shape[1]
+    trows = text_cache.shape[1]
+    vrows = video.shape[1]
+
+    def to_core(x):
+        return lax.ppermute(x, "job", [(i, i ^ 1) for i in range(job_count)])
+
+    def to_chip(x):
+        return lax.ppermute(x, "job", [(i, i ^ 2) for i in range(job_count)])
+
+    def over_seq(x):
+        return lax.all_to_all(x, "seq", split_axis=0, concat_axis=0, tiled=False)
+
+    def after(x, earlier):
+        return lax.optimization_barrier((x, earlier))[0]
+
+    qkv_w = jnp.transpose(w_qkv, (2, 1, 0, 3))
+    own_video = video[0]
+    core_video = to_core(own_video)
+
+    normed = norm_text(text_cache, text_gain)
+    normed_core = to_core(normed)
+    normed_chip = to_chip(normed)
+    chip_video = to_chip(after(own_video, normed))
+    local_send = qkv_local(own_video, core_video, mod_shift, mod_scale, qkv_w, q_gain, k_gain)
+    local_qkv = over_seq(local_send.reshape(shard_count, vrows, 3 * HD))
+    normed_core, normed_chip = after((normed_core, normed_chip), local_send)
+    normed_both = to_core(normed_chip)
+    lifted = jnp.dot(
+        jnp.concatenate([normed, normed_core, normed_chip, normed_both], axis=0),
+        refine_w,
+        preferred_element_type=jnp.float32,
+    )
+    refined = (lifted + refine_bias).astype(jnp.bfloat16).reshape(job_count, trows, -1)
+    refined_core = to_core(refined)
+    refined_chip = to_chip(refined)
+    refined_both = to_core(refined_chip)
+
+    chip_video = after(chip_video, refined)
+    both_video = to_core(chip_video)
+    send = qkv_remote(
+        holder,
+        (chip_video, both_video),
+        (refined, refined_core, refined_chip, refined_both),
+        mod_shift,
+        mod_scale,
+        qkv_w,
+        q_gain,
+        k_gain,
+    )
+    second = over_seq(after(send.reshape(shard_count, -1, 3 * HD), local_qkv))
+
+    remote_mixed = attend_pair(True, text_count, text_splits, second, second, vrows, trows)
+    remote_back = over_seq(remote_mixed)
+    local_mixed = attend_pair(
+        False, text_count, text_splits, after(local_qkv, remote_mixed), second, vrows, trows
+    )
+    out_weight = w_out.reshape(group_size * HD, w_out.shape[2])
+    rows = vrows + 2 * trows
+    remote_back = after(remote_back, local_mixed)
+    local_back = over_seq(after(local_mixed, remote_back))
+    from_core = to_core(project_out(remote_back, rows, 1, out_weight))
+    crossing = project_out(remote_back, rows, 0, out_weight, from_core)
+    from_chip = to_chip(crossing)
+    local_back = after(local_back, from_chip)
+    near_part, slot_rows = project_out(local_back, rows, 1, out_weight, slots=2 * trows)
+    local_part = project_out(local_back, rows, 0, out_weight, to_core(near_part))
+    return finish(
+        text_count, text_splits, video, local_part, from_chip, mod_gate, slot_rows
+    )
+
+
+def body(*arrays):
+    video, text_cache, w_qkv = arrays[0], arrays[1], arrays[11]
+    job_count = lax.axis_size("job")
+    shard_count = lax.axis_size("seq")
+    fits = (
+        job_count == 4
+        and shard_count == 2 * w_qkv.shape[1]
+        and video.shape[1] == 128
+        and text_cache.shape[1] == 32
+    )
+    return (two_wave_body if fits else general_body)(*arrays)
+
+
 def solution(mesh):
     placed = (
         P("job", "seq", None),

time: 340 us -> 157 us (0.46)
  waiting for transfers between devices: 148 us -> 42.6 us
  blocking collectives: 73.1 us -> 37.3 us
  matrix products: 38.3 us -> 3.97 us
  Pallas kernels: 0 us -> 32.3 us
  other arithmetic: 24.3 us -> 0 us
  local copies, waits for them, and re-layouts: 36.9 us -> 18 us
  starting transfers between devices: 4.41 us -> 21 us
  between operations: 14.2 us -> 1.08 us
    all_gather x4 -> x0, waiting for transfers between devices: 90 us -> none  [the longest x1 41.7 us: body(): gathered_text = lax.all_gather(refined, 'seq', axis=1, tiled=True)]
    reduce_scatter x1 -> x0, waiting for transfers between devices: 43.6 us -> none  [body(): lax.psum_scatter(jnp.dot(per_job, out_weight, preferred_element_type=jnp....]
    all_to_all x3 -> x1, blocking collectives: 73.1 us -> 37.3 us  [over_seq(): return lax.all_to_all(x, 'seq', split_axis=0, concat_axis=0, tiled=False)]
    dot_general x12 -> x1, matrix products: 38.3 us -> 3.97 us  [two_wave_body(): jnp.dot(jnp.concatenate([normed, normed_core, normed_chip, normed_both],...]
    pallas_call x0 -> x10, Pallas kernels: none -> 32.3 us  [the longest x2 10.2 us: attend_pair(): pl.pallas_call(functools.partial(attention_kernel, far, vrows + (trows if...]
    ppermute x0 -> x12, waiting for transfers between devices: none -> 20.6 us  [the longest x4 16.3 us: to_chip(): return lax.ppermute(x, 'job', [(i, i ^ 2) for i in range(job_count)])]
    unnamed x33 -> x41, local copies, waits for them, and re-layouts: 1.08 us -> 18 us
    reduce_sum x11 -> x0, other arithmetic: 13.8 us -> none  [the longest x2 4.23 us: modulate(): centre = jnp.mean(widened, axis=-1, keepdims=True)]
  transfers between devices with their start and end apart: 6 -> 15, of which waited for: 6 -> 7; matrix products, arithmetic and copies ran while one was open for 10% -> 8% of each run, Pallas kernels for 0% -> 12%
where the time goes in v2:
time: 157 us; the launch traced here: 156 us
  waiting for transfers between devices  42.6 us (27%)
  blocking collectives  37.3 us (24%)
  Pallas kernels  32.3 us (21%)
  starting transfers between devices  21 us (13%)
  local copies, waits for them, and re-layouts  18 us (11%)
  matrix products  3.97 us (3%)
    all_to_all x1, blocking collectives, over_seq(): return lax.all_to_all(x, 'seq', split_axis=0, concat_axis=0, tiled=False)  37.3 us
    all_to_all x3, waiting for transfers between devices, over_seq(): return lax.all_to_all(x, 'seq', split_axis=0, concat_axis=0, tiled=False)  22 us
    unnamed x41, local copies, waits for them, and re-layouts  18 us
    ppermute x4, waiting for transfers between devices, to_chip(): return lax.ppermute(x, 'job', [(i, i ^ 2) for i in range(job_count)])  16.3 us
    all_to_all x3, starting transfers between devices, over_seq(): return lax.all_to_all(x, 'seq', split_axis=0, concat_axis=0, tiled=False)  13.9 us
    pallas_call x2, Pallas kernels, attend_pair(): pl.pallas_call(functools.partial(attention_kernel, far, vrows + (trows if...  10.2 us
    pallas_call x2, Pallas kernels, qkv_call(): pl.pallas_call(kernel, out_shape=jax.ShapeDtypeStruct((2, group, rows_out...  10.1 us
    pallas_call x4, Pallas kernels, project_out(): pl.pallas_call(functools.partial(out_kernel, which, slots > 0, len(added)...  8.86 us
  transfers between devices with their start and end apart: 15, of which 7 were waited for; matrix products, arithmetic and copies ran while one was open for 8% of the time, Pallas kernels for 12%

profile of v2, /device:TPU:0, one launch (start us, length us, event | category | flops | bytes accessed | tf_op | source)
XLA Modules:
  0.0 156.3 jit_solution(11243591362964108570)
XLA Ops:
  3.1 2.6 %collective-permute-start.3 = (bf16[32,4096]{1,0:T(8,128)(2,1)S(1)}, bf16[32,4096]{1,0:T(8,128)(2,1)S(1)}, u32[]{:S(2)}, u32[]{:S(2)}) collective-permute-start(bf16[32,4096]{1,0:T(8,128)(2,1)S(1)} %shard_map.159), channel_id=1, source_target_pairs={{0,16},{8,24},{16,0},{24,8},{1,17},{9,25},{17,1},{25,9},{2,18},{10... | collective-permute-start | bytes 786440 | tf_op jit(solution)/shard_map/ppermute | solution.py:584
  6.2 9.0 %copy.19 = bf16[3072,4,3,128]{3,0,1,2:T(8,128)(2,1)} copy(bf16[3072,4,3,128]{3,1,2,0:T(4,128)(2,1)} %param.26) | data formatting | bytes 18874368 | tf_op args[11]
  15.2 3.7 %copy-done.1 = bf16[3072,4,3,128]{3,0,1,2:T(8,128)(2,1)S(1)} copy-done((bf16[3072,4,3,128]{3,0,1,2:T(8,128)(2,1)S(1)}, bf16[3072,4,3,128]{3,0,1,2:T(8,128)(2,1)}, u32[]{:S(2)}) %copy-start.1) | copy-done | bytes 9437208
  18.9 4.3 %shard_map.158 = bf16[2,4,128,384]{3,2,1,0:T(8,128)(2,1)} custom-call(bf16[128,3072]{1,0:T(8,128)(2,1)S(1)} %bitcast.18, bf16[128,3072]{1,0:T(8,128)(2,1)S(1)} %collective-permute-done.b_ref, f32[4,3072]{1,0:T(4,128)S(1)} %copy-done.10, f32[4,3072]{1,0:T(4,128)S(1)} %copy-done.11, bf16[3,4,3072,128]{3,2,1,0:T(8,128)(2,1)S(1)} %bitcast.14, ...), custom_call_target="tpu_custom_call" | custom-call | flops 2415919104 | bytes 12582912 | tf_op jit(solution)/shard_map/pallas_call | solution.py:310
  23.3 6.0 %all-to-all-start = ((bf16[8,128,384]{2,1,0:T(8,128)(2,1)}), bf16[8,128,384]{2,1,0:T(8,128)(2,1)S(1)}, u32[]{:S(2)}, u32[]{:S(2)}) async-start(bf16[8,128,384]{2,1,0:T(8,128)(2,1)} %bitcast.2), calls=%async_computation | async-start | bytes 1572864 | tf_op jit(solution)/shard_map/all_to_all | solution.py:587
  29.3 4.0 %fusion = bf16[128,768]{1,0:T(8,128)(2,1)S(1)} fusion(bf16[4096,768]{1,0:T(8,128)(2,1)} %param.24, bf16[32,4096]{1,0:T(8,128)(2,1)S(1)} %collective-permute-done.4, bf16[32,4096]{1,0:T(8,128)(2,1)S(1)} %collective-permute-done.3, bf16[32,4096]{1,0:T(8,128)(2,1)S(1)} %collective-permute-done.2, bf16[32,4096]{1,0:T(8,128)(2,1)S(1)} %shard_map.159, ...), kind=kOutput, calls=%fused_computation.2 | convolution fusion | flops 809697280 | bytes 7539712 | tf_op jit(solution)/shard_map/dot_general | solution.py:604
  35.1 5.6 %collective-permute-done.7.t2_ref = bf16[4,32,768]{2,1,0:T(8,128)(2,1)S(1)} collective-permute-done((bf16[4,32,768]{2,1,0:T(8,128)(2,1)S(1)}, bf16[4,32,768]{2,1,0:T(8,128)(2,1)S(1)}, u32[]{:S(2)}, u32[]{:S(2)}) %collective-permute-start.7) | collective-permute-done | bytes 196640 | tf_op jit(solution)/shard_map/ppermute | solution.py:584
  42.1 5.8 %shard_map.160 = bf16[2,4,224,384]{3,2,1,0:T(8,128)(2,1)S(1)} custom-call(s32[4]{0:T(128)S(1)} %copy-done.18, bf16[128,3072]{1,0:T(8,128)(2,1)S(1)} %collective-permute-done.1.a_ref, bf16[128,3072]{1,0:T(8,128)(2,1)S(1)} %collective-permute-done.5.b_ref, bf16[4,32,768]{2,1,0:T(8,128)(2,1)S(1)} %bitcast.23, ...), custom_call_target="tpu_custom_call" | custom-call | flops 3623878656 | bytes 14155776 | tf_op jit(solution)/shard_map/pallas_call | solution.py:310
  47.9 2.1 %all-to-all-done.video_hbm = bf16[8,128,384]{2,1,0:T(8,128)(2,1)S(1)} async-done(((bf16[8,128,384]{2,1,0:T(8,128)(2,1)}), bf16[8,128,384]{2,1,0:T(8,128)(2,1)S(1)}, u32[]{:S(2)}, u32[]{:S(2)}) %all-to-all-start) | async-done | bytes 786464 | tf_op jit(solution)/shard_map/all_to_all | solution.py:587
  50.0 37.3 %all_to_all.20.video_hbm.text_hbm = bf16[8,224,384]{2,1,0:T(8,128)(2,1)S(1)} all-to-all(bf16[8,224,384]{2,1,0:T(8,128)(2,1)S(1)} %bitcast.19), channel_id=1, replica_groups=mesh['job'=4,'seq'=8] {'seq'}, dimensions={0} | all-to-all | bytes 2752512 | tf_op jit(solution)/shard_map/all_to_all | solution.py:587
  87.4 5.0 %shard_map.161 = bf16[8,192,128]{2,1,0:T(8,128)(2,1)} custom-call(s32[4]{0:T(128)S(1)} %copy-done.15, s32[4,8]{1,0:T(4,128)S(1)} %copy-done.14, bf16[8,224,384]{2,1,0:T(8,128)(2,1)S(1)} %all_to_all.20.video_hbm.text_hbm, bf16[8,224,384]{2,1,0:T(8,128)(2,1)S(1)} %all_to_all.20.video_hbm.text_hbm), custom_call_target="tpu_custom_call" | custom-call | flops 838860800 | bytes 3145728 | tf_op jit(solution)/shard_map/pallas_call | solution.py:453
  93.5 3.7 %all-to-all-start.2 = ((bf16[8,192,128]{2,1,0:T(8,128)(2,1)}), bf16[8,192,128]{2,1,0:T(8,128)(2,1)S(1)}, u32[]{:S(2)}, u32[]{:S(2)}) async-start(bf16[8,192,128]{2,1,0:T(8,128)(2,1)} %shard_map.161), calls=%async_computation.2 | async-start | bytes 786432 | tf_op jit(solution)/shard_map/all_to_all | solution.py:587
  99.7 5.3 %shard_map.162 = bf16[8,384,128]{2,1,0:T(8,128)(2,1)} custom-call(s32[4]{0:T(128)S(1)} %copy-done.15, s32[4,8]{1,0:T(4,128)S(1)} %copy-done.14, bf16[8,128,384]{2,1,0:T(8,128)(2,1)S(1)} %copy-done.8, bf16[8,224,384]{2,1,0:T(8,128)(2,1)S(1)} %copy-done.4), custom_call_target="tpu_custom_call" | custom-call | flops 838860800 | bytes 3145728 | tf_op jit(solution)/shard_map/pallas_call | solution.py:453
  105.0 3.4 %all-to-all-done.2.refs_0_ = bf16[8,192,128]{2,1,0:T(8,128)(2,1)S(1)} async-done(((bf16[8,192,128]{2,1,0:T(8,128)(2,1)}), bf16[8,192,128]{2,1,0:T(8,128)(2,1)S(1)}, u32[]{:S(2)}, u32[]{:S(2)}) %all-to-all-start.2) | async-done | bytes 393248 | tf_op jit(solution)/shard_map/all_to_all | solution.py:587
  108.4 1.8 %shard_map.163 = bf16[192,3072]{1,0:T(8,128)(2,1)} custom-call(bf16[8,192,128]{2,1,0:T(8,128)(2,1)S(1)} %all-to-all-done.2.refs_0_, bf16[512,3072]{1,0:T(8,128)(2,1)S(1)} %bitcast.10), custom_call_target="tpu_custom_call" | custom-call | flops 603979776 | bytes 5505024 | tf_op jit(solution)/shard_map/pallas_call | solution.py:487
  110.2 4.2 %all-to-all-start.3 = ((bf16[8,384,128]{2,1,0:T(8,128)(2,1)}), bf16[8,384,128]{2,1,0:T(8,128)(2,1)}, u32[]{:S(2)}, u32[]{:S(2)}) async-start(bf16[8,384,128]{2,1,0:T(8,128)(2,1)} %shard_map.162), calls=%async_computation.3 | async-start | bytes 1572864 | tf_op jit(solution)/shard_map/all_to_all | solution.py:587
  114.4 3.1 %shard_map.164 = bf16[192,3072]{1,0:T(8,128)(2,1)} custom-call(bf16[8,192,128]{2,1,0:T(8,128)(2,1)S(1)} %all-to-all-done.2.refs_0_, bf16[512,3072]{1,0:T(8,128)(2,1)S(1)} %bitcast.11, bf16[192,3072]{1,0:T(8,128)(2,1)} %collective-permute-done.9.refs_2_), custom_call_target="tpu_custom_call" | custom-call | flops 603979776 | bytes 5505024 | tf_op jit(solution)/shard_map/pallas_call | solution.py:487
  117.5 1.5 collective-permute-start.10
  119.1 16.5 %all-to-all-done.3.refs_0_ = bf16[8,384,128]{2,1,0:T(8,128)(2,1)} async-done(((bf16[8,384,128]{2,1,0:T(8,128)(2,1)}), bf16[8,384,128]{2,1,0:T(8,128)(2,1)}, u32[]{:S(2)}, u32[]{:S(2)}) %all-to-all-start.3) | async-done | bytes 786464 | tf_op jit(solution)/shard_map/all_to_all | solution.py:587
  135.5 10.7 %collective-permute-done.10.chip_hbm = bf16[192,3072]{1,0:T(8,128)(2,1)} collective-permute-done((bf16[192,3072]{1,0:T(8,128)(2,1)}, bf16[192,3072]{1,0:T(8,128)(2,1)}, u32[]{:S(2)}, u32[]{:S(2)}) %collective-permute-start.10) | collective-permute-done | bytes 1179680 | tf_op jit(solution)/shard_map/ppermute | solution.py:584
  146.2 2.0 %shard_map.165 = (bf16[192,3072]{1,0:T(8,128)(2,1)S(1)}, bf16[64,3072]{1,0:T(8,128)(2,1)S(1)}) custom-call(bf16[8,384,128]{2,1,0:T(8,128)(2,1)} %all-to-all-done.3.refs_0_, bf16[512,3072]{1,0:T(8,128)(2,1)S(1)} %bitcast.12), custom_call_target="tpu_custom_call" | custom-call | flops 603979776 | bytes 5505024 | tf_op jit(solution)/shard_map/pallas_call | solution.py:487
  148.4 2.8 %collective-permute-done.11.refs_2_ = bf16[192,3072]{1,0:T(8,128)(2,1)S(1)} collective-permute-done((bf16[192,3072]{1,0:T(8,128)(2,1)S(1)}, bf16[192,3072]{1,0:T(8,128)(2,1)S(1)}, u32[]{:S(2)}, u32[]{:S(2)}) %collective-permute-start.11) | collective-permute-done | bytes 1179680 | tf_op jit(solution)/shard_map/ppermute | solution.py:581
  151.2 2.0 %shard_map.166.part_ref = bf16[192,3072]{1,0:T(8,128)(2,1)S(1)} custom-call(bf16[8,384,128]{2,1,0:T(8,128)(2,1)} %all-to-all-done.3.refs_0_, bf16[512,3072]{1,0:T(8,128)(2,1)S(1)} %bitcast.13, bf16[192,3072]{1,0:T(8,128)(2,1)S(1)} %collective-permute-done.11.refs_2_), custom_call_target="tpu_custom_call" | custom-call | flops 603979776 | bytes 5505024 | tf_op jit(solution)/shard_map/pallas_call | solution.py:487
  153.2 2.9 %shard_map.167 = (bf16[1,128,3072]{2,1,0:T(8,128)(2,1)}, bf16[1,64,3072]{2,1,0:T(8,128)(2,1)}) custom-call(s32[4]{0:T(128)S(1)} %copy-done.15, s32[4,8]{1,0:T(4,128)S(1)} %copy-done.14, bf16[1,128,3072]{2,1,0:T(8,128)(2,1)S(1)} %copy-done.6, bf16[192,3072]{1,0:T(8,128)(2,1)S(1)} %shard_map.166.part_ref, bf16[192,3072]{1,0:T(8,128)(2,1)} %collective-permute-done.10.chip_hbm, ...), custom_call_target="tpu_custom_call" | custom-call | flops 3538944 | bytes 5898240 | tf_op jit(solution)/shard_map/pallas_call | solution.py:536
  (59 shorter events, 9.9 us)
Async XLA Ops:
  0.6 14.5 %collective-permute-start = (bf16[128,3072]{1,0:T(8,128)(2,1)}, bf16[128,3072]{1,0:T(8,128)(2,1)S(1)}, u32[]{:S(2)}, u32[]{:S(2)}) collective-permute-start(bf16[128,3072]{1,0:T(8,128)(2,1)} %bitcast.16), channel_id=1, source_target_pairs={{0,8},{8,0},{16,24},{24,16},{1,9},{9,1},{17,25},{25,17},{2,10},{10... | collective-permute-start | bytes 2359304 | tf_op jit(solution)/shard_map/ppermute | solution.py:581
  3.0 12.2 %copy-start.5 = (bf16[1,128,3072]{2,1,0:T(8,128)(2,1)S(1)}, bf16[1,128,3072]{2,1,0:T(8,128)(2,1)}, u32[]{:S(2)}) copy-start(bf16[1,128,3072]{2,1,0:T(8,128)(2,1)} %video_ref.1) | copy-start | bytes 2359300
  3.0 12.2 %copy-start.10 = (f32[4,3072]{1,0:T(4,128)S(1)}, f32[4,3072]{1,0:T(4,128)}, u32[]{:S(2)}) copy-start(f32[4,3072]{1,0:T(4,128)} %shift_ref.3) | copy-start | bytes 147460
  3.0 12.2 %copy-start.11 = (f32[4,3072]{1,0:T(4,128)S(1)}, f32[4,3072]{1,0:T(4,128)}, u32[]{:S(2)}) copy-start(f32[4,3072]{1,0:T(4,128)} %scale_ref.3) | copy-start | bytes 147460
  3.1 20.2 %collective-permute-start.3 = (bf16[32,4096]{1,0:T(8,128)(2,1)S(1)}, bf16[32,4096]{1,0:T(8,128)(2,1)S(1)}, u32[]{:S(2)}, u32[]{:S(2)}) collective-permute-start(bf16[32,4096]{1,0:T(8,128)(2,1)S(1)} %shard_map.159), channel_id=1, source_target_pairs={{0,16},{8,24},{16,0},{24,8},{1,17},{9,25},{17,1},{25,9},{2,18},{10... | collective-permute-start | bytes 786440 | tf_op jit(solution)/shard_map/ppermute | solution.py:584
  5.6 17.6 %collective-permute-start.2 = (bf16[32,4096]{1,0:T(8,128)(2,1)S(1)}, bf16[32,4096]{1,0:T(8,128)(2,1)S(1)}, u32[]{:S(2)}, u32[]{:S(2)}) collective-permute-start(bf16[32,4096]{1,0:T(8,128)(2,1)S(1)} %shard_map.159), channel_id=1, source_target_pairs={{0,8},{8,0},{16,24},{24,16},{1,9},{9,1},{17,25},{25,17},{2,10},{10... | collective-permute-start | bytes 786440 | tf_op jit(solution)/shard_map/ppermute | solution.py:581
  5.9 27.4 %collective-permute-start.1 = (bf16[128,3072]{1,0:T(8,128)(2,1)}, bf16[128,3072]{1,0:T(8,128)(2,1)S(1)}, u32[]{:S(2)}, u32[]{:S(2)}) collective-permute-start(bf16[128,3072]{1,0:T(8,128)(2,1)} %bitcast.17), channel_id=1, source_target_pairs={{0,16},{8,24},{16,0},{24,8},{1,17},{9,25},{17,1},{25,9},{2,18},{10... | collective-permute-start | bytes 2359304 | tf_op jit(solution)/shard_map/ppermute | solution.py:584
  23.3 6.0 %collective-permute-start.4 = (bf16[32,4096]{1,0:T(8,128)(2,1)S(1)}, bf16[32,4096]{1,0:T(8,128)(2,1)S(1)}, u32[]{:S(2)}, u32[]{:S(2)}) collective-permute-start(bf16[32,4096]{1,0:T(8,128)(2,1)S(1)} %collective-permute-done.3), channel_id=1, source_target_pairs={{0,8},{8,0},{16,24},{24,16},{1,9},{9,1},{17,25},{25,17},{2,10},{10... | collective-permute-start | bytes 786440 | tf_op jit(solution)/shard_map/ppermute | solution.py:581
  23.3 26.8 %all-to-all-start = ((bf16[8,128,384]{2,1,0:T(8,128)(2,1)}), bf16[8,128,384]{2,1,0:T(8,128)(2,1)S(1)}, u32[]{:S(2)}, u32[]{:S(2)}) async-start(bf16[8,128,384]{2,1,0:T(8,128)(2,1)} %bitcast.2), calls=%async_computation | async-start | bytes 1572864 | tf_op jit(solution)/shard_map/all_to_all | solution.py:587
  29.2 12.9 %copy-start.2 = (bf16[3072,4,3,128]{3,0,1,2:T(8,128)(2,1)S(1)}, bf16[3072,4,3,128]{3,0,1,2:T(8,128)(2,1)}, u32[]{:S(2)}) copy-start(bf16[3072,4,3,128]{3,0,1,2:T(8,128)(2,1)} %copy.19) | copy-start | bytes 28311556
  29.2 12.9 %copy-start.18 = (s32[4]{0:T(128)S(1)}, s32[4]{0:T(128)}, u32[]{:S(2)}) copy-start(s32[4]{0:T(128)} %holder_ref.1) | copy-start | bytes 52
  33.3 8.8 %collective-permute-start.5 = (bf16[128,3072]{1,0:T(8,128)(2,1)S(1)}, bf16[128,3072]{1,0:T(8,128)(2,1)S(1)}, u32[]{:S(2)}, u32[]{:S(2)}) collective-permute-start(bf16[128,3072]{1,0:T(8,128)(2,1)S(1)} %collective-permute-done.1.a_ref), channel_id=1, source_target_pairs={{0,8},{8,0},{16,24},{24,16},{1,9},{9,1},{17,25},{25,17},{2,10},{10... | collective-permute-start | bytes 2359304 | tf_op jit(solution)/shard_map/ppermute | solution.py:581
  33.5 7.1 %collective-permute-start.7 = (bf16[4,32,768]{2,1,0:T(8,128)(2,1)S(1)}, bf16[4,32,768]{2,1,0:T(8,128)(2,1)S(1)}, u32[]{:S(2)}, u32[]{:S(2)}) collective-permute-start(bf16[4,32,768]{2,1,0:T(8,128)(2,1)S(1)} %bitcast.21), channel_id=1, source_target_pairs={{0,16},{8,24},{16,0},{24,8},{1,17},{9,25},{17,1},{25,9},{2,18},{10... | collective-permute-start | bytes 589832 | tf_op jit(solution)/shard_map/ppermute | solution.py:584
  35.1 5.6 %collective-permute-start.6 = (bf16[4,32,768]{2,1,0:T(8,128)(2,1)S(1)}, bf16[4,32,768]{2,1,0:T(8,128)(2,1)S(1)}, u32[]{:S(2)}, u32[]{:S(2)}) collective-permute-start(bf16[4,32,768]{2,1,0:T(8,128)(2,1)S(1)} %bitcast.22), channel_id=1, source_target_pairs={{0,8},{8,0},{16,24},{24,16},{1,9},{9,1},{17,25},{25,17},{2,10},{10... | collective-permute-start | bytes 589832 | tf_op jit(solution)/shard_map/ppermute | solution.py:581
  40.6 1.4 collective-permute-start.8
  47.9 39.5 %copy-start.14 = (s32[4,8]{1,0:T(4,128)S(1)}, s32[4,8]{1,0:T(4,128)}, u32[]{:S(2)}) copy-start(s32[4,8]{1,0:T(4,128)} %splits_ref.5) | copy-start | bytes 388
  47.9 39.5 %copy-start.15 = (s32[4]{0:T(128)S(1)}, s32[4]{0:T(128)}, u32[]{:S(2)}) copy-start(s32[4]{0:T(128)} %count_ref.5) | copy-start | bytes 52
  50.0 37.4 %copy-start.7 = (bf16[8,128,384]{2,1,0:T(8,128)(2,1)}, bf16[8,128,384]{2,1,0:T(8,128)(2,1)S(1)}, u32[]{:S(2)}) copy-start(bf16[8,128,384]{2,1,0:T(8,128)(2,1)S(1)} %all-to-all-done.video_hbm) | copy-start | bytes 2359300
  93.5 14.9 %copy-start = (bf16[4,128,3072]{2,1,0:T(8,128)(2,1)S(1)}, bf16[4,128,3072]{2,1,0:T(8,128)(2,1)}, u32[]{:S(2)}) copy-start(bf16[4,128,3072]{2,1,0:T(8,128)(2,1)} %param.29) | copy-start | bytes 9437188
  93.5 14.9 %all-to-all-start.2 = ((bf16[8,192,128]{2,1,0:T(8,128)(2,1)}), bf16[8,192,128]{2,1,0:T(8,128)(2,1)S(1)}, u32[]{:S(2)}, u32[]{:S(2)}) async-start(bf16[8,192,128]{2,1,0:T(8,128)(2,1)} %shard_map.161), calls=%async_computation.2 | async-start | bytes 786432 | tf_op jit(solution)/shard_map/all_to_all | solution.py:587
  110.2 4.2 %collective-permute-start.9 = (bf16[192,3072]{1,0:T(8,128)(2,1)}, bf16[192,3072]{1,0:T(8,128)(2,1)}, u32[]{:S(2)}, u32[]{:S(2)}) collective-permute-start(bf16[192,3072]{1,0:T(8,128)(2,1)} %shard_map.163), channel_id=1, source_target_pairs={{0,8},{8,0},{16,24},{24,16},{1,9},{9,1},{17,25},{25,17},{2,10},{10... | collective-permute-start | bytes 3538952 | tf_op jit(solution)/shard_map/ppermute | solution.py:581
  110.2 25.3 %all-to-all-start.3 = ((bf16[8,384,128]{2,1,0:T(8,128)(2,1)}), bf16[8,384,128]{2,1,0:T(8,128)(2,1)}, u32[]{:S(2)}, u32[]{:S(2)}) async-start(bf16[8,384,128]{2,1,0:T(8,128)(2,1)} %shard_map.162), calls=%async_computation.3 | async-start | bytes 1572864 | tf_op jit(solution)/shard_map/all_to_all | solution.py:587
  117.5 28.7 %collective-permute-start.10 = (bf16[192,3072]{1,0:T(8,128)(2,1)}, bf16[192,3072]{1,0:T(8,128)(2,1)}, u32[]{:S(2)}, u32[]{:S(2)}) collective-permute-start(bf16[192,3072]{1,0:T(8,128)(2,1)} %shard_map.164), channel_id=1, source_target_pairs={{0,16},{8,24},{16,0},{24,8},{1,17},{9,25},{17,1},{25,9},{2,18},{10... | collective-permute-start | bytes 3538952 | tf_op jit(solution)/shard_map/ppermute | solution.py:584
  148.3 2.9 %collective-permute-start.11 = (bf16[192,3072]{1,0:T(8,128)(2,1)S(1)}, bf16[192,3072]{1,0:T(8,128)(2,1)S(1)}, u32[]{:S(2)}, u32[]{:S(2)}) collective-permute-start(bf16[192,3072]{1,0:T(8,128)(2,1)S(1)} %get-tuple-element.22), channel_id=1, source_target_pairs={{0,8},{8,0},{16,24},{24,16},{1,9},{9,1},{17,25},{25,17},{2,10},{10... | collective-permute-start | bytes 3538952 | tf_op jit(solution)/shard_map/ppermute | solution.py:581
  (11 other events, 53.5 us)

commit v3 on v2

--- a/solution.py
+++ b/solution.py
@@ -309,7 +309,7 @@
     group, width = weights.shape[1:3]
     return pl.pallas_call(
         kernel,
-        out_shape=jax.ShapeDtypeStruct((2, group, rows_out, 3 * HD), jnp.bfloat16),
+        out_shape=pltpu.HBM((2, group, rows_out, 3 * HD), jnp.bfloat16),
         in_specs=specs + [vmem_spec()] * 3,
         out_specs=vmem_spec(),
         scratch_shapes=[pltpu.VMEM((rows_in, width), jnp.bfloat16), *extra],
@@ -461,37 +461,60 @@
     )(count, splits, video_qkv, text_qkv)
 
 
-def out_kernel(which, with_slots, added, *refs):
-    heads_ref, w_ref, out_ref = refs[0], refs[1], refs[2 + added]
-    group = w_ref.shape[0] // HD
-    count, width = out_ref.shape
+def project_rows(heads_ref, w_ref, which, count, put):
+    group, width = w_ref.shape[0] // HD, w_ref.shape[1]
     rows = jnp.concatenate([heads_ref[which * group + h, 0:count] for h in range(group)], axis=1)
     for lo in range(0, width, width // 4):
         cols = slice(lo, lo + width // 4)
-        total = jnp.dot(rows, w_ref[:, cols], preferred_element_type=jnp.float32)
-        if added:
-            total = total + refs[2][:, cols].astype(jnp.float32)
-        out_ref[:, cols] = total.astype(jnp.bfloat16)
-    if with_slots:
-        slot_ref = refs[3 + added]
-        slots = slot_ref.shape[0]
+        put(cols, jnp.dot(rows, w_ref[:, cols], preferred_element_type=jnp.float32))
+
+
+def give_kernel(heads_ref, w_ref, *out_refs):
+    size = out_refs[0].shape[0]
+
+    def put(cols, total):
+        for i, ref in enumerate(out_refs):
+            ref[:, cols] = total[i * size : (i + 1) * size].astype(jnp.bfloat16)
+
+    project_rows(heads_ref, w_ref, 1, size * len(out_refs), put)
+
+
+def keep_kernel(pieces, heads_ref, w_ref, *refs):
+    out_ref = refs[pieces]
+    size = refs[0].shape[0]
+
+    def put(cols, total):
+        for i in range(pieces):
+            part = total[i * size : (i + 1) * size] + refs[i][:, cols].astype(jnp.float32)
+            out_ref[i * size : (i + 1) * size, cols] = part.astype(jnp.bfloat16)
+
+    count = size * pieces
+    project_rows(heads_ref, w_ref, 0, count, put)
+    if len(refs) > pieces + 1:
+        slot_ref = refs[pieces + 1]
+        slots, width = slot_ref.shape
         for block in range(width // HD):
             lo = count + (block % 3) * slots
             slot_ref[:, block * HD : (block + 1) * HD] = heads_ref[block // 3, lo : lo + slots]
 
 
-def project_out(heads, rows, which, weights, *added, slots=0):
+def out_call(kernel, rows, weights, inputs, outs):
     depth, width = weights.shape
-    out = jax.ShapeDtypeStruct((rows, width), jnp.bfloat16)
-    slot_out = jax.ShapeDtypeStruct((slots, width), jnp.bfloat16)
     return pl.pallas_call(
-        functools.partial(out_kernel, which, slots > 0, len(added)),
-        out_shape=(out, slot_out) if slots else out,
-        in_specs=[vmem_spec()] * (2 + len(added)),
-        out_specs=(vmem_spec(), vmem_spec()) if slots else vmem_spec(),
+        kernel,
+        out_shape=tuple(jax.ShapeDtypeStruct((n, width), jnp.bfloat16) for n in outs),
+        in_specs=[vmem_spec()] * len(inputs),
+        out_specs=(vmem_spec(),) * len(outs),
         compiler_params=params(8),
         cost_estimate=cost(2 * rows * depth * width, 2 * (depth + 2 * rows) * width),
-    )(heads, weights, *added)
+    )(*inputs)
+
+
+def project_out(heads, rows, pieces, slots, weights, to_core):
+    given = out_call(give_kernel, rows, weights, (heads, weights), (rows // pieces,) * pieces)
+    kernel = functools.partial(keep_kernel, pieces)
+    outs = (rows, slots) if slots else (rows,)
+    return out_call(kernel, rows, weights, (heads, weights, *map(to_core, given)), outs)
 
 
 def final_kernel(
@@ -624,6 +647,7 @@
         k_gain,
     )
     second = over_seq(after(send.reshape(shard_count, -1, 3 * HD), local_qkv))
+    second = pltpu.with_memory_space_constraint(second, pltpu.HBM)
 
     remote_mixed = attend_pair(True, text_count, text_splits, second, second, vrows, trows)
     remote_back = over_seq(remote_mixed)
@@ -634,12 +658,11 @@
     rows = vrows + 2 * trows
     remote_back = after(remote_back, local_mixed)
     local_back = over_seq(after(local_mixed, remote_back))
-    from_core = to_core(project_out(remote_back, rows, 1, out_weight))
-    crossing = project_out(remote_back, rows, 0, out_weight, from_core)
+    (crossing,) = project_out(remote_back, rows, 1, 0, out_weight, to_core)
     from_chip = to_chip(crossing)
-    local_back = after(local_back, from_chip)
-    near_part, slot_rows = project_out(local_back, rows, 1, out_weight, slots=2 * trows)
-    local_part = project_out(local_back, rows, 0, out_weight, to_core(near_part))
+    local_part, slot_rows = project_out(
+        after(local_back, crossing), rows, 3, 2 * trows, out_weight, to_core
+    )
     return finish(
         text_count, text_splits, video, local_part, from_chip, mod_gate, slot_rows
     )

time: 157 us -> 151 us (0.962)
  waiting for transfers between devices: 42.6 us -> 34.5 us
  Pallas kernels: 32.3 us -> 35.3 us
  local copies, waits for them, and re-layouts: 18 us -> 15.5 us
  blocking collectives: 37.3 us -> 38.9 us
    ppermute x4, waiting for transfers between devices: 16.3 us -> 9.36 us  [to_chip(): return lax.ppermute(x, 'job', [(i, i ^ 2) for i in range(job_count)])]
    unnamed x41 -> x37, local copies, waits for them, and re-layouts: 18 us -> 15.5 us
    pallas_call x2, Pallas kernels: 10.2 us -> 12.1 us  [attend_pair(): pl.pallas_call(functools.partial(attention_kernel, far, vrows + (trows if...]
    ppermute x8 -> x10, waiting for transfers between devices: 4.29 us -> 3.7 us  [to_core(): return lax.ppermute(x, 'job', [(i, i ^ 1) for i in range(job_count)])]
  transfers between devices with their start and end apart: 15 -> 17, of which waited for: 7 -> 9; matrix products, arithmetic and copies ran while one was open for 8% -> 9% of each run, Pallas kernels for 12% -> 16%
where the time goes in v3:
time: 151 us
  blocking collectives  38.9 us (26%)
  Pallas kernels  35.3 us (23%)
  waiting for transfers between devices  34.5 us (23%)
  starting transfers between devices  21.6 us (14%)
  local copies, waits for them, and re-layouts  15.5 us (10%)
  matrix products  3.97 us (3%)
    all_to_all x1, blocking collectives, over_seq(): return lax.all_to_all(x, 'seq', split_axis=0, concat_axis=0, tiled=False)  38.9 us
    all_to_all x3, waiting for transfers between devices, over_seq(): return lax.all_to_all(x, 'seq', split_axis=0, concat_axis=0, tiled=False)  21.4 us
    unnamed x37, local copies, waits for them, and re-layouts  15.5 us
    all_to_all x3, starting transfers between devices, over_seq(): return lax.all_to_all(x, 'seq', split_axis=0, concat_axis=0, tiled=False)  13.9 us
    pallas_call x2, Pallas kernels, attend_pair(): pl.pallas_call(functools.partial(attention_kernel, far, vrows + (trows if...  12.1 us
    pallas_call x2, Pallas kernels, qkv_call(): pl.pallas_call(kernel, out_shape=pltpu.HBM((2, group, rows_out, 3 * HD),...  11.3 us
    ppermute x4, waiting for transfers between devices, to_chip(): return lax.ppermute(x, 'job', [(i, i ^ 2) for i in range(job_count)])  9.36 us
    pallas_call x4, Pallas kernels, out_call(): pl.pallas_call(kernel, out_shape=tuple((jax.ShapeDtypeStruct((n, width),...  8.85 us
  transfers between devices with their start and end apart: 17, of which 9 were waited for; matrix products, arithmetic and copies ran while one was open for 9% of the time, Pallas kernels for 16%

profile of v3, /device:TPU:0, one launch (start us, length us, event | category | flops | bytes accessed | tf_op | source)
XLA Modules:
  0.0 150.7 jit_solution(2286051287979667924)
XLA Ops:
  3.1 2.6 %collective-permute-start.3 = (bf16[32,4096]{1,0:T(8,128)(2,1)S(1)}, bf16[32,4096]{1,0:T(8,128)(2,1)S(1)}, u32[]{:S(2)}, u32[]{:S(2)}) collective-permute-start(bf16[32,4096]{1,0:T(8,128)(2,1)S(1)} %shard_map.159), channel_id=1, source_target_pairs={{0,16},{8,24},{16,0},{24,8},{1,17},{9,25},{17,1},{25,9},{2,18},{10... | collective-permute-start | bytes 786440 | tf_op jit(solution)/shard_map/ppermute | solution.py:607
  6.2 8.9 %copy.19 = bf16[3072,4,3,128]{3,0,1,2:T(8,128)(2,1)} copy(bf16[3072,4,3,128]{3,1,2,0:T(4,128)(2,1)} %param.26) | data formatting | bytes 18874368 | tf_op args[11]
  15.2 3.7 %copy-done.1 = bf16[3072,4,3,128]{3,0,1,2:T(8,128)(2,1)S(1)} copy-done((bf16[3072,4,3,128]{3,0,1,2:T(8,128)(2,1)S(1)}, bf16[3072,4,3,128]{3,0,1,2:T(8,128)(2,1)}, u32[]{:S(2)}) %copy-start.1) | copy-done | bytes 9437208
  18.9 4.4 %shard_map.158 = bf16[2,4,128,384]{3,2,1,0:T(8,128)(2,1)} custom-call(bf16[128,3072]{1,0:T(8,128)(2,1)S(1)} %bitcast.18, bf16[128,3072]{1,0:T(8,128)(2,1)S(1)} %collective-permute-done.b_ref, f32[4,3072]{1,0:T(4,128)S(1)} %copy-done.8, f32[4,3072]{1,0:T(4,128)S(1)} %copy-done.9, bf16[3,4,3072,128]{3,2,1,0:T(8,128)(2,1)S(1)} %bitcast.14, ...), custom_call_target="tpu_custom_call" | custom-call | flops 2415919104 | bytes 12582912 | tf_op jit(solution)/shard_map/pallas_call | solution.py:310
  23.3 6.0 %all-to-all-start = ((bf16[8,128,384]{2,1,0:T(8,128)(2,1)}), bf16[8,128,384]{2,1,0:T(8,128)(2,1)S(1)}, u32[]{:S(2)}, u32[]{:S(2)}) async-start(bf16[8,128,384]{2,1,0:T(8,128)(2,1)} %bitcast.23), calls=%async_computation | async-start | bytes 1572864 | tf_op jit(solution)/shard_map/all_to_all | solution.py:610
  29.3 4.0 %fusion = bf16[128,768]{1,0:T(8,128)(2,1)S(1)} fusion(bf16[4096,768]{1,0:T(8,128)(2,1)} %param.24, bf16[32,4096]{1,0:T(8,128)(2,1)S(1)} %collective-permute-done.4, bf16[32,4096]{1,0:T(8,128)(2,1)S(1)} %collective-permute-done.3, bf16[32,4096]{1,0:T(8,128)(2,1)S(1)} %collective-permute-done.2, bf16[32,4096]{1,0:T(8,128)(2,1)S(1)} %shard_map.159, ...), kind=kOutput, calls=%fused_computation.2 | convolution fusion | flops 809697280 | bytes 7539712 | tf_op jit(solution)/shard_map/dot_general | solution.py:627
  33.5 1.5 %collective-permute-start.7 = (bf16[4,32,768]{2,1,0:T(8,128)(2,1)S(1)}, bf16[4,32,768]{2,1,0:T(8,128)(2,1)S(1)}, u32[]{:S(2)}, u32[]{:S(2)}) collective-permute-start(bf16[4,32,768]{2,1,0:T(8,128)(2,1)S(1)} %bitcast.20), channel_id=1, source_target_pairs={{0,16},{8,24},{16,0},{24,8},{1,17},{9,25},{17,1},{25,9},{2,18},{10... | collective-permute-start | bytes 589832 | tf_op jit(solution)/shard_map/ppermute | solution.py:607
  35.1 5.6 %collective-permute-done.7.t2_ref = bf16[4,32,768]{2,1,0:T(8,128)(2,1)S(1)} collective-permute-done((bf16[4,32,768]{2,1,0:T(8,128)(2,1)S(1)}, bf16[4,32,768]{2,1,0:T(8,128)(2,1)S(1)}, u32[]{:S(2)}, u32[]{:S(2)}) %collective-permute-start.7) | collective-permute-done | bytes 196640 | tf_op jit(solution)/shard_map/ppermute | solution.py:607
  40.6 1.4 collective-permute-done.8.t3_ref
  42.1 6.9 %shard_map.160 = bf16[2,4,224,384]{3,2,1,0:T(8,128)(2,1)} custom-call(s32[4]{0:T(128)S(1)} %copy-done.16, bf16[128,3072]{1,0:T(8,128)(2,1)S(1)} %collective-permute-done.1.a_ref, bf16[128,3072]{1,0:T(8,128)(2,1)S(1)} %collective-permute-done.5.b_ref, bf16[4,32,768]{2,1,0:T(8,128)(2,1)S(1)} %bitcast.22, ...), custom_call_target="tpu_custom_call" | custom-call | flops 3623878656 | bytes 14155776 | tf_op jit(solution)/shard_map/pallas_call | solution.py:310
  50.0 38.9 %all_to_all.20.video_hbm.text_hbm = bf16[8,224,384]{2,1,0:T(8,128)(2,1)} all-to-all(bf16[8,224,384]{2,1,0:T(8,128)(2,1)} %bitcast.24), channel_id=1, replica_groups=mesh['job'=4,'seq'=8] {'seq'}, dimensions={0} | all-to-all | bytes 2752512 | tf_op jit(solution)/shard_map/all_to_all | solution.py:610
  89.0 6.0 %shard_map.161 = bf16[8,192,128]{2,1,0:T(8,128)(2,1)} custom-call(s32[4]{0:T(128)S(1)} %copy-done.13, s32[4,8]{1,0:T(4,128)S(1)} %copy-done.12, bf16[8,224,384]{2,1,0:T(8,128)(2,1)} %all_to_all.20.video_hbm.text_hbm, bf16[8,224,384]{2,1,0:T(8,128)(2,1)} %all_to_all.20.video_hbm.text_hbm), custom_call_target="tpu_custom_call" | custom-call | flops 838860800 | bytes 3145728 | tf_op jit(solution)/shard_map/pallas_call | solution.py:453
  94.9 3.7 %all-to-all-start.2 = ((bf16[8,192,128]{2,1,0:T(8,128)(2,1)}), bf16[8,192,128]{2,1,0:T(8,128)(2,1)S(1)}, u32[]{:S(2)}, u32[]{:S(2)}) async-start(bf16[8,192,128]{2,1,0:T(8,128)(2,1)} %shard_map.161), calls=%async_computation.2 | async-start | bytes 786432 | tf_op jit(solution)/shard_map/all_to_all | solution.py:610
  99.8 6.2 %shard_map.162 = bf16[8,384,128]{2,1,0:T(8,128)(2,1)} custom-call(s32[4]{0:T(128)S(1)} %copy-done.13, s32[4,8]{1,0:T(4,128)S(1)} %copy-done.12, bf16[8,128,384]{2,1,0:T(8,128)(2,1)S(1)} %copy-done.6, bf16[8,224,384]{2,1,0:T(8,128)(2,1)} %all_to_all.20.video_hbm.text_hbm), custom_call_target="tpu_custom_call" | custom-call | flops 838860800 | bytes 3145728 | tf_op jit(solution)/shard_map/pallas_call | solution.py:453
  106.0 3.9 %all-to-all-done.2.heads_ref = bf16[8,192,128]{2,1,0:T(8,128)(2,1)S(1)} async-done(((bf16[8,192,128]{2,1,0:T(8,128)(2,1)}), bf16[8,192,128]{2,1,0:T(8,128)(2,1)S(1)}, u32[]{:S(2)}, u32[]{:S(2)}) %all-to-all-start.2) | async-done | bytes 393248 | tf_op jit(solution)/shard_map/all_to_all | solution.py:610
  109.8 1.8 %shard_map.163 = bf16[192,3072]{1,0:T(8,128)(2,1)} custom-call(bf16[8,192,128]{2,1,0:T(8,128)(2,1)S(1)} %all-to-all-done.2.heads_ref, bf16[512,3072]{1,0:T(8,128)(2,1)S(1)} %bitcast.10), custom_call_target="tpu_custom_call" | custom-call | flops 603979776 | bytes 5505024 | tf_op jit(solution)/shard_map/pallas_call | solution.py:503
  111.6 4.2 %all-to-all-start.3 = ((bf16[8,384,128]{2,1,0:T(8,128)(2,1)}), bf16[8,384,128]{2,1,0:T(8,128)(2,1)}, u32[]{:S(2)}, u32[]{:S(2)}) async-start(bf16[8,384,128]{2,1,0:T(8,128)(2,1)} %shard_map.162), calls=%async_computation.3 | async-start | bytes 1572864 | tf_op jit(solution)/shard_map/all_to_all | solution.py:610
  115.9 3.1 %shard_map.164 = bf16[192,3072]{1,0:T(8,128)(2,1)} custom-call(bf16[8,192,128]{2,1,0:T(8,128)(2,1)S(1)} %all-to-all-done.2.heads_ref, bf16[512,3072]{1,0:T(8,128)(2,1)S(1)} %bitcast.11, bf16[192,3072]{1,0:T(8,128)(2,1)} %collective-permute-done.9.refs_0_), custom_call_target="tpu_custom_call" | custom-call | flops 603979776 | bytes 5505024 | tf_op jit(solution)/shard_map/pallas_call | solution.py:503
  119.0 1.5 collective-permute-start.13
  120.5 16.5 %all-to-all-done.3.heads_ref = bf16[8,384,128]{2,1,0:T(8,128)(2,1)} async-done(((bf16[8,384,128]{2,1,0:T(8,128)(2,1)}), bf16[8,384,128]{2,1,0:T(8,128)(2,1)}, u32[]{:S(2)}, u32[]{:S(2)}) %all-to-all-start.3) | async-done | bytes 786464 | tf_op jit(solution)/shard_map/all_to_all | solution.py:610
  137.0 1.9 %shard_map.165 = (bf16[64,3072]{1,0:T(8,128)(2,1)S(1)}, bf16[64,3072]{1,0:T(8,128)(2,1)S(1)}, bf16[64,3072]{1,0:T(8,128)(2,1)S(1)}) custom-call(bf16[8,384,128]{2,1,0:T(8,128)(2,1)} %all-to-all-done.3.heads_ref, bf16[512,3072]{1,0:T(8,128)(2,1)S(1)} %bitcast.12), custom_call_target="tpu_custom_call" | custom-call | flops 603979776 | bytes 5505024 | tf_op jit(solution)/shard_map/pallas_call | solution.py:503
  141.8 2.0 %shard_map.166 = (bf16[192,3072]{1,0:T(8,128)(2,1)S(1)}, bf16[64,3072]{1,0:T(8,128)(2,1)S(1)}) custom-call(bf16[8,384,128]{2,1,0:T(8,128)(2,1)} %all-to-all-done.3.heads_ref, bf16[512,3072]{1,0:T(8,128)(2,1)S(1)} %bitcast.13, bf16[64,3072]{1,0:T(8,128)(2,1)S(1)} %collective-permute-done.10.refs_0_, bf16[64,3072]{1,0:T(8,128)(2,1)S(1)} %collective-permute-done.11.refs_1_, ...), custom_call_target="tpu_custom_call" | custom-call | flops 603979776 | bytes 5505024 | tf_op jit(solution)/shard_map/pallas_call | solution.py:503
  143.9 3.8 %collective-permute-done.13.chip_hbm = bf16[192,3072]{1,0:T(8,128)(2,1)} collective-permute-done((bf16[192,3072]{1,0:T(8,128)(2,1)}, bf16[192,3072]{1,0:T(8,128)(2,1)}, u32[]{:S(2)}, u32[]{:S(2)}) %collective-permute-start.13) | collective-permute-done | bytes 1179680 | tf_op jit(solution)/shard_map/ppermute | solution.py:607
  147.7 2.9 %shard_map.167 = (bf16[1,128,3072]{2,1,0:T(8,128)(2,1)}, bf16[1,64,3072]{2,1,0:T(8,128)(2,1)}) custom-call(s32[4]{0:T(128)S(1)} %copy-done.13, s32[4,8]{1,0:T(4,128)S(1)} %copy-done.12, bf16[1,128,3072]{2,1,0:T(8,128)(2,1)S(1)} %copy-done.4, bf16[192,3072]{1,0:T(8,128)(2,1)S(1)} %get-tuple-element.28.part_ref, ...), custom_call_target="tpu_custom_call" | custom-call | flops 3538944 | bytes 5898240 | tf_op jit(solution)/shard_map/pallas_call | solution.py:559
  (59 shorter events, 8.4 us)
Async XLA Ops:
  0.6 14.5 %collective-permute-start = (bf16[128,3072]{1,0:T(8,128)(2,1)}, bf16[128,3072]{1,0:T(8,128)(2,1)S(1)}, u32[]{:S(2)}, u32[]{:S(2)}) collective-permute-start(bf16[128,3072]{1,0:T(8,128)(2,1)} %bitcast.16), channel_id=1, source_target_pairs={{0,8},{8,0},{16,24},{24,16},{1,9},{9,1},{17,25},{25,17},{2,10},{10... | collective-permute-start | bytes 2359304 | tf_op jit(solution)/shard_map/ppermute | solution.py:604
  3.0 12.2 %copy-start.3 = (bf16[1,128,3072]{2,1,0:T(8,128)(2,1)S(1)}, bf16[1,128,3072]{2,1,0:T(8,128)(2,1)}, u32[]{:S(2)}) copy-start(bf16[1,128,3072]{2,1,0:T(8,128)(2,1)} %video_ref.1) | copy-start | bytes 2359300
  3.1 20.2 %collective-permute-start.3 = (bf16[32,4096]{1,0:T(8,128)(2,1)S(1)}, bf16[32,4096]{1,0:T(8,128)(2,1)S(1)}, u32[]{:S(2)}, u32[]{:S(2)}) collective-permute-start(bf16[32,4096]{1,0:T(8,128)(2,1)S(1)} %shard_map.159), channel_id=1, source_target_pairs={{0,16},{8,24},{16,0},{24,8},{1,17},{9,25},{17,1},{25,9},{2,18},{10... | collective-permute-start | bytes 786440 | tf_op jit(solution)/shard_map/ppermute | solution.py:607
  5.6 17.6 %collective-permute-start.2 = (bf16[32,4096]{1,0:T(8,128)(2,1)S(1)}, bf16[32,4096]{1,0:T(8,128)(2,1)S(1)}, u32[]{:S(2)}, u32[]{:S(2)}) collective-permute-start(bf16[32,4096]{1,0:T(8,128)(2,1)S(1)} %shard_map.159), channel_id=1, source_target_pairs={{0,8},{8,0},{16,24},{24,16},{1,9},{9,1},{17,25},{25,17},{2,10},{10... | collective-permute-start | bytes 786440 | tf_op jit(solution)/shard_map/ppermute | solution.py:604
  5.9 27.4 %collective-permute-start.1 = (bf16[128,3072]{1,0:T(8,128)(2,1)}, bf16[128,3072]{1,0:T(8,128)(2,1)S(1)}, u32[]{:S(2)}, u32[]{:S(2)}) collective-permute-start(bf16[128,3072]{1,0:T(8,128)(2,1)} %bitcast.17), channel_id=1, source_target_pairs={{0,16},{8,24},{16,0},{24,8},{1,17},{9,25},{17,1},{25,9},{2,18},{10... | collective-permute-start | bytes 2359304 | tf_op jit(solution)/shard_map/ppermute | solution.py:607
  23.3 6.0 %collective-permute-start.4 = (bf16[32,4096]{1,0:T(8,128)(2,1)S(1)}, bf16[32,4096]{1,0:T(8,128)(2,1)S(1)}, u32[]{:S(2)}, u32[]{:S(2)}) collective-permute-start(bf16[32,4096]{1,0:T(8,128)(2,1)S(1)} %collective-permute-done.3), channel_id=1, source_target_pairs={{0,8},{8,0},{16,24},{24,16},{1,9},{9,1},{17,25},{25,17},{2,10},{10... | collective-permute-start | bytes 786440 | tf_op jit(solution)/shard_map/ppermute | solution.py:604
  23.3 26.8 %all-to-all-start = ((bf16[8,128,384]{2,1,0:T(8,128)(2,1)}), bf16[8,128,384]{2,1,0:T(8,128)(2,1)S(1)}, u32[]{:S(2)}, u32[]{:S(2)}) async-start(bf16[8,128,384]{2,1,0:T(8,128)(2,1)} %bitcast.23), calls=%async_computation | async-start | bytes 1572864 | tf_op jit(solution)/shard_map/all_to_all | solution.py:610
  29.2 12.9 %copy-start.2 = (bf16[3072,4,3,128]{3,0,1,2:T(8,128)(2,1)S(1)}, bf16[3072,4,3,128]{3,0,1,2:T(8,128)(2,1)}, u32[]{:S(2)}) copy-start(bf16[3072,4,3,128]{3,0,1,2:T(8,128)(2,1)} %copy.19) | copy-start | bytes 28311556
  29.2 12.9 %copy-start.16 = (s32[4]{0:T(128)S(1)}, s32[4]{0:T(128)}, u32[]{:S(2)}) copy-start(s32[4]{0:T(128)} %holder_ref.1) | copy-start | bytes 52
  33.3 8.8 %collective-permute-start.5 = (bf16[128,3072]{1,0:T(8,128)(2,1)S(1)}, bf16[128,3072]{1,0:T(8,128)(2,1)S(1)}, u32[]{:S(2)}, u32[]{:S(2)}) collective-permute-start(bf16[128,3072]{1,0:T(8,128)(2,1)S(1)} %collective-permute-done.1.a_ref), channel_id=1, source_target_pairs={{0,8},{8,0},{16,24},{24,16},{1,9},{9,1},{17,25},{25,17},{2,10},{10... | collective-permute-start | bytes 2359304 | tf_op jit(solution)/shard_map/ppermute | solution.py:604
  33.5 7.1 %collective-permute-start.7 = (bf16[4,32,768]{2,1,0:T(8,128)(2,1)S(1)}, bf16[4,32,768]{2,1,0:T(8,128)(2,1)S(1)}, u32[]{:S(2)}, u32[]{:S(2)}) collective-permute-start(bf16[4,32,768]{2,1,0:T(8,128)(2,1)S(1)} %bitcast.20), channel_id=1, source_target_pairs={{0,16},{8,24},{16,0},{24,8},{1,17},{9,25},{17,1},{25,9},{2,18},{10... | collective-permute-start | bytes 589832 | tf_op jit(solution)/shard_map/ppermute | solution.py:607
  35.0 5.6 %collective-permute-start.6 = (bf16[4,32,768]{2,1,0:T(8,128)(2,1)S(1)}, bf16[4,32,768]{2,1,0:T(8,128)(2,1)S(1)}, u32[]{:S(2)}, u32[]{:S(2)}) collective-permute-start(bf16[4,32,768]{2,1,0:T(8,128)(2,1)S(1)} %bitcast.21), channel_id=1, source_target_pairs={{0,8},{8,0},{16,24},{24,16},{1,9},{9,1},{17,25},{25,17},{2,10},{10... | collective-permute-start | bytes 589832 | tf_op jit(solution)/shard_map/ppermute | solution.py:604
  40.6 1.4 collective-permute-start.8
  49.0 40.0 %copy-start.12 = (s32[4,8]{1,0:T(4,128)S(1)}, s32[4,8]{1,0:T(4,128)}, u32[]{:S(2)}) copy-start(s32[4,8]{1,0:T(4,128)} %splits_ref.5) | copy-start | bytes 388
  49.0 40.0 %copy-start.13 = (s32[4]{0:T(128)S(1)}, s32[4]{0:T(128)}, u32[]{:S(2)}) copy-start(s32[4]{0:T(128)} %count_ref.5) | copy-start | bytes 52
  50.0 38.9 %copy-start.5 = (bf16[8,128,384]{2,1,0:T(8,128)(2,1)}, bf16[8,128,384]{2,1,0:T(8,128)(2,1)S(1)}, u32[]{:S(2)}) copy-start(bf16[8,128,384]{2,1,0:T(8,128)(2,1)S(1)} %all-to-all-done.video_hbm) | copy-start | bytes 2359300
  94.9 14.9 %copy-start = (bf16[4,128,3072]{2,1,0:T(8,128)(2,1)S(1)}, bf16[4,128,3072]{2,1,0:T(8,128)(2,1)}, u32[]{:S(2)}) copy-start(bf16[4,128,3072]{2,1,0:T(8,128)(2,1)} %param.29) | copy-start | bytes 9437188
  94.9 14.9 %all-to-all-start.2 = ((bf16[8,192,128]{2,1,0:T(8,128)(2,1)}), bf16[8,192,128]{2,1,0:T(8,128)(2,1)S(1)}, u32[]{:S(2)}, u32[]{:S(2)}) async-start(bf16[8,192,128]{2,1,0:T(8,128)(2,1)} %shard_map.161), calls=%async_computation.2 | async-start | bytes 786432 | tf_op jit(solution)/shard_map/all_to_all | solution.py:610
  111.6 4.2 %collective-permute-start.9 = (bf16[192,3072]{1,0:T(8,128)(2,1)}, bf16[192,3072]{1,0:T(8,128)(2,1)}, u32[]{:S(2)}, u32[]{:S(2)}) collective-permute-start(bf16[192,3072]{1,0:T(8,128)(2,1)} %shard_map.163), channel_id=1, source_target_pairs={{0,8},{8,0},{16,24},{24,16},{1,9},{9,1},{17,25},{25,17},{2,10},{10... | collective-permute-start | bytes 3538952 | tf_op jit(solution)/shard_map/ppermute | solution.py:604
  111.6 25.3 %all-to-all-start.3 = ((bf16[8,384,128]{2,1,0:T(8,128)(2,1)}), bf16[8,384,128]{2,1,0:T(8,128)(2,1)}, u32[]{:S(2)}, u32[]{:S(2)}) async-start(bf16[8,384,128]{2,1,0:T(8,128)(2,1)} %shard_map.162), calls=%async_computation.3 | async-start | bytes 1572864 | tf_op jit(solution)/shard_map/all_to_all | solution.py:610
  119.0 28.7 %collective-permute-start.13 = (bf16[192,3072]{1,0:T(8,128)(2,1)}, bf16[192,3072]{1,0:T(8,128)(2,1)}, u32[]{:S(2)}, u32[]{:S(2)}) collective-permute-start(bf16[192,3072]{1,0:T(8,128)(2,1)} %shard_map.164), channel_id=1, source_target_pairs={{0,16},{8,24},{16,0},{24,8},{1,17},{9,25},{17,1},{25,9},{2,18},{10... | collective-permute-start | bytes 3538952 | tf_op jit(solution)/shard_map/ppermute | solution.py:607
  138.9 1.8 %collective-permute-start.10 = (bf16[64,3072]{1,0:T(8,128)(2,1)S(1)}, bf16[64,3072]{1,0:T(8,128)(2,1)S(1)}, u32[]{:S(2)}, u32[]{:S(2)}) collective-permute-start(bf16[64,3072]{1,0:T(8,128)(2,1)S(1)} %get-tuple-element.25), channel_id=1, source_target_pairs={{0,8},{8,0},{16,24},{24,16},{1,9},{9,1},{17,25},{25,17},{2,10},{10... | collective-permute-start | bytes 1179656 | tf_op jit(solution)/shard_map/ppermute | solution.py:604
  139.0 2.3 %collective-permute-start.11 = (bf16[64,3072]{1,0:T(8,128)(2,1)S(1)}, bf16[64,3072]{1,0:T(8,128)(2,1)S(1)}, u32[]{:S(2)}, u32[]{:S(2)}) collective-permute-start(bf16[64,3072]{1,0:T(8,128)(2,1)S(1)} %get-tuple-element.26), channel_id=1, source_target_pairs={{0,8},{8,0},{16,24},{24,16},{1,9},{9,1},{17,25},{25,17},{2,10},{10... | collective-permute-start | bytes 1179656 | tf_op jit(solution)/shard_map/ppermute | solution.py:604
  139.5 2.3 %collective-permute-start.12 = (bf16[64,3072]{1,0:T(8,128)(2,1)S(1)}, bf16[64,3072]{1,0:T(8,128)(2,1)S(1)}, u32[]{:S(2)}, u32[]{:S(2)}) collective-permute-start(bf16[64,3072]{1,0:T(8,128)(2,1)S(1)} %get-tuple-element.27), channel_id=1, source_target_pairs={{0,8},{8,0},{16,24},{24,16},{1,9},{9,1},{17,25},{25,17},{2,10},{10... | collective-permute-start | bytes 1179656 | tf_op jit(solution)/shard_map/ppermute | solution.py:604
  (11 other events, 81.8 us)

commit v4 on v0

--- a/solution.py
+++ b/solution.py
@@ -1,6 +1,11 @@
+import functools
+import math
+
 import jax
 import jax.numpy as jnp
 from jax import lax
+from jax.experimental import pallas as pl
+from jax.experimental.pallas import tpu as pltpu
 from jax.sharding import PartitionSpec as P
 
 HD = 128
@@ -65,7 +70,7 @@
     return lax.map(one_block, stacked_blocks).reshape(query_count, queries.shape[1])
 
 
-def body(
+def general_body(
     video,
     text_cache,
     text_count,
@@ -194,6 +199,657 @@
     return (result[:video_rows][None], text_result[None])
 
 
+def vmem_spec():
+    return pl.BlockSpec(memory_space=pltpu.VMEM)
+
+
+def smem_spec():
+    return pl.BlockSpec(memory_space=pltpu.SMEM)
+
+
+def hbm_spec():
+    return pl.BlockSpec(memory_space=pltpu.HBM)
+
+
+def params(mib):
+    return pltpu.CompilerParams(vmem_limit_bytes=mib << 20)
+
+
+def cost(flops, moved, exps=0):
+    return pl.CostEstimate(flops=int(flops), bytes_accessed=int(moved), transcendentals=int(exps))
+
+
+def fetch(sources, targets, sems):
+    copies = [
+        pltpu.make_async_copy(source, target, sems.at[i])
+        for i, (source, target) in enumerate(zip(sources, targets))
+    ]
+    for copy in copies:
+        copy.start()
+    return copies
+
+
+def in_hbm(x):
+    return pltpu.with_memory_space_constraint(x, pltpu.HBM)
+
+
+def norm_kernel(rows_hbm, gain_hbm, out_ref, rows_ref, gain_ref, sems):
+    for copy in fetch((rows_hbm.at[0], gain_hbm), (rows_ref, gain_ref), sems):
+        copy.wait()
+    out_ref[...] = rms_scale(rows_ref[...].astype(jnp.float32), gain_ref[...]).astype(jnp.bfloat16)
+
+
+def norm_text(rows, gain):
+    _, count, depth = rows.shape
+    return pl.pallas_call(
+        norm_kernel,
+        out_shape=jax.ShapeDtypeStruct((count, depth), jnp.bfloat16),
+        in_specs=[hbm_spec(), hbm_spec()],
+        out_specs=vmem_spec(),
+        scratch_shapes=[
+            pltpu.VMEM((count, depth), jnp.bfloat16),
+            pltpu.VMEM((1, depth), jnp.float32),
+            pltpu.SemaphoreType.DMA((2,)),
+        ],
+        compiler_params=params(8),
+        cost_estimate=cost(4 * rows.size, 4 * rows.size),
+    )(in_hbm(rows), in_hbm(gain[None]))
+
+
+def table_row(ref, index):
+    return ref[pl.ds(index, 1)]
+
+
+def weight_copies(w_hbm, w_ref, sems, first):
+    return [
+        pltpu.make_async_copy(w_hbm.at[:, h], w_ref.at[:, h], sems.at[h])
+        for h in (first, first + 1)
+    ]
+
+
+def project_heads_into(out_hbm, out_ref, x_ref, w_hbm, w_ref, sems, qg_ref, kg_ref):
+    heads, rows = w_ref.shape[1], x_ref.shape[0]
+    sends = []
+    for first in range(0, heads, 2):
+        for copy in weight_copies(w_hbm, w_ref, sems, first):
+            copy.wait()
+        if first + 2 < heads:
+            for copy in weight_copies(w_hbm, w_ref, sems, first + 2):
+                copy.start()
+        pair = (first, first + 1)
+        weights = jnp.concatenate([w_ref[c, h] for h in pair for c in range(3)], axis=1)
+        raw = jnp.dot(x_ref[...], weights, preferred_element_type=jnp.float32)
+        for i, h in enumerate(pair):
+            lo = 3 * HD * i
+            queries = rms_scale(raw[:, lo : lo + HD], qg_ref[h : h + 1]).astype(jnp.bfloat16)
+            keys = rms_scale(raw[:, lo + HD : lo + 2 * HD], kg_ref[h : h + 1]).astype(jnp.bfloat16)
+            values = raw[:, lo + 2 * HD : lo + 3 * HD].astype(jnp.bfloat16)
+            for c, part in enumerate((queries, keys, values)):
+                out_ref[h, 0:rows, c * HD : (c + 1) * HD] = part
+            sends.append(pltpu.make_async_copy(out_ref.at[h], out_hbm.at[h], sems.at[heads + h]))
+            sends[-1].start()
+    for send in sends:
+        send.wait()
+
+
+def my_place(group):
+    mine = lax.axis_index("job")
+    core, half = mine & 1, lax.axis_index("seq") // group
+    return mine, core, half, (mine - core) | half
+
+
+def take_rows(x_ref, lo, here_ref, core_refs, stays):
+    rows = here_ref.shape[0]
+
+    @pl.when(stays)
+    def _():
+        x_ref[lo : lo + rows] = here_ref[...]
+
+    @pl.when(jnp.logical_not(stays))
+    def _():
+        size = rows // len(core_refs)
+        for i, ref in enumerate(core_refs):
+            x_ref[lo + i * size : lo + (i + 1) * size] = ref[...]
+
+
+def modulate_rows(x_ref, lo, hi, shift_ref, scale_ref, job):
+    x_ref[lo:hi] = modulate(x_ref[lo:hi], table_row(shift_ref, job), table_row(scale_ref, job))
+
+
+def qkv_kernel(pieces, has_text, *refs):
+    (a_ref, b_ref), refs = refs[:2], refs[2:]
+    a_core, refs = refs[: pieces[0]], refs[pieces[0] :]
+    b_core, refs = refs[: pieces[1]], refs[pieces[1] :]
+    if has_text:
+        (text_here_ref, text_core_ref), refs = refs[:2], refs[2:]
+    table_hbm, w_hbm, out_hbm, refs = refs[:4], refs[4], refs[5], refs[6:]
+    x_ref, w_ref, out_ref, table_refs, sems, refs = refs[0], refs[1], refs[2], refs[3:7], refs[7], refs[8:]
+    shift_ref, scale_ref, qg_ref, kg_ref = table_refs
+    rows, group = a_ref.shape[0], w_ref.shape[1]
+    tables = fetch(table_hbm, table_refs, sems.at[pl.ds(2 * group, 4)])
+    for copy in weight_copies(w_hbm, w_ref, sems, 0):
+        copy.start()
+    mine, core, half, job = my_place(group)
+    take_rows(x_ref, 0, a_ref, a_core, core == half)
+    take_rows(x_ref, rows, b_ref, b_core, core == half)
+    for copy in tables:
+        copy.wait()
+    modulate_rows(x_ref, 0, rows, shift_ref, scale_ref, job)
+    modulate_rows(x_ref, rows, 2 * rows, shift_ref, scale_ref, job ^ 2)
+    lo = 2 * rows
+    if has_text:
+        text_ref = refs[0]
+        blocks, trows, width = text_here_ref.shape
+        blocks = blocks // 2
+        for b in range(4):
+            for q in range(4):
+                part = text_core_ref if q & 1 else text_here_ref
+
+                @pl.when(mine ^ b == q)
+                def _():
+                    for t in range(blocks):
+                        job_of, shard_of, chip_of = t // 2, t % 2, q // 2
+                        text_ref[t * trows : (t + 1) * trows, b * width : (b + 1) * width] = part[
+                            4 * chip_of + 2 * shard_of + (job_of ^ chip_of)
+                        ]
+
+        x_ref[lo:] = text_ref[...]
+        modulate_rows(x_ref, lo, lo + 2 * trows, shift_ref, scale_ref, job)
+        modulate_rows(x_ref, lo + 2 * trows, lo + 4 * trows, shift_ref, scale_ref, job ^ 2)
+        for h in range(group):
+            cols = pl.ds(pl.multiple_of((2 * h + core) * 3 * HD, HD), 3 * HD)
+            out_ref[h, lo + 4 * trows :] = text_ref[0 : 2 * trows, cols]
+    project_heads_into(out_hbm, out_ref, x_ref, w_hbm, w_ref, sems, qg_ref, kg_ref)
+
+
+def qkv_half(here, from_core, text, tables, weights, q_gain, k_gain):
+    group, width = weights.shape[1:3]
+    pieces = tuple(map(len, from_core))
+    rows_in = rows_out = 2 * here[0].shape[0]
+    extra = []
+    if text:
+        blocks, trows, _ = text[0].shape
+        rows_in += blocks // 2 * trows
+        rows_out = rows_in + 2 * trows
+        extra = [pltpu.VMEM((blocks // 2 * trows, width), jnp.bfloat16)]
+    inputs = (*here, *from_core[0], *from_core[1], *text)
+    tables = (*tables, q_gain, k_gain)
+    return pl.pallas_call(
+        functools.partial(qkv_kernel, pieces, bool(text)),
+        out_shape=pltpu.HBM((group, rows_out, 3 * HD), jnp.bfloat16),
+        in_specs=[vmem_spec()] * len(inputs) + [hbm_spec()] * 5,
+        out_specs=hbm_spec(),
+        scratch_shapes=[
+            pltpu.VMEM((rows_in, width), jnp.bfloat16),
+            pltpu.VMEM(weights.shape, jnp.bfloat16),
+            pltpu.VMEM((group, rows_out, 3 * HD), jnp.bfloat16),
+            *[pltpu.VMEM(table.shape, jnp.float32) for table in tables],
+            pltpu.SemaphoreType.DMA((2 * group + 4,)),
+            *extra,
+        ],
+        compiler_params=params(24),
+        cost_estimate=cost(2 * rows_in * weights.size, 2 * weights.size + 4 * rows_in * width),
+    )(*inputs, *map(in_hbm, tables), in_hbm(weights))
+
+
+def refine_kernel(
+    group, holder_ref, n0_ref, n1_ref, n2_ref, n3_ref, w_hbm, bias_hbm, keep_ref, send_ref, x_ref,
+    w_ref, bias_ref, sems,
+):
+    mine, _, _, job = my_place(group)
+    chunks, depth, _ = w_ref.shape
+    copies = fetch(
+        [w_hbm.at[pl.ds(i * depth, depth)] for i in range(chunks)] + [bias_hbm],
+        [w_ref.at[i] for i in range(chunks)] + [bias_ref],
+        sems,
+    )
+    rows = n0_ref.shape[0]
+    for k, flip in enumerate((0, 2, 1, 3)):
+        for r, part in enumerate((n0_ref, n1_ref, n2_ref, n3_ref)):
+
+            @pl.when(holder_ref[job ^ flip] ^ mine == r)
+            def _():
+                x_ref[k * rows : (k + 1) * rows] = part[...]
+
+    copies[-1].wait()
+    lifted = bias_ref[...]
+    for i in range(chunks):
+        copies[i].wait()
+        part = x_ref[:, i * depth : (i + 1) * depth]
+        lifted = lifted + jnp.dot(part, w_ref[i], preferred_element_type=jnp.float32)
+    refined = lifted.astype(jnp.bfloat16)
+    for k in range(2):
+        keep_ref[k] = refined[k * rows : (k + 1) * rows]
+        send_ref[k] = refined[(2 + k) * rows : (3 + k) * rows]
+
+
+def refine_text(group, holder, normed, weights, bias):
+    rows, depth = normed[0].shape
+    width = weights.shape[1]
+    chunks = 4
+    out = jax.ShapeDtypeStruct((2, rows, width), jnp.bfloat16)
+    return pl.pallas_call(
+        functools.partial(refine_kernel, group),
+        out_shape=(out, out),
+        in_specs=[smem_spec()] + [vmem_spec()] * 4 + [hbm_spec()] * 2,
+        out_specs=(vmem_spec(), vmem_spec()),
+        scratch_shapes=[
+            pltpu.VMEM((4 * rows, depth), jnp.bfloat16),
+            pltpu.VMEM((chunks, depth // chunks, width), jnp.bfloat16),
+            pltpu.VMEM((1, width), jnp.float32),
+            pltpu.SemaphoreType.DMA((chunks + 1,)),
+        ],
+        compiler_params=params(14),
+        cost_estimate=cost(8 * rows * depth * width, 2 * depth * width),
+    )(holder, *normed, in_hbm(weights), in_hbm(bias[None]))
+
+
+def pack_kernel(*refs):
+    out_ref = refs[-1]
+    for i, ref in enumerate(refs[:-1]):
+        out_ref[i * ref.shape[0] : (i + 1) * ref.shape[0]] = ref[...]
+
+
+def pack(parts):
+    jobs, rows, width = parts[0].shape
+    return pl.pallas_call(
+        pack_kernel,
+        out_shape=jax.ShapeDtypeStruct((len(parts) * jobs, rows, width), jnp.bfloat16),
+        in_specs=[vmem_spec()] * len(parts),
+        out_specs=vmem_spec(),
+        compiler_params=params(4),
+        cost_estimate=cost(0, 4 * len(parts) * parts[0].size),
+    )(*parts)
+
+
+def choose_slots(count_ref, splits_ref, job, row, table, put):
+    shards = splits_ref.shape[1]
+    slot = lax.broadcasted_iota(jnp.int32, (2 * row.shape[1] // shards, row.shape[1]), 0)
+    offset = jnp.int32(0)
+    for s in range(shards):
+        chosen = (row == slot + offset) & (slot < splits_ref[job, s]) & (row < count_ref[job])
+        chosen = jnp.where(chosen, 1.0, 0.0).astype(jnp.bfloat16)
+        put(s, jnp.dot(chosen, table, preferred_element_type=jnp.float32).astype(jnp.bfloat16))
+        offset = offset + splits_ref[job, s]
+
+
+def attention_kernel(far, count_ref, splits_ref, first_hbm, second_hbm, *refs):
+    out_hbm, v_refs, t_refs, mixed_ref, out_ref, sems = refs[0], refs[1:4], refs[4:7], *refs[7:10]
+    col_ref = None if far else refs[10]
+    group, vrows, _ = v_refs[0].shape
+    trows = t_refs[0].shape[1]
+    one = vrows // 2
+    copies = []
+
+    def fetch(source, target):
+        copies.append(pltpu.make_async_copy(source, target, sems.at[len(copies)]))
+
+    for c in (1, 0, 2):
+        cols = pl.ds(c * HD, HD)
+        mine = pl.ds(one if far else 0, one)
+        fetch(first_hbm.at[:, mine, cols], v_refs[c].at[:, pl.ds(0, one)])
+        fetch(second_hbm.at[:, mine, cols], v_refs[c].at[:, pl.ds(one, one)])
+        text_rows = pl.ds(vrows + (trows if far else 0), trows)
+        fetch(second_hbm.at[:, text_rows, cols], t_refs[c])
+    if not far:
+        fetch(second_hbm.at[:, pl.ds(vrows + 2 * trows, trows)], col_ref)
+    for copy in copies:
+        copy.start()
+    for copy in copies:
+        copy.wait()
+    _, _, half, job = my_place(group)
+    job = job ^ 2 if far else job
+    block = trows // 2
+    place = lax.broadcasted_iota(jnp.int32, (1, group * trows), 1)
+    row = (place // trows) * block + place % block
+    row = row + (((place // block) & 1) ^ half) * (group * block)
+    key_ok = row < count_ref[job]
+    scale = HD ** (-0.5) * math.log2(math.e)
+    ones = jnp.ones((group * vrows, HD), jnp.bfloat16)
+    video_keys = v_refs[1][...].reshape(group * vrows, HD)
+    text_keys = t_refs[1][...].reshape(group * trows, HD)
+    video_values = jnp.concatenate([v_refs[2][...].reshape(group * vrows, HD), ones], axis=1)
+    text_values = jnp.concatenate(
+        [t_refs[2][...].reshape(group * trows, HD), ones[: group * trows]], axis=1
+    )
+
+    def product(a, b):
+        return lax.dot_general(a, b, (((1,), (1,)), ((), ())), preferred_element_type=jnp.float32)
+
+    def one_block(queries):
+        video_scores = product(queries, video_keys)
+        text_scores = jnp.where(key_ok, product(queries, text_keys), -1e30)
+        highest = jnp.maximum(
+            jnp.max(video_scores, axis=-1, keepdims=True),
+            jnp.max(text_scores, axis=-1, keepdims=True),
+        )
+        video_w = jnp.exp2((video_scores - highest) * scale)
+        text_w = jnp.exp2((text_scores - highest) * scale)
+        mixed = jnp.dot(
+            video_w.astype(jnp.bfloat16), video_values, preferred_element_type=jnp.float32
+        ) + jnp.dot(text_w.astype(jnp.bfloat16), text_values, preferred_element_type=jnp.float32)
+        return (mixed[:, :HD] / mixed[:, HD:]).astype(jnp.bfloat16)
+
+    mixed_ref[...] = one_block(t_refs[0][...].reshape(group * trows, HD))
+    rows = vrows // 2 + trows
+
+    def put(s, chosen):
+        out_ref[s, vrows // 2 : rows] = chosen
+
+    choose_slots(count_ref, splits_ref, job, row, mixed_ref[...], put)
+    if not far:
+
+        def put_columns(s, chosen):
+            for c in range(3):
+                lo = rows + trows * c
+                out_ref[s, lo : lo + trows] = chosen[:, c * HD : (c + 1) * HD]
+
+        columns = col_ref[...].reshape(group * trows, 3 * HD)
+        choose_slots(count_ref, splits_ref, job, row, columns, put_columns)
+    sends = []
+    for i in range(group):
+        done = one_block(v_refs[0][i])
+        for part in range(2):
+            shard = (half ^ part) * group + i
+            out_ref[shard, 0 : vrows // 2] = done[part * (vrows // 2) : (part + 1) * (vrows // 2)]
+            sends.append(
+                pltpu.make_async_copy(
+                    out_ref.at[shard], out_hbm.at[shard], sems.at[10 + 2 * i + part]
+                )
+            )
+            sends[-1].start()
+    for send in sends:
+        send.wait()
+
+
+def attend_pair(far, count, splits, first, second, vrows, trows):
+    group, shards = first.shape[0], splits.shape[1]
+    total = group * (vrows + trows)
+    rows_out = vrows // 2 + trows * (1 if far else 4)
+    scratch = [pltpu.VMEM((group, vrows, HD), jnp.bfloat16)] * 3
+    scratch += [pltpu.VMEM((group, trows, HD), jnp.bfloat16)] * 3
+    scratch += [pltpu.VMEM((group * trows, HD), jnp.bfloat16)]
+    scratch += [pltpu.VMEM((shards, rows_out, HD), jnp.bfloat16)]
+    scratch += [pltpu.SemaphoreType.DMA((10 + shards,))]
+    if not far:
+        scratch += [pltpu.VMEM((group, trows, 3 * HD), jnp.bfloat16)]
+    return pl.pallas_call(
+        functools.partial(attention_kernel, far),
+        out_shape=pltpu.HBM((shards, rows_out, HD), jnp.bfloat16),
+        in_specs=[smem_spec(), smem_spec(), hbm_spec(), hbm_spec()],
+        out_specs=hbm_spec(),
+        scratch_shapes=scratch,
+        compiler_params=params(12),
+        cost_estimate=cost(4 * total * total * HD, 3 << 20, total * total),
+    )(count, splits, first, second)
+
+
+def project_rows(heads_ref, w_ref, job, count, put):
+    group, width = w_ref.shape[0] // HD, w_ref.shape[1]
+    rows = jnp.concatenate([heads_ref[job * group + h, 0:count] for h in range(group)], axis=1)
+    for lo in range(0, width, width // 4):
+        cols = slice(lo, lo + width // 4)
+        put(cols, jnp.dot(rows, w_ref[:, cols], preferred_element_type=jnp.float32))
+
+
+def give_kernel(pieces, heads_ref, w_ref, *refs):
+    core = lax.axis_index("job") & 1
+    size = refs[0].shape[0]
+
+    def put(cols, total):
+        for i, ref in enumerate(refs[:pieces]):
+            ref[:, cols] = total[i * size : (i + 1) * size].astype(jnp.bfloat16)
+
+    project_rows(heads_ref, w_ref, 1 - core, size * pieces, put)
+    if len(refs) > pieces:
+        slot_ref = refs[pieces]
+        slots = slot_ref.shape[0]
+        for h in range(w_ref.shape[0] // HD):
+            for c in range(3):
+                lo = size * pieces + slots * c
+                slot_ref[:, (3 * h + c) * HD : (3 * h + c + 1) * HD] = heads_ref[
+                    (1 - core) * (w_ref.shape[0] // HD) + h, lo : lo + slots
+                ]
+
+
+def keep_kernel(pieces, given, heads_ref, w_ref, *refs):
+    core = lax.axis_index("job") & 1
+    out_ref = refs[given]
+    size = refs[0].shape[0]
+
+    def put(cols, total):
+        for i in range(pieces):
+            part = total[i * size : (i + 1) * size] + refs[i][:, cols].astype(jnp.float32)
+            out_ref[i * size : (i + 1) * size, cols] = part.astype(jnp.bfloat16)
+
+    project_rows(heads_ref, w_ref, core, size * pieces, put)
+    if given > pieces:
+        slot_ref, other_ref = refs[given + 1], refs[pieces]
+        slots, group = slot_ref.shape[0], w_ref.shape[0] // HD
+        for h in range(group):
+            for c in range(3):
+                lo = size * pieces + slots * c
+                cols = pl.ds(pl.multiple_of((3 * (2 * h + core) + c) * HD, HD), HD)
+                slot_ref[:, cols] = heads_ref[core * group + h, lo : lo + slots]
+                cols = pl.ds(pl.multiple_of((3 * (2 * h + 1 - core) + c) * HD, HD), HD)
+                slot_ref[:, cols] = other_ref[:, (3 * h + c) * HD : (3 * h + c + 1) * HD]
+
+
+def out_call(kernel, rows, weights, inputs, outs):
+    depth, width = weights.shape
+    return pl.pallas_call(
+        kernel,
+        out_shape=tuple(jax.ShapeDtypeStruct(shape, jnp.bfloat16) for shape in outs),
+        in_specs=[vmem_spec()] * len(inputs),
+        out_specs=(vmem_spec(),) * len(outs),
+        compiler_params=params(8),
+        cost_estimate=cost(2 * rows * depth * width, 2 * (depth + 2 * rows) * width),
+    )(*inputs)
+
+
+def project_out(heads, rows, pieces, slots, weights, to_core):
+    width = weights.shape[1]
+    outs = [(rows // pieces, width)] * pieces + ([(slots, width // 2)] if slots else [])
+    kernel = functools.partial(give_kernel, pieces)
+    given = [to_core(x) for x in out_call(kernel, rows, weights, (heads, weights), outs)]
+    kernel = functools.partial(keep_kernel, pieces, len(given))
+    outs = [(rows, width)] + ([(slots, width)] if slots else [])
+    return out_call(kernel, rows, weights, (heads, weights, *given), outs)
+
+
+def final_kernel(
+    count_ref, splits_ref, video_hbm, part_ref, chip_hbm, gate_hbm, slot_ref, vout_hbm, tout_hbm,
+    chip_ref, out_ref, video_ref, gate_ref, in_sems, out_sems,
+):
+    vrows, step = video_ref.shape[0], slot_ref.shape[0]
+    total_rows = part_ref.shape[0]
+    reads, writes = [], []
+    for i, lo in enumerate(range(0, total_rows, step)):
+        rows = pl.ds(lo, step)
+        reads.append(pltpu.make_async_copy(chip_hbm.at[rows], chip_ref.at[rows], in_sems.at[i]))
+        target = vout_hbm.at[0, rows] if lo < vrows else tout_hbm.at[0]
+        writes.append(pltpu.make_async_copy(out_ref.at[rows], target, out_sems.at[i]))
+    for read in reads:
+        read.start()
+    steps = len(reads)
+    for copy in fetch((video_hbm.at[0], gate_hbm), (video_ref, gate_ref), in_sems.at[pl.ds(steps, 2)]):
+        copy.wait()
+    job, shard = lax.axis_index("job"), lax.axis_index("seq")
+    gate = table_row(gate_ref, job)
+    offset = jnp.int32(0)
+    for s in range(splits_ref.shape[1]):
+        offset = offset + jnp.where(s < shard, splits_ref[job, s], 0)
+    slot = lax.broadcasted_iota(jnp.int32, (step, 1), 0)
+    valid = (slot < splits_ref[job, shard]) & (slot + offset < count_ref[job])
+    for i, lo in enumerate(range(0, total_rows, step)):
+        reads[i].wait()
+        rows = slice(lo, lo + step)
+        total = part_ref[rows].astype(jnp.float32) + chip_ref[rows].astype(jnp.float32)
+        base = video_ref[rows] if lo < vrows else slot_ref[...]
+        result = base.astype(jnp.float32) + gate * total
+        if lo >= vrows:
+            result = jnp.where(valid, result, 0.0)
+        out_ref[rows] = result.astype(jnp.bfloat16)
+        writes[i].start()
+    for write in writes:
+        write.wait()
+
+
+def finish(count, splits, video, part, from_chip, gate, slot_rows):
+    rows, width = part.shape
+    steps = rows // slot_rows.shape[0]
+    vrows = video.shape[1]
+    return pl.pallas_call(
+        final_kernel,
+        out_shape=(
+            jax.ShapeDtypeStruct((1, vrows, width), jnp.bfloat16),
+            jax.ShapeDtypeStruct((1, rows - vrows, width), jnp.bfloat16),
+        ),
+        in_specs=[
+            smem_spec(), smem_spec(), hbm_spec(), vmem_spec(), hbm_spec(), hbm_spec(), vmem_spec(),
+        ],
+        out_specs=(hbm_spec(), hbm_spec()),
+        scratch_shapes=[
+            pltpu.VMEM((rows, width), jnp.bfloat16),
+            pltpu.VMEM((rows, width), jnp.bfloat16),
+            pltpu.VMEM((vrows, width), jnp.bfloat16),
+            pltpu.VMEM(gate.shape, jnp.float32),
+            pltpu.SemaphoreType.DMA((steps + 2,)),
+            pltpu.SemaphoreType.DMA((steps,)),
+        ],
+        compiler_params=params(8),
+        cost_estimate=cost(6 * rows * width, 10 * rows * width),
+    )(count, splits, in_hbm(video), part, from_chip, in_hbm(gate), slot_rows)
+
+
+def two_wave_body(
+    video,
+    text_cache,
+    text_count,
+    holder,
+    text_splits,
+    mod_shift,
+    mod_scale,
+    mod_gate,
+    text_gain,
+    refine_w,
+    refine_bias,
+    w_qkv,
+    q_gain,
+    k_gain,
+    w_out,
+):
+    job_count = lax.axis_size("job")
+    shard_count = lax.axis_size("seq")
+    group_size = w_qkv.shape[1]
+    trows = text_cache.shape[1]
+    vrows = video.shape[1]
+
+    def to_core(x):
+        return lax.ppermute(x, "job", [(i, i ^ 1) for i in range(job_count)])
+
+    def to_chip(x):
+        return lax.ppermute(x, "job", [(i, i ^ 2) for i in range(job_count)])
+
+    def over_seq(x):
+        return lax.all_to_all(x, "seq", split_axis=0, concat_axis=0, tiled=False)
+
+    def after(x, earlier):
+        return lax.optimization_barrier((x, earlier))[0]
+
+    def to_device(x, chip, other_half, staying=None):
+        perm = []
+        for job in range(job_count):
+            for shard in range(shard_count):
+                if staying is None or (job % 2 == shard // group_size) == staying:
+                    to = (job ^ chip, shard ^ (group_size if other_half else 0))
+                    perm.append((job * shard_count + shard, to[0] * shard_count + to[1]))
+        return lax.ppermute(x, ("job", "seq"), perm)
+
+    def over_half(x):
+        halves = [list(range(i, i + group_size)) for i in range(0, shard_count, group_size)]
+        return lax.all_to_all(
+            x, "seq", split_axis=0, concat_axis=0, tiled=False, axis_index_groups=halves
+        )
+
+    def core_pieces(x, count):
+        return [to_core(part) for part in jnp.split(x, count)]
+
+    tables = (mod_shift, mod_scale)
+    qkv_w = jnp.transpose(w_qkv, (2, 1, 0, 3))
+    own = video[0]
+    normed = norm_text(text_cache, text_gain)
+    other = to_device(after(own, normed), 0, True, staying=False)
+    normed_chip = after(to_chip(normed), qkv_w)
+    own_chip = to_device(after(own, normed_chip), 2, False, staying=True)
+    normed_core = to_core(after(normed, qkv_w))
+
+    normed_both = to_core(normed_chip)
+    keep, send = refine_text(
+        group_size, holder, (normed, normed_core, normed_chip, normed_both), refine_w, refine_bias
+    )
+    text = (
+        keep,
+        to_device(send, 0, True),
+        to_device(keep, 2, False),
+        to_device(send, 2, True),
+    )
+
+    other = after(other, keep)
+    other_chip = to_device(other, 2, False, staying=True)
+    own_chip = after(own_chip, keep)
+    first_send = qkv_half(
+        (own, own_chip), (core_pieces(own, 1), core_pieces(own_chip, 4)), (), tables, qkv_w, q_gain, k_gain
+    )
+    text = pack(after(text, first_send))
+    first = over_half(after(first_send, text))
+
+    other_chip = after(other_chip, first_send)
+    second_send = qkv_half(
+        (other, other_chip),
+        (core_pieces(other, 1), core_pieces(other_chip, 2)),
+        (text, to_core(text)),
+        tables,
+        qkv_w,
+        q_gain,
+        k_gain,
+    )
+    second = over_half(after(second_send, first))
+    second = in_hbm(second)
+
+    shapes = (2 * vrows, 2 * trows)
+    remote_mixed = attend_pair(True, text_count, text_splits, first, second, *shapes)
+    remote_back = over_seq(remote_mixed)
+    local_mixed = attend_pair(
+        False, text_count, text_splits, after(first, remote_mixed), second, *shapes
+    )
+    out_weight = w_out.reshape(group_size * HD, w_out.shape[2])
+    rows, slots = vrows + 2 * trows, 2 * trows
+    remote_back = after(remote_back, local_mixed)
+    local_back = over_seq(after(local_mixed, remote_back))
+    (crossing,) = project_out(remote_back, rows, 1, 0, out_weight, to_core)
+    from_chip = to_chip(crossing)
+    local_part, slot_rows = project_out(
+        after(local_back, crossing), rows, 3, slots, out_weight, to_core
+    )
+    return finish(
+        text_count, text_splits, video, local_part, from_chip, mod_gate, slot_rows
+    )
+
+
+def body(*arrays):
+    video, text_cache, w_qkv = arrays[0], arrays[1], arrays[11]
+    job_count = lax.axis_size("job")
+    shard_count = lax.axis_size("seq")
+    fits = (
+        job_count == 4
+        and shard_count == 2 * w_qkv.shape[1]
+        and video.shape[1] == 128
+        and text_cache.shape[1] == 32
+    )
+    return (two_wave_body if fits else general_body)(*arrays)
+
+
 def solution(mesh):
     placed = (
         P("job", "seq", None),

time: 340 us -> 149 us (0.44)
  waiting for transfers between devices: 148 us -> 38.2 us
  blocking collectives: 73.1 us -> 22.9 us
  Pallas kernels: 0 us -> 46.5 us
  matrix products: 38.3 us -> 0 us
  local copies, waits for them, and re-layouts: 36.9 us -> 9.66 us
  starting transfers between devices: 4.41 us -> 29.6 us
  other arithmetic: 24.3 us -> 0 us
  between operations: 14.2 us -> 1.07 us
    all_gather x4 -> x0, waiting for transfers between devices: 90 us -> none  [the longest x1 41.7 us: body(): gathered_text = lax.all_gather(refined, 'seq', axis=1, tiled=True)]
    all_to_all x3 -> x1, blocking collectives: 73.1 us -> 22.9 us  [over_half(): lax.all_to_all(x, 'seq', split_axis=0, concat_axis=0, tiled=False, axis_i...]
    pallas_call x0 -> x12, Pallas kernels: none -> 46.5 us  [the longest x2 16.6 us: qkv_half(): pl.pallas_call(functools.partial(qkv_kernel, pieces, bool(text)), out_sha...]
    reduce_scatter x1 -> x0, waiting for transfers between devices: 43.6 us -> none  [body(): lax.psum_scatter(jnp.dot(per_job, out_weight, preferred_element_type=jnp....]
    dot_general x12 -> x0, matrix products: 38.3 us -> none  [the longest x2 15.8 us: project_heads(): jnp.einsum('jrd,dhce->jrhce', modded, w_qkv, preferred_element_type=jnp.f...]
    ppermute x0 -> x24, starting transfers between devices: none -> 17.2 us  [the longest x6 9.43 us: to_device(): return lax.ppermute(x, ('job', 'seq'), perm)]
    ppermute x0 -> x24, waiting for transfers between devices: none -> 14.9 us  [the longest x6 6.1 us: to_device(): return lax.ppermute(x, ('job', 'seq'), perm)]
    reduce_sum x11 -> x0, other arithmetic: 13.8 us -> none  [the longest x2 4.23 us: modulate(): centre = jnp.mean(widened, axis=-1, keepdims=True)]
  transfers between devices with their start and end apart: 6 -> 27, of which waited for: 6 -> 13; matrix products, arithmetic and copies ran while one was open for 10% -> 7% of each run, Pallas kernels for 0% -> 23%
where the time goes in v4:
time: 149 us; the launch traced here: 148 us
  Pallas kernels  46.5 us (31%)
  waiting for transfers between devices  38.2 us (26%)
  starting transfers between devices  29.6 us (20%)
  blocking collectives  22.9 us (15%)
  local copies, waits for them, and re-layouts  9.66 us (6%)
    all_to_all x2, waiting for transfers between devices, over_seq(): return lax.all_to_all(x, 'seq', split_axis=0, concat_axis=0, tiled=False)  23.1 us
    all_to_all x1, blocking collectives, over_half(): lax.all_to_all(x, 'seq', split_axis=0, concat_axis=0, tiled=False, axis_i...  22.9 us
    pallas_call x2, Pallas kernels, qkv_half(): pl.pallas_call(functools.partial(qkv_kernel, pieces, bool(text)), out_sha...  16.6 us
    pallas_call x2, Pallas kernels, attend_pair(): pl.pallas_call(functools.partial(attention_kernel, far), out_shape=pltpu....  11.6 us
    ppermute x6, starting transfers between devices, to_device(): return lax.ppermute(x, ('job', 'seq'), perm)  9.43 us
    unnamed x13, local copies, waits for them, and re-layouts  8.97 us
    pallas_call x4, Pallas kernels, out_call(): pl.pallas_call(kernel, out_shape=tuple((jax.ShapeDtypeStruct(shape, jnp.b...  8.87 us
    all_to_all x2, starting transfers between devices, over_seq(): return lax.all_to_all(x, 'seq', split_axis=0, concat_axis=0, tiled=False)  8.17 us
  transfers between devices with their start and end apart: 27, of which 13 were waited for; matrix products, arithmetic and copies ran while one was open for 7% of the time, Pallas kernels for 23%

profile of v4, /device:TPU:0, one launch (start us, length us, event | category | flops | bytes accessed | tf_op | source)
XLA Modules:
  0.0 147.9 jit_solution(9739992960798640257)
XLA Ops:
  1.8 3.0 %collective-permute-start = (bf16[32,4096]{1,0:T(8,128)(2,1)S(1)}, bf16[32,4096]{1,0:T(8,128)(2,1)S(1)}, u32[]{:S(2)}, u32[]{:S(2)}) collective-permute-start(bf16[32,4096]{1,0:T(8,128)(2,1)S(1)} %shard_map.158.n0_ref), channel_id=1, source_target_pairs={{0,16},{8,24},{16,0},{24,8},{1,17},{9,25},{17,1},{25,9},{2,18},{10... | collective-permute-start | bytes 786440 | tf_op jit(solution)/shard_map/ppermute | solution.py:752
  6.2 8.9 %copy.19 = bf16[3072,4,3,128]{3,0,1,2:T(8,128)(2,1)} copy(bf16[3072,4,3,128]{3,1,2,0:T(4,128)(2,1)} %param.26) | data formatting | bytes 18874368 | tf_op args[11]
  15.2 2.0 %collective-permute-start.1 = (bf16[128,3072]{1,0:T(8,128)(2,1)S(1)}, bf16[128,3072]{1,0:T(8,128)(2,1)S(1)}, u32[]{:S(2)}, u32[]{:S(2)}) collective-permute-start(bf16[128,3072]{1,0:T(8,128)(2,1)S(1)} %bitcast.11), channel_id=1, source_target_pairs={{0,16},{1,17},{2,18},{3,19},{12,28},{13,29},{14,30},{15,31},{16,0}... | collective-permute-start | bytes 2359304 | tf_op jit(solution)/shard_map/ppermute | solution.py:767
  20.0 4.8 %shard_map.159 = (bf16[2,32,768]{2,1,0:T(8,128)(2,1)S(1)}, bf16[2,32,768]{2,1,0:T(8,128)(2,1)S(1)}) custom-call(s32[4]{0:T(128)S(1)} %copy-done.3, bf16[32,4096]{1,0:T(8,128)(2,1)S(1)} %shard_map.158.n0_ref, bf16[32,4096]{1,0:T(8,128)(2,1)S(1)} %collective-permute-done.2.n1_ref, bf16[32,4096]{1,0:T(8,128)(2,1)S(1)} %collective-permute-done.n2_ref, ...), custom_call_target="tpu_custom_call" | custom-call | flops 805306368 | bytes 6291456 | tf_op jit(solution)/shard_map/pallas_call | solution.py:431
  24.8 3.6 %collective-permute-done.12.refs_0_ = bf16[128,3072]{1,0:T(8,128)(2,1)S(1)} collective-permute-done((bf16[128,3072]{1,0:T(8,128)(2,1)}, bf16[128,3072]{1,0:T(8,128)(2,1)S(1)}, u32[]{:S(2)}, u32[]{:S(2)}) %collective-permute-start.12) | collective-permute-done | bytes 786464 | tf_op jit(solution)/shard_map/ppermute | solution.py:767
  28.4 2.0 %collective-permute-start.13 = (bf16[128,3072]{1,0:T(8,128)(2,1)S(1)}, bf16[128,3072]{1,0:T(8,128)(2,1)S(1)}, u32[]{:S(2)}, u32[]{:S(2)}) collective-permute-start(bf16[128,3072]{1,0:T(8,128)(2,1)S(1)} %collective-permute-done.12.refs_0_), channel_id=1, source_target_pairs={{0,16},{1,17},{2,18},{3,19},{12,28},{13,29},{14,30},{15,31},{16,0}... | collective-permute-start | bytes 2359304 | tf_op jit(solution)/shard_map/ppermute | solution.py:767
  32.2 4.1 %collective-permute-start.9 = (bf16[2,32,768]{2,1,0:T(8,128)(2,1)S(1)}, bf16[2,32,768]{2,1,0:T(8,128)(2,1)S(1)}, u32[]{:S(2)}, u32[]{:S(2)}) collective-permute-start(bf16[2,32,768]{2,1,0:T(8,128)(2,1)S(1)} %get-tuple-element.32), channel_id=1, source_target_pairs={{0,4},{1,5},{2,6},{3,7},{4,0},{5,1},{6,2},{7,3},{8,12},{9,13},{10,... | collective-permute-start | bytes 294920 | tf_op jit(solution)/shard_map/ppermute | solution.py:767
  36.3 7.6 %shard_map.160 = bf16[4,256,384]{2,1,0:T(8,128)(2,1)} custom-call(bf16[128,3072]{1,0:T(8,128)(2,1)S(1)} %bitcast.13, bf16[128,3072]{1,0:T(8,128)(2,1)S(1)} %collective-permute-done.1.refs_1_, bf16[128,3072]{1,0:T(8,128)(2,1)S(1)} %collective-permute-done.4.refs_2_, bf16[32,3072]{1,0:T(8,128)(2,1)S(1)} %collective-permute-done.5.refs_3_, ...), custom_call_target="tpu_custom_call" | custom-call | flops 2415919104 | bytes 12582912 | tf_op jit(solution)/shard_map/pallas_call | solution.py:377
  43.9 2.5 %collective-permute-done.10.refs_2_ = bf16[2,32,768]{2,1,0:T(8,128)(2,1)S(1)} collective-permute-done((bf16[2,32,768]{2,1,0:T(8,128)(2,1)S(1)}, bf16[2,32,768]{2,1,0:T(8,128)(2,1)S(1)}, u32[]{:S(2)}, u32[]{:S(2)}) %collective-permute-start.10) | collective-permute-done | bytes 98336 | tf_op jit(solution)/shard_map/ppermute | solution.py:767
  46.6 4.2 %all-to-all-start = ((bf16[4,256,384]{2,1,0:T(8,128)(2,1)}), bf16[4,256,384]{2,1,0:T(8,128)(2,1)}, u32[]{:S(2)}, u32[]{:S(2)}) async-start(bf16[4,256,384]{2,1,0:T(8,128)(2,1)} %shard_map.160), calls=%async_computation | async-start | bytes 1572864 | tf_op jit(solution)/shard_map/all_to_all | solution.py:771
  53.3 9.1 %shard_map.162 = bf16[4,448,384]{2,1,0:T(8,128)(2,1)} custom-call(bf16[128,3072]{1,0:T(8,128)(2,1)S(1)} %collective-permute-done.12.refs_0_, bf16[128,3072]{1,0:T(8,128)(2,1)S(1)} %collective-permute-done.13.refs_1_, bf16[128,3072]{1,0:T(8,128)(2,1)S(1)} %collective-permute-done.14.refs_2_, bf16[64,3072]{1,0:T(8,128)(2,1)S(1)} %collective-permute-done.15.refs_3_, ...), custom_call_target="tpu_custom_call" | custom-call | flops 3623878656 | bytes 14155776 | tf_op jit(solution)/shard_map/pallas_call | solution.py:377
  62.6 22.9 %all_to_all.20.second_hbm = bf16[4,448,384]{2,1,0:T(8,128)(2,1)} all-to-all(bf16[4,448,384]{2,1,0:T(8,128)(2,1)} %shard_map.162), channel_id=1, replica_groups={{0,1,2,3},{4,5,6,7},{8,9,10,11},{12,13,14,15},{16,17,18,19},{20,21,22,2..., dimensions={0} | all-to-all | bytes 2752512 | tf_op jit(solution)/shard_map/all_to_all | solution.py:771
  85.4 5.7 %shard_map.163 = bf16[8,192,128]{2,1,0:T(8,128)(2,1)} custom-call(s32[4]{0:T(128)S(1)} %copy-done.4, s32[4,8]{1,0:T(4,128)S(1)} %copy-done.2, bf16[4,256,384]{2,1,0:T(8,128)(2,1)} %all-to-all-done.first_hbm, bf16[4,448,384]{2,1,0:T(8,128)(2,1)} %all_to_all.20.second_hbm), custom_call_target="tpu_custom_call" | custom-call | flops 838860800 | bytes 3145728 | tf_op jit(solution)/shard_map/pallas_call | solution.py:576
  91.1 3.7 %all-to-all-start.2 = ((bf16[8,192,128]{2,1,0:T(8,128)(2,1)}), bf16[8,192,128]{2,1,0:T(8,128)(2,1)S(1)}, u32[]{:S(2)}, u32[]{:S(2)}) async-start(bf16[8,192,128]{2,1,0:T(8,128)(2,1)} %shard_map.163), calls=%async_computation.2 | async-start | bytes 786432 | tf_op jit(solution)/shard_map/all_to_all | solution.py:755
  94.9 6.0 %shard_map.164 = bf16[8,384,128]{2,1,0:T(8,128)(2,1)} custom-call(s32[4]{0:T(128)S(1)} %copy-done.4, s32[4,8]{1,0:T(4,128)S(1)} %copy-done.2, bf16[4,256,384]{2,1,0:T(8,128)(2,1)} %all-to-all-done.first_hbm, bf16[4,448,384]{2,1,0:T(8,128)(2,1)} %all_to_all.20.second_hbm), custom_call_target="tpu_custom_call" | custom-call | flops 838860800 | bytes 3145728 | tf_op jit(solution)/shard_map/pallas_call | solution.py:576
  100.8 5.3 %all-to-all-done.2.heads_ref = bf16[8,192,128]{2,1,0:T(8,128)(2,1)S(1)} async-done(((bf16[8,192,128]{2,1,0:T(8,128)(2,1)}), bf16[8,192,128]{2,1,0:T(8,128)(2,1)S(1)}, u32[]{:S(2)}, u32[]{:S(2)}) %all-to-all-start.2) | async-done | bytes 393248 | tf_op jit(solution)/shard_map/all_to_all | solution.py:755
  108.0 4.4 %all-to-all-start.3 = ((bf16[8,384,128]{2,1,0:T(8,128)(2,1)}), bf16[8,384,128]{2,1,0:T(8,128)(2,1)}, u32[]{:S(2)}, u32[]{:S(2)}) async-start(bf16[8,384,128]{2,1,0:T(8,128)(2,1)} %shard_map.164), calls=%async_computation.3 | async-start | bytes 1572864 | tf_op jit(solution)/shard_map/all_to_all | solution.py:755
  112.5 3.1 %shard_map.166 = bf16[192,3072]{1,0:T(8,128)(2,1)} custom-call(bf16[8,192,128]{2,1,0:T(8,128)(2,1)S(1)} %all-to-all-done.2.heads_ref, bf16[512,3072]{1,0:T(8,128)(2,1)S(1)} %bitcast.7, bf16[192,3072]{1,0:T(8,128)(2,1)} %collective-permute-done.18.refs_0_), custom_call_target="tpu_custom_call" | custom-call | flops 603979776 | bytes 5505024 | tf_op jit(solution)/shard_map/pallas_call | solution.py:640
  115.6 17.8 %all-to-all-done.3.heads_ref = bf16[8,384,128]{2,1,0:T(8,128)(2,1)} async-done(((bf16[8,384,128]{2,1,0:T(8,128)(2,1)}), bf16[8,384,128]{2,1,0:T(8,128)(2,1)}, u32[]{:S(2)}, u32[]{:S(2)}) %all-to-all-start.3) | async-done | bytes 786464 | tf_op jit(solution)/shard_map/all_to_all | solution.py:755
  133.3 2.0 %shard_map.167 = (bf16[64,3072]{1,0:T(8,128)(2,1)S(1)}, bf16[64,3072]{1,0:T(8,128)(2,1)S(1)}, bf16[64,3072]{1,0:T(8,128)(2,1)S(1)}, bf16[64,1536]{1,0:T(8,128)(2,1)S(1)}) custom-call(bf16[8,384,128]{2,1,0:T(8,128)(2,1)} %all-to-all-done.3.heads_ref, bf16[512,3072]{1,0:T(8,128)(2,1)S(1)} %bitcast.8), custom_call_target="tpu_custom_call" | custom-call | flops 603979776 | bytes 5505024 | tf_op jit(solution)/shard_map/pallas_call | solution.py:640
  136.4 2.1 %collective-permute-done.22.refs_3_ = bf16[64,1536]{1,0:T(8,128)(2,1)S(1)} collective-permute-done((bf16[64,1536]{1,0:T(8,128)(2,1)S(1)}, bf16[64,1536]{1,0:T(8,128)(2,1)S(1)}, u32[]{:S(2)}, u32[]{:S(2)}) %collective-permute-start.22) | collective-permute-done | bytes 196640 | tf_op jit(solution)/shard_map/ppermute | solution.py:749
  138.5 2.0 %shard_map.168 = (bf16[192,3072]{1,0:T(8,128)(2,1)S(1)}, bf16[64,3072]{1,0:T(8,128)(2,1)S(1)}) custom-call(bf16[8,384,128]{2,1,0:T(8,128)(2,1)} %all-to-all-done.3.heads_ref, bf16[512,3072]{1,0:T(8,128)(2,1)S(1)} %bitcast.9, bf16[64,3072]{1,0:T(8,128)(2,1)S(1)} %collective-permute-done.19.refs_0_, bf16[64,3072]{1,0:T(8,128)(2,1)S(1)} %collective-permute-done.20.refs_1_, ...), custom_call_target="tpu_custom_call" | custom-call | flops 603979776 | bytes 5505024 | tf_op jit(solution)/shard_map/pallas_call | solution.py:640
  140.5 3.7 %collective-permute-done.23.chip_hbm = bf16[192,3072]{1,0:T(8,128)(2,1)} collective-permute-done((bf16[192,3072]{1,0:T(8,128)(2,1)}, bf16[192,3072]{1,0:T(8,128)(2,1)}, u32[]{:S(2)}, u32[]{:S(2)}) %collective-permute-start.23) | collective-permute-done | bytes 1179680 | tf_op jit(solution)/shard_map/ppermute | solution.py:752
  144.2 3.4 %shard_map.169 = (bf16[1,128,3072]{2,1,0:T(8,128)(2,1)}, bf16[1,64,3072]{2,1,0:T(8,128)(2,1)}) custom-call(s32[4]{0:T(128)S(1)} %copy-done.4, s32[4,8]{1,0:T(4,128)S(1)} %copy-done.2, bf16[1,128,3072]{2,1,0:T(8,128)(2,1)} %video_hbm.1, bf16[192,3072]{1,0:T(8,128)(2,1)S(1)} %get-tuple-element.50.part_ref, bf16[192,3072]{1,0:T(8,128)(2,1)} %collective-permute-done.23.chip_hbm, ...), custom_call_target="tpu_custom_call" | custom-call | flops 3538944 | bytes 5898240 | tf_op jit(solution)/shard_map/pallas_call | solution.py:702
  (59 shorter events, 13.1 us)
Async XLA Ops:
  1.8 13.4 %collective-permute-start = (bf16[32,4096]{1,0:T(8,128)(2,1)S(1)}, bf16[32,4096]{1,0:T(8,128)(2,1)S(1)}, u32[]{:S(2)}, u32[]{:S(2)}) collective-permute-start(bf16[32,4096]{1,0:T(8,128)(2,1)S(1)} %shard_map.158.n0_ref), channel_id=1, source_target_pairs={{0,16},{8,24},{16,0},{24,8},{1,17},{9,25},{17,1},{25,9},{2,18},{10... | collective-permute-start | bytes 786440 | tf_op jit(solution)/shard_map/ppermute | solution.py:752
  4.8 23.5 %collective-permute-start.12 = (bf16[128,3072]{1,0:T(8,128)(2,1)}, bf16[128,3072]{1,0:T(8,128)(2,1)S(1)}, u32[]{:S(2)}, u32[]{:S(2)}) collective-permute-start(bf16[128,3072]{1,0:T(8,128)(2,1)} %bitcast.10), channel_id=1, source_target_pairs={{4,0},{5,1},{6,2},{7,3},{8,12},{9,13},{10,14},{11,15},{20,16},{21,... | collective-permute-start | bytes 2359304 | tf_op jit(solution)/shard_map/ppermute | solution.py:767
  15.2 15.1 %collective-permute-start.1 = (bf16[128,3072]{1,0:T(8,128)(2,1)S(1)}, bf16[128,3072]{1,0:T(8,128)(2,1)S(1)}, u32[]{:S(2)}, u32[]{:S(2)}) collective-permute-start(bf16[128,3072]{1,0:T(8,128)(2,1)S(1)} %bitcast.11), channel_id=1, source_target_pairs={{0,16},{1,17},{2,18},{3,19},{12,28},{13,29},{14,30},{15,31},{16,0}... | collective-permute-start | bytes 2359304 | tf_op jit(solution)/shard_map/ppermute | solution.py:767
  17.1 2.5 %collective-permute-start.2 = (bf16[32,4096]{1,0:T(8,128)(2,1)S(1)}, bf16[32,4096]{1,0:T(8,128)(2,1)S(1)}, u32[]{:S(2)}, u32[]{:S(2)}) collective-permute-start(bf16[32,4096]{1,0:T(8,128)(2,1)S(1)} %shard_map.158.n0_ref), channel_id=1, source_target_pairs={{0,8},{8,0},{16,24},{24,16},{1,9},{9,1},{17,25},{25,17},{2,10},{10... | collective-permute-start | bytes 786440 | tf_op jit(solution)/shard_map/ppermute | solution.py:749
  18.6 12.5 %collective-permute-start.4 = (bf16[128,3072]{1,0:T(8,128)(2,1)S(1)}, bf16[128,3072]{1,0:T(8,128)(2,1)S(1)}, u32[]{:S(2)}, u32[]{:S(2)}) collective-permute-start(bf16[128,3072]{1,0:T(8,128)(2,1)S(1)} %bitcast.12), channel_id=1, source_target_pairs={{0,8},{8,0},{16,24},{24,16},{1,9},{9,1},{17,25},{25,17},{2,10},{10... | collective-permute-start | bytes 2359304 | tf_op jit(solution)/shard_map/ppermute | solution.py:749
  28.4 22.4 %collective-permute-start.13 = (bf16[128,3072]{1,0:T(8,128)(2,1)S(1)}, bf16[128,3072]{1,0:T(8,128)(2,1)S(1)}, u32[]{:S(2)}, u32[]{:S(2)}) collective-permute-start(bf16[128,3072]{1,0:T(8,128)(2,1)S(1)} %collective-permute-done.12.refs_0_), channel_id=1, source_target_pairs={{0,16},{1,17},{2,18},{3,19},{12,28},{13,29},{14,30},{15,31},{16,0}... | collective-permute-start | bytes 2359304 | tf_op jit(solution)/shard_map/ppermute | solution.py:767
  31.0 5.3 %collective-permute-start.6 = (bf16[32,3072]{1,0:T(8,128)(2,1)S(1)}, bf16[32,3072]{1,0:T(8,128)(2,1)S(1)}, u32[]{:S(2)}, u32[]{:S(2)}) collective-permute-start(bf16[32,3072]{1,0:T(8,128)(2,1)S(1)} %get-tuple-element.56), channel_id=1, source_target_pairs={{0,8},{8,0},{16,24},{24,16},{1,9},{9,1},{17,25},{25,17},{2,10},{10... | collective-permute-start | bytes 589832 | tf_op jit(solution)/shard_map/ppermute | solution.py:749
  31.1 5.2 %collective-permute-start.5 = (bf16[32,3072]{1,0:T(8,128)(2,1)S(1)}, bf16[32,3072]{1,0:T(8,128)(2,1)S(1)}, u32[]{:S(2)}, u32[]{:S(2)}) collective-permute-start(bf16[32,3072]{1,0:T(8,128)(2,1)S(1)} %get-tuple-element.57), channel_id=1, source_target_pairs={{0,8},{8,0},{16,24},{24,16},{1,9},{9,1},{17,25},{25,17},{2,10},{10... | collective-permute-start | bytes 589832 | tf_op jit(solution)/shard_map/ppermute | solution.py:749
  31.9 12.0 %collective-permute-start.11 = (bf16[2,32,768]{2,1,0:T(8,128)(2,1)S(1)}, bf16[2,32,768]{2,1,0:T(8,128)(2,1)S(1)}, u32[]{:S(2)}, u32[]{:S(2)}) collective-permute-start(bf16[2,32,768]{2,1,0:T(8,128)(2,1)S(1)} %get-tuple-element.32), channel_id=1, source_target_pairs={{0,20},{1,21},{2,22},{3,23},{4,16},{5,17},{6,18},{7,19},{8,28},{9,... | collective-permute-start | bytes 294920 | tf_op jit(solution)/shard_map/ppermute | solution.py:767
  32.2 11.7 %collective-permute-start.9 = (bf16[2,32,768]{2,1,0:T(8,128)(2,1)S(1)}, bf16[2,32,768]{2,1,0:T(8,128)(2,1)S(1)}, u32[]{:S(2)}, u32[]{:S(2)}) collective-permute-start(bf16[2,32,768]{2,1,0:T(8,128)(2,1)S(1)} %get-tuple-element.32), channel_id=1, source_target_pairs={{0,4},{1,5},{2,6},{3,7},{4,0},{5,1},{6,2},{7,3},{8,12},{9,13},{10,... | collective-permute-start | bytes 294920 | tf_op jit(solution)/shard_map/ppermute | solution.py:767
  36.2 10.2 %collective-permute-start.10 = (bf16[2,32,768]{2,1,0:T(8,128)(2,1)S(1)}, bf16[2,32,768]{2,1,0:T(8,128)(2,1)S(1)}, u32[]{:S(2)}, u32[]{:S(2)}) collective-permute-start(bf16[2,32,768]{2,1,0:T(8,128)(2,1)S(1)} %get-tuple-element.33.refs_0_), channel_id=1, source_target_pairs={{0,16},{1,17},{2,18},{3,19},{4,20},{5,21},{6,22},{7,23},{8,24},{9,... | collective-permute-start | bytes 294920 | tf_op jit(solution)/shard_map/ppermute | solution.py:767
  36.3 15.2 %collective-permute-start.14 = (bf16[128,3072]{1,0:T(8,128)(2,1)S(1)}, bf16[128,3072]{1,0:T(8,128)(2,1)S(1)}, u32[]{:S(2)}, u32[]{:S(2)}) collective-permute-start(bf16[128,3072]{1,0:T(8,128)(2,1)S(1)} %collective-permute-done.12.refs_0_), channel_id=1, source_target_pairs={{0,8},{8,0},{16,24},{24,16},{1,9},{9,1},{17,25},{25,17},{2,10},{10... | collective-permute-start | bytes 2359304 | tf_op jit(solution)/shard_map/ppermute | solution.py:749
  46.5 5.0 %collective-permute-start.17 = (bf16[8,32,768]{2,1,0:T(8,128)(2,1)S(1)}, bf16[8,32,768]{2,1,0:T(8,128)(2,1)S(1)}, u32[]{:S(2)}, u32[]{:S(2)}) collective-permute-start(bf16[8,32,768]{2,1,0:T(8,128)(2,1)S(1)} %shard_map.161.refs_5_), channel_id=1, source_target_pairs={{0,8},{8,0},{16,24},{24,16},{1,9},{9,1},{17,25},{25,17},{2,10},{10... | collective-permute-start | bytes 1179656 | tf_op jit(solution)/shard_map/ppermute | solution.py:749
  46.6 16.0 %all-to-all-start = ((bf16[4,256,384]{2,1,0:T(8,128)(2,1)}), bf16[4,256,384]{2,1,0:T(8,128)(2,1)}, u32[]{:S(2)}, u32[]{:S(2)}) async-start(bf16[4,256,384]{2,1,0:T(8,128)(2,1)} %shard_map.160), calls=%async_computation | async-start | bytes 1572864 | tf_op jit(solution)/shard_map/all_to_all | solution.py:771
  50.8 1.9 %collective-permute-start.16 = (bf16[64,3072]{1,0:T(8,128)(2,1)S(1)}, bf16[64,3072]{1,0:T(8,128)(2,1)S(1)}, u32[]{:S(2)}, u32[]{:S(2)}) collective-permute-start(bf16[64,3072]{1,0:T(8,128)(2,1)S(1)} %get-tuple-element.52), channel_id=1, source_target_pairs={{0,8},{8,0},{16,24},{24,16},{1,9},{9,1},{17,25},{25,17},{2,10},{10... | collective-permute-start | bytes 1179656 | tf_op jit(solution)/shard_map/ppermute | solution.py:749
  51.4 1.9 %collective-permute-start.15 = (bf16[64,3072]{1,0:T(8,128)(2,1)S(1)}, bf16[64,3072]{1,0:T(8,128)(2,1)S(1)}, u32[]{:S(2)}, u32[]{:S(2)}) collective-permute-start(bf16[64,3072]{1,0:T(8,128)(2,1)S(1)} %get-tuple-element.53), channel_id=1, source_target_pairs={{0,8},{8,0},{16,24},{24,16},{1,9},{9,1},{17,25},{25,17},{2,10},{10... | collective-permute-start | bytes 1179656 | tf_op jit(solution)/shard_map/ppermute | solution.py:749
  91.1 15.0 %all-to-all-start.2 = ((bf16[8,192,128]{2,1,0:T(8,128)(2,1)}), bf16[8,192,128]{2,1,0:T(8,128)(2,1)S(1)}, u32[]{:S(2)}, u32[]{:S(2)}) async-start(bf16[8,192,128]{2,1,0:T(8,128)(2,1)} %shard_map.163), calls=%async_computation.2 | async-start | bytes 786432 | tf_op jit(solution)/shard_map/all_to_all | solution.py:755
  108.0 4.5 %collective-permute-start.18 = (bf16[192,3072]{1,0:T(8,128)(2,1)}, bf16[192,3072]{1,0:T(8,128)(2,1)}, u32[]{:S(2)}, u32[]{:S(2)}) collective-permute-start(bf16[192,3072]{1,0:T(8,128)(2,1)} %shard_map.165), channel_id=1, source_target_pairs={{0,8},{8,0},{16,24},{24,16},{1,9},{9,1},{17,25},{25,17},{2,10},{10... | collective-permute-start | bytes 3538952 | tf_op jit(solution)/shard_map/ppermute | solution.py:749
  108.0 25.3 %all-to-all-start.3 = ((bf16[8,384,128]{2,1,0:T(8,128)(2,1)}), bf16[8,384,128]{2,1,0:T(8,128)(2,1)}, u32[]{:S(2)}, u32[]{:S(2)}) async-start(bf16[8,384,128]{2,1,0:T(8,128)(2,1)} %shard_map.164), calls=%async_computation.3 | async-start | bytes 1572864 | tf_op jit(solution)/shard_map/all_to_all | solution.py:755
  115.6 28.7 %collective-permute-start.23 = (bf16[192,3072]{1,0:T(8,128)(2,1)}, bf16[192,3072]{1,0:T(8,128)(2,1)}, u32[]{:S(2)}, u32[]{:S(2)}) collective-permute-start(bf16[192,3072]{1,0:T(8,128)(2,1)} %shard_map.166), channel_id=1, source_target_pairs={{0,16},{8,24},{16,0},{24,8},{1,17},{9,25},{17,1},{25,9},{2,18},{10... | collective-permute-start | bytes 3538952 | tf_op jit(solution)/shard_map/ppermute | solution.py:752
  135.3 3.2 %collective-permute-start.19 = (bf16[64,3072]{1,0:T(8,128)(2,1)S(1)}, bf16[64,3072]{1,0:T(8,128)(2,1)S(1)}, u32[]{:S(2)}, u32[]{:S(2)}) collective-permute-start(bf16[64,3072]{1,0:T(8,128)(2,1)S(1)} %get-tuple-element.46), channel_id=1, source_target_pairs={{0,8},{8,0},{16,24},{24,16},{1,9},{9,1},{17,25},{25,17},{2,10},{10... | collective-permute-start | bytes 1179656 | tf_op jit(solution)/shard_map/ppermute | solution.py:749
  135.4 3.1 %collective-permute-start.20 = (bf16[64,3072]{1,0:T(8,128)(2,1)S(1)}, bf16[64,3072]{1,0:T(8,128)(2,1)S(1)}, u32[]{:S(2)}, u32[]{:S(2)}) collective-permute-start(bf16[64,3072]{1,0:T(8,128)(2,1)S(1)} %get-tuple-element.47), channel_id=1, source_target_pairs={{0,8},{8,0},{16,24},{24,16},{1,9},{9,1},{17,25},{25,17},{2,10},{10... | collective-permute-start | bytes 1179656 | tf_op jit(solution)/shard_map/ppermute | solution.py:749
  135.9 2.6 %collective-permute-start.21 = (bf16[64,3072]{1,0:T(8,128)(2,1)S(1)}, bf16[64,3072]{1,0:T(8,128)(2,1)S(1)}, u32[]{:S(2)}, u32[]{:S(2)}) collective-permute-start(bf16[64,3072]{1,0:T(8,128)(2,1)S(1)} %get-tuple-element.48), channel_id=1, source_target_pairs={{0,8},{8,0},{16,24},{24,16},{1,9},{9,1},{17,25},{25,17},{2,10},{10... | collective-permute-start | bytes 1179656 | tf_op jit(solution)/shard_map/ppermute | solution.py:749
  135.9 2.5 %collective-permute-start.22 = (bf16[64,1536]{1,0:T(8,128)(2,1)S(1)}, bf16[64,1536]{1,0:T(8,128)(2,1)S(1)}, u32[]{:S(2)}, u32[]{:S(2)}) collective-permute-start(bf16[64,1536]{1,0:T(8,128)(2,1)S(1)} %get-tuple-element.49), channel_id=1, source_target_pairs={{0,8},{8,0},{16,24},{24,16},{1,9},{9,1},{17,25},{25,17},{2,10},{10... | collective-permute-start | bytes 589832 | tf_op jit(solution)/shard_map/ppermute | solution.py:749
  (9 other events, 105.7 us)

commit v5 on v4

--- a/solution.py
+++ b/solution.py
@@ -339,8 +339,8 @@
     lo = 2 * rows
     if has_text:
         text_ref = refs[0]
-        blocks, trows, width = text_here_ref.shape
-        blocks = blocks // 2
+        _, _, trows, width = text_here_ref.shape
+        blocks, row = 4, mine // 2
         for b in range(4):
             for q in range(4):
                 part = text_core_ref if q & 1 else text_here_ref
@@ -350,7 +350,7 @@
                     for t in range(blocks):
                         job_of, shard_of, chip_of = t // 2, t % 2, q // 2
                         text_ref[t * trows : (t + 1) * trows, b * width : (b + 1) * width] = part[
-                            4 * chip_of + 2 * shard_of + (job_of ^ chip_of)
+                            2 * (row ^ chip_of) + (half ^ shard_of), job_of ^ chip_of
                         ]
 
         x_ref[lo:] = text_ref[...]
@@ -368,10 +368,10 @@
     rows_in = rows_out = 2 * here[0].shape[0]
     extra = []
     if text:
-        blocks, trows, _ = text[0].shape
-        rows_in += blocks // 2 * trows
+        blocks, jobs, trows, _ = text[0].shape
+        rows_in += blocks * trows
         rows_out = rows_in + 2 * trows
-        extra = [pltpu.VMEM((blocks // 2 * trows, width), jnp.bfloat16)]
+        extra = [pltpu.VMEM((blocks * trows, width), jnp.bfloat16)]
     inputs = (*here, *from_core[0], *from_core[1], *text)
     tables = (*tables, q_gain, k_gain)
     return pl.pallas_call(
@@ -393,16 +393,18 @@
 
 
 def refine_kernel(
-    group, holder_ref, n0_ref, n1_ref, n2_ref, n3_ref, w_hbm, bias_hbm, keep_ref, send_ref, x_ref,
-    w_ref, bias_ref, sems,
+    group, holder_ref, n0_ref, n1_ref, n2_ref, n3_ref, w_hbm, bias_hbm, out_ref, x_ref, w_ref,
+    bias_ref, sems,
 ):
-    mine, _, _, job = my_place(group)
+    mine, _, half, job = my_place(group)
     chunks, depth, _ = w_ref.shape
-    copies = fetch(
-        [w_hbm.at[pl.ds(i * depth, depth)] for i in range(chunks)] + [bias_hbm],
-        [w_ref.at[i] for i in range(chunks)] + [bias_ref],
-        sems,
-    )
+    copies = [
+        pltpu.make_async_copy(w_hbm.at[pl.ds(i * depth, depth)], w_ref.at[i], sems.at[i])
+        for i in range(chunks)
+    ]
+    (bias_copy,) = fetch([bias_hbm], [bias_ref], sems.at[pl.ds(chunks, 1)])
+    copies[0].start()
+    copies[1].start()
     rows = n0_ref.shape[0]
     for k, flip in enumerate((0, 2, 1, 3)):
         for r, part in enumerate((n0_ref, n1_ref, n2_ref, n3_ref)):
@@ -411,28 +413,30 @@
             def _():
                 x_ref[k * rows : (k + 1) * rows] = part[...]
 
-    copies[-1].wait()
+    bias_copy.wait()
     lifted = bias_ref[...]
     for i in range(chunks):
         copies[i].wait()
+        if i + 2 < chunks:
+            copies[i + 2].start()
         part = x_ref[:, i * depth : (i + 1) * depth]
         lifted = lifted + jnp.dot(part, w_ref[i], preferred_element_type=jnp.float32)
     refined = lifted.astype(jnp.bfloat16)
-    for k in range(2):
-        keep_ref[k] = refined[k * rows : (k + 1) * rows]
-        send_ref[k] = refined[(2 + k) * rows : (3 + k) * rows]
+    for chip in range(2):
+        for k in range(2):
+            out_ref[2 * chip + half, k] = refined[k * rows : (k + 1) * rows]
+            out_ref[2 * chip + 1 - half, k] = refined[(2 + k) * rows : (3 + k) * rows]
 
 
 def refine_text(group, holder, normed, weights, bias):
     rows, depth = normed[0].shape
     width = weights.shape[1]
     chunks = 4
-    out = jax.ShapeDtypeStruct((2, rows, width), jnp.bfloat16)
     return pl.pallas_call(
         functools.partial(refine_kernel, group),
-        out_shape=(out, out),
+        out_shape=pltpu.HBM((4, 2, rows, width), jnp.bfloat16),
         in_specs=[smem_spec()] + [vmem_spec()] * 4 + [hbm_spec()] * 2,
-        out_specs=(vmem_spec(), vmem_spec()),
+        out_specs=vmem_spec(),
         scratch_shapes=[
             pltpu.VMEM((4 * rows, depth), jnp.bfloat16),
             pltpu.VMEM((chunks, depth // chunks, width), jnp.bfloat16),
@@ -442,24 +446,6 @@
         compiler_params=params(14),
         cost_estimate=cost(8 * rows * depth * width, 2 * depth * width),
     )(holder, *normed, in_hbm(weights), in_hbm(bias[None]))
-
-
-def pack_kernel(*refs):
-    out_ref = refs[-1]
-    for i, ref in enumerate(refs[:-1]):
-        out_ref[i * ref.shape[0] : (i + 1) * ref.shape[0]] = ref[...]
-
-
-def pack(parts):
-    jobs, rows, width = parts[0].shape
-    return pl.pallas_call(
-        pack_kernel,
-        out_shape=jax.ShapeDtypeStruct((len(parts) * jobs, rows, width), jnp.bfloat16),
-        in_specs=[vmem_spec()] * len(parts),
-        out_specs=vmem_spec(),
-        compiler_params=params(4),
-        cost_estimate=cost(0, 4 * len(parts) * parts[0].size),
-    )(*parts)
 
 
 def choose_slots(count_ref, splits_ref, job, row, table, put):
@@ -658,10 +644,10 @@
 
 
 def final_kernel(
-    count_ref, splits_ref, video_hbm, part_ref, chip_hbm, gate_hbm, slot_ref, vout_hbm, tout_hbm,
-    chip_ref, out_ref, video_ref, gate_ref, in_sems, out_sems,
+    count_ref, splits_ref, video_ref, part_ref, chip_hbm, gate_ref, slot_ref, vout_hbm, tout_hbm,
+    chip_ref, out_ref, in_sems, out_sems,
 ):
-    vrows, step = video_ref.shape[0], slot_ref.shape[0]
+    vrows, step = video_ref.shape[1], slot_ref.shape[0]
     total_rows = part_ref.shape[0]
     reads, writes = [], []
     for i, lo in enumerate(range(0, total_rows, step)):
@@ -671,9 +657,6 @@
         writes.append(pltpu.make_async_copy(out_ref.at[rows], target, out_sems.at[i]))
     for read in reads:
         read.start()
-    steps = len(reads)
-    for copy in fetch((video_hbm.at[0], gate_hbm), (video_ref, gate_ref), in_sems.at[pl.ds(steps, 2)]):
-        copy.wait()
     job, shard = lax.axis_index("job"), lax.axis_index("seq")
     gate = table_row(gate_ref, job)
     offset = jnp.int32(0)
@@ -685,7 +668,7 @@
         reads[i].wait()
         rows = slice(lo, lo + step)
         total = part_ref[rows].astype(jnp.float32) + chip_ref[rows].astype(jnp.float32)
-        base = video_ref[rows] if lo < vrows else slot_ref[...]
+        base = video_ref[0, rows] if lo < vrows else slot_ref[...]
         result = base.astype(jnp.float32) + gate * total
         if lo >= vrows:
             result = jnp.where(valid, result, 0.0)
@@ -706,20 +689,18 @@
             jax.ShapeDtypeStruct((1, rows - vrows, width), jnp.bfloat16),
         ),
         in_specs=[
-            smem_spec(), smem_spec(), hbm_spec(), vmem_spec(), hbm_spec(), hbm_spec(), vmem_spec(),
+            smem_spec(), smem_spec(), vmem_spec(), vmem_spec(), hbm_spec(), vmem_spec(), vmem_spec(),
         ],
         out_specs=(hbm_spec(), hbm_spec()),
         scratch_shapes=[
             pltpu.VMEM((rows, width), jnp.bfloat16),
             pltpu.VMEM((rows, width), jnp.bfloat16),
-            pltpu.VMEM((vrows, width), jnp.bfloat16),
-            pltpu.VMEM(gate.shape, jnp.float32),
-            pltpu.SemaphoreType.DMA((steps + 2,)),
+            pltpu.SemaphoreType.DMA((steps,)),
             pltpu.SemaphoreType.DMA((steps,)),
         ],
         compiler_params=params(8),
         cost_estimate=cost(6 * rows * width, 10 * rows * width),
-    )(count, splits, in_hbm(video), part, from_chip, in_hbm(gate), slot_rows)
+    )(count, splits, video, part, from_chip, gate, slot_rows)
 
 
 def two_wave_body(
@@ -785,23 +766,29 @@
     normed_core = to_core(after(normed, qkv_w))
 
     normed_both = to_core(normed_chip)
-    keep, send = refine_text(
+    refined = refine_text(
         group_size, holder, (normed, normed_core, normed_chip, normed_both), refine_w, refine_bias
     )
-    text = (
-        keep,
-        to_device(send, 0, True),
-        to_device(keep, 2, False),
-        to_device(send, 2, True),
-    )
-
-    other = after(other, keep)
+    fours = [
+        [
+            (job + chip) * shard_count + shard + half
+            for chip in (0, 2)
+            for half in (0, group_size)
+        ]
+        for job in range(2)
+        for shard in range(group_size)
+    ]
+    text = lax.all_to_all(
+        refined, ("job", "seq"), split_axis=0, concat_axis=0, tiled=False, axis_index_groups=fours
+    )
+
+    other = after(other, refined)
     other_chip = to_device(other, 2, False, staying=True)
-    own_chip = after(own_chip, keep)
+    own_chip = after(own_chip, refined)
     first_send = qkv_half(
         (own, own_chip), (core_pieces(own, 1), core_pieces(own_chip, 4)), (), tables, qkv_w, q_gain, k_gain
     )
-    text = pack(after(text, first_send))
+    text = after(text, first_send)
     first = over_half(after(first_send, text))
 
     other_chip = after(other_chip, first_send)

time: 149 us -> 147 us (0.987)
  waiting for transfers between devices: 38.2 us -> 31 us
  Pallas kernels: 46.5 us -> 48.5 us
  starting transfers between devices: 29.6 us -> 31.3 us
    ppermute x6 -> x3, waiting for transfers between devices: 6.1 us -> 0.01 us  [to_device(): return lax.ppermute(x, ('job', 'seq'), perm)]
    all_to_all x0 -> x1, starting transfers between devices: none -> 3.47 us  [two_wave_body(): lax.all_to_all(refined, ('job', 'seq'), split_axis=0, concat_axis=0, tile...]
    pallas_call x2, Pallas kernels: 16.6 us -> 18.9 us  [qkv_half(): pl.pallas_call(functools.partial(qkv_kernel, pieces, bool(text)), out_sha...]
    ppermute x6 -> x3, starting transfers between devices: 9.43 us -> 7.26 us  [to_device(): return lax.ppermute(x, ('job', 'seq'), perm)]
    unnamed x13 -> x21, local copies, waits for them, and re-layouts: 8.97 us -> 10.1 us
    pallas_call x2 -> x1, Pallas kernels: 4.78 us -> 5.29 us  [refine_text(): pl.pallas_call(functools.partial(refine_kernel, group), out_shape=pltpu.H...]
  transfers between devices with their start and end apart: 27 -> 25, of which waited for: 13 -> 12; matrix products, arithmetic and copies ran while one was open for 7% -> 7% of each run, Pallas kernels for 23% -> 25%
where the time goes in v5:
time: 147 us; the launch traced here: 146 us
  Pallas kernels  48.5 us (33%)
  starting transfers between devices  31.3 us (21%)
  waiting for transfers between devices  31 us (21%)
  blocking collectives  23.1 us (16%)
  local copies, waits for them, and re-layouts  10.8 us (7%)
    all_to_all x1, blocking collectives, over_half(): lax.all_to_all(x, 'seq', split_axis=0, concat_axis=0, tiled=False, axis_i...  23.1 us
    all_to_all x2, waiting for transfers between devices, over_seq(): return lax.all_to_all(x, 'seq', split_axis=0, concat_axis=0, tiled=False)  21.8 us
    pallas_call x2, Pallas kernels, qkv_half(): pl.pallas_call(functools.partial(qkv_kernel, pieces, bool(text)), out_sha...  18.9 us
    pallas_call x2, Pallas kernels, attend_pair(): pl.pallas_call(functools.partial(attention_kernel, far), out_shape=pltpu....  11.4 us
    unnamed x21, local copies, waits for them, and re-layouts  10.1 us
    pallas_call x4, Pallas kernels, out_call(): pl.pallas_call(kernel, out_shape=tuple((jax.ShapeDtypeStruct(shape, jnp.b...  8.85 us
    all_to_all x2, starting transfers between devices, over_seq(): return lax.all_to_all(x, 'seq', split_axis=0, concat_axis=0, tiled=False)  8.18 us
    ppermute x3, starting transfers between devices, to_device(): return lax.ppermute(x, ('job', 'seq'), perm)  7.26 us
  transfers between devices with their start and end apart: 25, of which 12 were waited for; matrix products, arithmetic and copies ran while one was open for 7% of the time, Pallas kernels for 25%

profile of v5, /device:TPU:0, one launch (start us, length us, event | category | flops | bytes accessed | tf_op | source)
XLA Modules:
  0.0 145.7 jit_solution(13698242277583659877)
XLA Ops:
  1.8 3.0 %collective-permute-start = (bf16[32,4096]{1,0:T(8,128)(2,1)S(1)}, bf16[32,4096]{1,0:T(8,128)(2,1)S(1)}, u32[]{:S(2)}, u32[]{:S(2)}) collective-permute-start(bf16[32,4096]{1,0:T(8,128)(2,1)S(1)} %shard_map.158.n0_ref), channel_id=1, source_target_pairs={{0,16},{8,24},{16,0},{24,8},{1,17},{9,25},{17,1},{25,9},{2,18},{10... | collective-permute-start | bytes 786440 | tf_op jit(solution)/shard_map/ppermute | solution.py:733
  4.8 1.4 collective-permute-start.9
  6.2 8.9 %copy.19 = bf16[3072,4,3,128]{3,0,1,2:T(8,128)(2,1)} copy(bf16[3072,4,3,128]{3,1,2,0:T(4,128)(2,1)} %param.26) | data formatting | bytes 18874368 | tf_op args[11]
  15.2 2.0 %collective-permute-start.1 = (bf16[128,3072]{1,0:T(8,128)(2,1)S(1)}, bf16[128,3072]{1,0:T(8,128)(2,1)S(1)}, u32[]{:S(2)}, u32[]{:S(2)}) collective-permute-start(bf16[128,3072]{1,0:T(8,128)(2,1)S(1)} %bitcast.11), channel_id=1, source_target_pairs={{0,16},{1,17},{2,18},{3,19},{12,28},{13,29},{14,30},{15,31},{16,0}... | collective-permute-start | bytes 2359304 | tf_op jit(solution)/shard_map/ppermute | solution.py:748
  20.0 5.3 %shard_map.159 = bf16[4,2,32,768]{3,2,1,0:T(8,128)(2,1)} custom-call(s32[4]{0:T(128)S(1)} %copy-done.7, bf16[32,4096]{1,0:T(8,128)(2,1)S(1)} %shard_map.158.n0_ref, bf16[32,4096]{1,0:T(8,128)(2,1)S(1)} %collective-permute-done.2.n1_ref, bf16[32,4096]{1,0:T(8,128)(2,1)S(1)} %collective-permute-done.n2_ref, ...), custom_call_target="tpu_custom_call" | custom-call | flops 805306368 | bytes 6291456 | tf_op jit(solution)/shard_map/pallas_call | solution.py:435
  25.3 3.5 %all-to-all-start = ((bf16[4,2,32,768]{3,2,1,0:T(8,128)(2,1)}), bf16[4,2,32,768]{3,2,1,0:T(8,128)(2,1)S(1)}, u32[]{:S(2)}, u32[]{:S(2)}) async-start(bf16[4,2,32,768]{3,2,1,0:T(8,128)(2,1)} %shard_map.159), calls=%async_computation | async-start | bytes 786432 | tf_op jit(solution)/shard_map/all_to_all | solution.py:781
  28.8 3.9 %collective-permute-start.10 = (bf16[128,3072]{1,0:T(8,128)(2,1)S(1)}, bf16[128,3072]{1,0:T(8,128)(2,1)S(1)}, u32[]{:S(2)}, u32[]{:S(2)}) collective-permute-start(bf16[128,3072]{1,0:T(8,128)(2,1)S(1)} %collective-permute-done.9.refs_0_), channel_id=1, source_target_pairs={{0,16},{1,17},{2,18},{3,19},{12,28},{13,29},{14,30},{15,31},{16,0}... | collective-permute-start | bytes 2359304 | tf_op jit(solution)/shard_map/ppermute | solution.py:748
  35.1 8.7 %shard_map.160 = bf16[4,256,384]{2,1,0:T(8,128)(2,1)} custom-call(bf16[128,3072]{1,0:T(8,128)(2,1)S(1)} %bitcast.13, bf16[128,3072]{1,0:T(8,128)(2,1)S(1)} %collective-permute-done.1.refs_1_, bf16[128,3072]{1,0:T(8,128)(2,1)} %collective-permute-done.4.refs_2_, bf16[32,3072]{1,0:T(8,128)(2,1)S(1)} %collective-permute-done.5.refs_3_, ...), custom_call_target="tpu_custom_call" | custom-call | flops 2415919104 | bytes 12582912 | tf_op jit(solution)/shard_map/pallas_call | solution.py:377
  44.1 3.8 %all-to-all-start.1 = ((bf16[4,256,384]{2,1,0:T(8,128)(2,1)}), bf16[4,256,384]{2,1,0:T(8,128)(2,1)S(1)}, u32[]{:S(2)}, u32[]{:S(2)}) async-start(bf16[4,256,384]{2,1,0:T(8,128)(2,1)} %shard_map.160), calls=%async_computation.1 | async-start | bytes 1572864 | tf_op jit(solution)/shard_map/all_to_all | solution.py:752
  50.3 10.2 %shard_map.161 = bf16[4,448,384]{2,1,0:T(8,128)(2,1)} custom-call(bf16[128,3072]{1,0:T(8,128)(2,1)S(1)} %collective-permute-done.9.refs_0_, bf16[128,3072]{1,0:T(8,128)(2,1)S(1)} %collective-permute-done.10.refs_1_, bf16[128,3072]{1,0:T(8,128)(2,1)} %collective-permute-done.11.refs_2_, bf16[64,3072]{1,0:T(8,128)(2,1)S(1)} %collective-permute-done.12.refs_3_, ...), custom_call_target="tpu_custom_call" | custom-call | flops 3623878656 | bytes 14155776 | tf_op jit(solution)/shard_map/pallas_call | solution.py:377
  60.6 23.1 %all_to_all.25.second_hbm = bf16[4,448,384]{2,1,0:T(8,128)(2,1)} all-to-all(bf16[4,448,384]{2,1,0:T(8,128)(2,1)} %shard_map.161), channel_id=1, replica_groups={{0,1,2,3},{4,5,6,7},{8,9,10,11},{12,13,14,15},{16,17,18,19},{20,21,22,2..., dimensions={0} | all-to-all | bytes 2752512 | tf_op jit(solution)/shard_map/all_to_all | solution.py:752
  83.7 5.5 %shard_map.162 = bf16[8,192,128]{2,1,0:T(8,128)(2,1)} custom-call(s32[4]{0:T(128)S(1)} %copy-done.8, s32[4,8]{1,0:T(4,128)S(1)} %copy-done.6, bf16[4,256,384]{2,1,0:T(8,128)(2,1)S(1)} %all-to-all-done.1.first_hbm, bf16[4,448,384]{2,1,0:T(8,128)(2,1)} %all_to_all.25.second_hbm), custom_call_target="tpu_custom_call" | custom-call | flops 838860800 | bytes 3145728 | tf_op jit(solution)/shard_map/pallas_call | solution.py:562
  89.3 3.7 %all-to-all-start.3 = ((bf16[8,192,128]{2,1,0:T(8,128)(2,1)}), bf16[8,192,128]{2,1,0:T(8,128)(2,1)S(1)}, u32[]{:S(2)}, u32[]{:S(2)}) async-start(bf16[8,192,128]{2,1,0:T(8,128)(2,1)} %shard_map.162), calls=%async_computation.3 | async-start | bytes 786432 | tf_op jit(solution)/shard_map/all_to_all | solution.py:736
  94.1 5.9 %shard_map.163 = bf16[8,384,128]{2,1,0:T(8,128)(2,1)} custom-call(s32[4]{0:T(128)S(1)} %copy-done.8, s32[4,8]{1,0:T(4,128)S(1)} %copy-done.6, bf16[4,256,384]{2,1,0:T(8,128)(2,1)S(1)} %copy-done.4, bf16[4,448,384]{2,1,0:T(8,128)(2,1)} %all_to_all.25.second_hbm), custom_call_target="tpu_custom_call" | custom-call | flops 838860800 | bytes 3145728 | tf_op jit(solution)/shard_map/pallas_call | solution.py:562
  100.0 4.5 %all-to-all-done.3.heads_ref = bf16[8,192,128]{2,1,0:T(8,128)(2,1)S(1)} async-done(((bf16[8,192,128]{2,1,0:T(8,128)(2,1)}), bf16[8,192,128]{2,1,0:T(8,128)(2,1)S(1)}, u32[]{:S(2)}, u32[]{:S(2)}) %all-to-all-start.3) | async-done | bytes 393248 | tf_op jit(solution)/shard_map/all_to_all | solution.py:736
  104.5 1.8 %shard_map.164 = bf16[192,3072]{1,0:T(8,128)(2,1)} custom-call(bf16[8,192,128]{2,1,0:T(8,128)(2,1)S(1)} %all-to-all-done.3.heads_ref, bf16[512,3072]{1,0:T(8,128)(2,1)S(1)} %bitcast.6), custom_call_target="tpu_custom_call" | custom-call | flops 603979776 | bytes 5505024 | tf_op jit(solution)/shard_map/pallas_call | solution.py:626
  106.3 4.4 %all-to-all-start.4 = ((bf16[8,384,128]{2,1,0:T(8,128)(2,1)}), bf16[8,384,128]{2,1,0:T(8,128)(2,1)}, u32[]{:S(2)}, u32[]{:S(2)}) async-start(bf16[8,384,128]{2,1,0:T(8,128)(2,1)} %shard_map.163), calls=%async_computation.4 | async-start | bytes 1572864 | tf_op jit(solution)/shard_map/all_to_all | solution.py:736
  110.8 3.1 %shard_map.165 = bf16[192,3072]{1,0:T(8,128)(2,1)} custom-call(bf16[8,192,128]{2,1,0:T(8,128)(2,1)S(1)} %all-to-all-done.3.heads_ref, bf16[512,3072]{1,0:T(8,128)(2,1)S(1)} %bitcast.7, bf16[192,3072]{1,0:T(8,128)(2,1)} %collective-permute-done.15.refs_0_), custom_call_target="tpu_custom_call" | custom-call | flops 603979776 | bytes 5505024 | tf_op jit(solution)/shard_map/pallas_call | solution.py:626
  114.4 17.2 %all-to-all-done.4.heads_ref = bf16[8,384,128]{2,1,0:T(8,128)(2,1)} async-done(((bf16[8,384,128]{2,1,0:T(8,128)(2,1)}), bf16[8,384,128]{2,1,0:T(8,128)(2,1)}, u32[]{:S(2)}, u32[]{:S(2)}) %all-to-all-start.4) | async-done | bytes 786464 | tf_op jit(solution)/shard_map/all_to_all | solution.py:736
  131.7 2.0 %shard_map.166 = (bf16[64,3072]{1,0:T(8,128)(2,1)S(1)}, bf16[64,3072]{1,0:T(8,128)(2,1)S(1)}, bf16[64,3072]{1,0:T(8,128)(2,1)S(1)}, bf16[64,1536]{1,0:T(8,128)(2,1)S(1)}) custom-call(bf16[8,384,128]{2,1,0:T(8,128)(2,1)} %all-to-all-done.4.heads_ref, bf16[512,3072]{1,0:T(8,128)(2,1)S(1)} %bitcast.8), custom_call_target="tpu_custom_call" | custom-call | flops 603979776 | bytes 5505024 | tf_op jit(solution)/shard_map/pallas_call | solution.py:626
  134.7 2.1 %collective-permute-done.19.refs_3_ = bf16[64,1536]{1,0:T(8,128)(2,1)S(1)} collective-permute-done((bf16[64,1536]{1,0:T(8,128)(2,1)S(1)}, bf16[64,1536]{1,0:T(8,128)(2,1)S(1)}, u32[]{:S(2)}, u32[]{:S(2)}) %collective-permute-start.19) | collective-permute-done | bytes 196640 | tf_op jit(solution)/shard_map/ppermute | solution.py:730
  136.9 2.0 %shard_map.167 = (bf16[192,3072]{1,0:T(8,128)(2,1)S(1)}, bf16[64,3072]{1,0:T(8,128)(2,1)S(1)}) custom-call(bf16[8,384,128]{2,1,0:T(8,128)(2,1)} %all-to-all-done.4.heads_ref, bf16[512,3072]{1,0:T(8,128)(2,1)S(1)} %bitcast.9, bf16[64,3072]{1,0:T(8,128)(2,1)S(1)} %collective-permute-done.16.refs_0_, bf16[64,3072]{1,0:T(8,128)(2,1)S(1)} %collective-permute-done.17.refs_1_, ...), custom_call_target="tpu_custom_call" | custom-call | flops 603979776 | bytes 5505024 | tf_op jit(solution)/shard_map/pallas_call | solution.py:626
  138.9 3.7 %collective-permute-done.20.chip_hbm = bf16[192,3072]{1,0:T(8,128)(2,1)} collective-permute-done((bf16[192,3072]{1,0:T(8,128)(2,1)}, bf16[192,3072]{1,0:T(8,128)(2,1)}, u32[]{:S(2)}, u32[]{:S(2)}) %collective-permute-start.20) | collective-permute-done | bytes 1179680 | tf_op jit(solution)/shard_map/ppermute | solution.py:733
  142.6 2.9 %shard_map.168 = (bf16[1,128,3072]{2,1,0:T(8,128)(2,1)}, bf16[1,64,3072]{2,1,0:T(8,128)(2,1)}) custom-call(s32[4]{0:T(128)S(1)} %copy-done.8, s32[4,8]{1,0:T(4,128)S(1)} %copy-done.6, bf16[1,128,3072]{2,1,0:T(8,128)(2,1)S(1)} %copy-done.2, bf16[192,3072]{1,0:T(8,128)(2,1)S(1)} %get-tuple-element.40.part_ref, ...), custom_call_target="tpu_custom_call" | custom-call | flops 3538944 | bytes 5898240 | tf_op jit(solution)/shard_map/pallas_call | solution.py:685
  (62 shorter events, 11.9 us)
Async XLA Ops:
  1.8 13.4 %collective-permute-start = (bf16[32,4096]{1,0:T(8,128)(2,1)S(1)}, bf16[32,4096]{1,0:T(8,128)(2,1)S(1)}, u32[]{:S(2)}, u32[]{:S(2)}) collective-permute-start(bf16[32,4096]{1,0:T(8,128)(2,1)S(1)} %shard_map.158.n0_ref), channel_id=1, source_target_pairs={{0,16},{8,24},{16,0},{24,8},{1,17},{9,25},{17,1},{25,9},{2,18},{10... | collective-permute-start | bytes 786440 | tf_op jit(solution)/shard_map/ppermute | solution.py:733
  4.8 24.0 %collective-permute-start.9 = (bf16[128,3072]{1,0:T(8,128)(2,1)}, bf16[128,3072]{1,0:T(8,128)(2,1)S(1)}, u32[]{:S(2)}, u32[]{:S(2)}) collective-permute-start(bf16[128,3072]{1,0:T(8,128)(2,1)} %bitcast.10), channel_id=1, source_target_pairs={{4,0},{5,1},{6,2},{7,3},{8,12},{9,13},{10,14},{11,15},{20,16},{21,... | collective-permute-start | bytes 2359304 | tf_op jit(solution)/shard_map/ppermute | solution.py:748
  15.2 17.5 %collective-permute-start.1 = (bf16[128,3072]{1,0:T(8,128)(2,1)S(1)}, bf16[128,3072]{1,0:T(8,128)(2,1)S(1)}, u32[]{:S(2)}, u32[]{:S(2)}) collective-permute-start(bf16[128,3072]{1,0:T(8,128)(2,1)S(1)} %bitcast.11), channel_id=1, source_target_pairs={{0,16},{1,17},{2,18},{3,19},{12,28},{13,29},{14,30},{15,31},{16,0}... | collective-permute-start | bytes 2359304 | tf_op jit(solution)/shard_map/ppermute | solution.py:748
  17.1 2.5 %collective-permute-start.2 = (bf16[32,4096]{1,0:T(8,128)(2,1)S(1)}, bf16[32,4096]{1,0:T(8,128)(2,1)S(1)}, u32[]{:S(2)}, u32[]{:S(2)}) collective-permute-start(bf16[32,4096]{1,0:T(8,128)(2,1)S(1)} %shard_map.158.n0_ref), channel_id=1, source_target_pairs={{0,8},{8,0},{16,24},{24,16},{1,9},{9,1},{17,25},{25,17},{2,10},{10... | collective-permute-start | bytes 786440 | tf_op jit(solution)/shard_map/ppermute | solution.py:730
  18.5 1.5 %collective-permute-start.3 = (bf16[32,4096]{1,0:T(8,128)(2,1)S(1)}, bf16[32,4096]{1,0:T(8,128)(2,1)S(1)}, u32[]{:S(2)}, u32[]{:S(2)}) collective-permute-start(bf16[32,4096]{1,0:T(8,128)(2,1)S(1)} %collective-permute-done.n2_ref), channel_id=1, source_target_pairs={{0,8},{8,0},{16,24},{24,16},{1,9},{9,1},{17,25},{25,17},{2,10},{10... | collective-permute-start | bytes 786440 | tf_op jit(solution)/shard_map/ppermute | solution.py:730
  18.6 14.9 %collective-permute-start.4 = (bf16[128,3072]{1,0:T(8,128)(2,1)S(1)}, bf16[128,3072]{1,0:T(8,128)(2,1)}, u32[]{:S(2)}, u32[]{:S(2)}) collective-permute-start(bf16[128,3072]{1,0:T(8,128)(2,1)S(1)} %bitcast.12), channel_id=1, source_target_pairs={{0,8},{8,0},{16,24},{24,16},{1,9},{9,1},{17,25},{25,17},{2,10},{10... | collective-permute-start | bytes 2359304 | tf_op jit(solution)/shard_map/ppermute | solution.py:730
  25.3 18.5 %all-to-all-start = ((bf16[4,2,32,768]{3,2,1,0:T(8,128)(2,1)}), bf16[4,2,32,768]{3,2,1,0:T(8,128)(2,1)S(1)}, u32[]{:S(2)}, u32[]{:S(2)}) async-start(bf16[4,2,32,768]{3,2,1,0:T(8,128)(2,1)} %shard_map.159), calls=%async_computation | async-start | bytes 786432 | tf_op jit(solution)/shard_map/all_to_all | solution.py:781
  28.8 19.1 %collective-permute-start.10 = (bf16[128,3072]{1,0:T(8,128)(2,1)S(1)}, bf16[128,3072]{1,0:T(8,128)(2,1)S(1)}, u32[]{:S(2)}, u32[]{:S(2)}) collective-permute-start(bf16[128,3072]{1,0:T(8,128)(2,1)S(1)} %collective-permute-done.9.refs_0_), channel_id=1, source_target_pairs={{0,16},{1,17},{2,18},{3,19},{12,28},{13,29},{14,30},{15,31},{16,0}... | collective-permute-start | bytes 2359304 | tf_op jit(solution)/shard_map/ppermute | solution.py:748
  32.8 1.5 %collective-permute-start.8 = (bf16[32,3072]{1,0:T(8,128)(2,1)S(1)}, bf16[32,3072]{1,0:T(8,128)(2,1)S(1)}, u32[]{:S(2)}, u32[]{:S(2)}) collective-permute-start(bf16[32,3072]{1,0:T(8,128)(2,1)S(1)} %get-tuple-element.44), channel_id=1, source_target_pairs={{0,8},{8,0},{16,24},{24,16},{1,9},{9,1},{17,25},{25,17},{2,10},{10... | collective-permute-start | bytes 589832 | tf_op jit(solution)/shard_map/ppermute | solution.py:730
  32.9 1.7 %collective-permute-start.7 = (bf16[32,3072]{1,0:T(8,128)(2,1)S(1)}, bf16[32,3072]{1,0:T(8,128)(2,1)S(1)}, u32[]{:S(2)}, u32[]{:S(2)}) collective-permute-start(bf16[32,3072]{1,0:T(8,128)(2,1)S(1)} %get-tuple-element.45), channel_id=1, source_target_pairs={{0,8},{8,0},{16,24},{24,16},{1,9},{9,1},{17,25},{25,17},{2,10},{10... | collective-permute-start | bytes 589832 | tf_op jit(solution)/shard_map/ppermute | solution.py:730
  33.4 1.7 %collective-permute-start.5 = (bf16[32,3072]{1,0:T(8,128)(2,1)S(1)}, bf16[32,3072]{1,0:T(8,128)(2,1)S(1)}, u32[]{:S(2)}, u32[]{:S(2)}) collective-permute-start(bf16[32,3072]{1,0:T(8,128)(2,1)S(1)} %get-tuple-element.47), channel_id=1, source_target_pairs={{0,8},{8,0},{16,24},{24,16},{1,9},{9,1},{17,25},{25,17},{2,10},{10... | collective-permute-start | bytes 589832 | tf_op jit(solution)/shard_map/ppermute | solution.py:730
  34.3 14.3 %collective-permute-start.11 = (bf16[128,3072]{1,0:T(8,128)(2,1)S(1)}, bf16[128,3072]{1,0:T(8,128)(2,1)}, u32[]{:S(2)}, u32[]{:S(2)}) collective-permute-start(bf16[128,3072]{1,0:T(8,128)(2,1)S(1)} %collective-permute-done.9.refs_0_), channel_id=1, source_target_pairs={{0,8},{8,0},{16,24},{24,16},{1,9},{9,1},{17,25},{25,17},{2,10},{10... | collective-permute-start | bytes 2359304 | tf_op jit(solution)/shard_map/ppermute | solution.py:730
  43.8 4.7 %collective-permute-start.14 = (bf16[4,2,32,768]{3,2,1,0:T(8,128)(2,1)S(1)}, bf16[4,2,32,768]{3,2,1,0:T(8,128)(2,1)S(1)}, u32[]{:S(2)}, u32[]{:S(2)}) collective-permute-start(bf16[4,2,32,768]{3,2,1,0:T(8,128)(2,1)S(1)} %all-to-all-done.refs_5_), channel_id=1, source_target_pairs={{0,8},{8,0},{16,24},{24,16},{1,9},{9,1},{17,25},{25,17},{2,10},{10... | collective-permute-start | bytes 1179656 | tf_op jit(solution)/shard_map/ppermute | solution.py:730
  44.1 16.4 %all-to-all-start.1 = ((bf16[4,256,384]{2,1,0:T(8,128)(2,1)}), bf16[4,256,384]{2,1,0:T(8,128)(2,1)S(1)}, u32[]{:S(2)}, u32[]{:S(2)}) async-start(bf16[4,256,384]{2,1,0:T(8,128)(2,1)} %shard_map.160), calls=%async_computation.1 | async-start | bytes 1572864 | tf_op jit(solution)/shard_map/all_to_all | solution.py:752
  48.0 1.8 %collective-permute-start.13 = (bf16[64,3072]{1,0:T(8,128)(2,1)S(1)}, bf16[64,3072]{1,0:T(8,128)(2,1)S(1)}, u32[]{:S(2)}, u32[]{:S(2)}) collective-permute-start(bf16[64,3072]{1,0:T(8,128)(2,1)S(1)} %get-tuple-element.42), channel_id=1, source_target_pairs={{0,8},{8,0},{16,24},{24,16},{1,9},{9,1},{17,25},{25,17},{2,10},{10... | collective-permute-start | bytes 1179656 | tf_op jit(solution)/shard_map/ppermute | solution.py:730
  48.1 2.3 %collective-permute-start.12 = (bf16[64,3072]{1,0:T(8,128)(2,1)S(1)}, bf16[64,3072]{1,0:T(8,128)(2,1)S(1)}, u32[]{:S(2)}, u32[]{:S(2)}) collective-permute-start(bf16[64,3072]{1,0:T(8,128)(2,1)S(1)} %get-tuple-element.43), channel_id=1, source_target_pairs={{0,8},{8,0},{16,24},{24,16},{1,9},{9,1},{17,25},{25,17},{2,10},{10... | collective-permute-start | bytes 1179656 | tf_op jit(solution)/shard_map/ppermute | solution.py:730
  89.3 15.3 %all-to-all-start.3 = ((bf16[8,192,128]{2,1,0:T(8,128)(2,1)}), bf16[8,192,128]{2,1,0:T(8,128)(2,1)S(1)}, u32[]{:S(2)}, u32[]{:S(2)}) async-start(bf16[8,192,128]{2,1,0:T(8,128)(2,1)} %shard_map.162), calls=%async_computation.3 | async-start | bytes 786432 | tf_op jit(solution)/shard_map/all_to_all | solution.py:736
  106.3 4.5 %collective-permute-start.15 = (bf16[192,3072]{1,0:T(8,128)(2,1)}, bf16[192,3072]{1,0:T(8,128)(2,1)}, u32[]{:S(2)}, u32[]{:S(2)}) collective-permute-start(bf16[192,3072]{1,0:T(8,128)(2,1)} %shard_map.164), channel_id=1, source_target_pairs={{0,8},{8,0},{16,24},{24,16},{1,9},{9,1},{17,25},{25,17},{2,10},{10... | collective-permute-start | bytes 3538952 | tf_op jit(solution)/shard_map/ppermute | solution.py:730
  106.3 25.3 %all-to-all-start.4 = ((bf16[8,384,128]{2,1,0:T(8,128)(2,1)}), bf16[8,384,128]{2,1,0:T(8,128)(2,1)}, u32[]{:S(2)}, u32[]{:S(2)}) async-start(bf16[8,384,128]{2,1,0:T(8,128)(2,1)} %shard_map.163), calls=%async_computation.4 | async-start | bytes 1572864 | tf_op jit(solution)/shard_map/all_to_all | solution.py:736
  113.9 28.7 %collective-permute-start.20 = (bf16[192,3072]{1,0:T(8,128)(2,1)}, bf16[192,3072]{1,0:T(8,128)(2,1)}, u32[]{:S(2)}, u32[]{:S(2)}) collective-permute-start(bf16[192,3072]{1,0:T(8,128)(2,1)} %shard_map.165), channel_id=1, source_target_pairs={{0,16},{8,24},{16,0},{24,8},{1,17},{9,25},{17,1},{25,9},{2,18},{10... | collective-permute-start | bytes 3538952 | tf_op jit(solution)/shard_map/ppermute | solution.py:733
  133.6 3.2 %collective-permute-start.16 = (bf16[64,3072]{1,0:T(8,128)(2,1)S(1)}, bf16[64,3072]{1,0:T(8,128)(2,1)S(1)}, u32[]{:S(2)}, u32[]{:S(2)}) collective-permute-start(bf16[64,3072]{1,0:T(8,128)(2,1)S(1)} %get-tuple-element.36), channel_id=1, source_target_pairs={{0,8},{8,0},{16,24},{24,16},{1,9},{9,1},{17,25},{25,17},{2,10},{10... | collective-permute-start | bytes 1179656 | tf_op jit(solution)/shard_map/ppermute | solution.py:730
  133.7 3.1 %collective-permute-start.17 = (bf16[64,3072]{1,0:T(8,128)(2,1)S(1)}, bf16[64,3072]{1,0:T(8,128)(2,1)S(1)}, u32[]{:S(2)}, u32[]{:S(2)}) collective-permute-start(bf16[64,3072]{1,0:T(8,128)(2,1)S(1)} %get-tuple-element.37), channel_id=1, source_target_pairs={{0,8},{8,0},{16,24},{24,16},{1,9},{9,1},{17,25},{25,17},{2,10},{10... | collective-permute-start | bytes 1179656 | tf_op jit(solution)/shard_map/ppermute | solution.py:730
  134.2 2.6 %collective-permute-start.18 = (bf16[64,3072]{1,0:T(8,128)(2,1)S(1)}, bf16[64,3072]{1,0:T(8,128)(2,1)S(1)}, u32[]{:S(2)}, u32[]{:S(2)}) collective-permute-start(bf16[64,3072]{1,0:T(8,128)(2,1)S(1)} %get-tuple-element.38), channel_id=1, source_target_pairs={{0,8},{8,0},{16,24},{24,16},{1,9},{9,1},{17,25},{25,17},{2,10},{10... | collective-permute-start | bytes 1179656 | tf_op jit(solution)/shard_map/ppermute | solution.py:730
  134.3 2.5 %collective-permute-start.19 = (bf16[64,1536]{1,0:T(8,128)(2,1)S(1)}, bf16[64,1536]{1,0:T(8,128)(2,1)S(1)}, u32[]{:S(2)}, u32[]{:S(2)}) collective-permute-start(bf16[64,1536]{1,0:T(8,128)(2,1)S(1)} %get-tuple-element.39), channel_id=1, source_target_pairs={{0,8},{8,0},{16,24},{24,16},{1,9},{9,1},{17,25},{25,17},{2,10},{10... | collective-permute-start | bytes 589832 | tf_op jit(solution)/shard_map/ppermute | solution.py:730
  (11 other events, 143.7 us)

commit v6 on v5

--- a/solution.py
+++ b/solution.py
@@ -273,9 +273,6 @@
     for first in range(0, heads, 2):
         for copy in weight_copies(w_hbm, w_ref, sems, first):
             copy.wait()
-        if first + 2 < heads:
-            for copy in weight_copies(w_hbm, w_ref, sems, first + 2):
-                copy.start()
         pair = (first, first + 1)
         weights = jnp.concatenate([w_ref[c, h] for h in pair for c in range(3)], axis=1)
         raw = jnp.dot(x_ref[...], weights, preferred_element_type=jnp.float32)
@@ -327,8 +324,9 @@
     shift_ref, scale_ref, qg_ref, kg_ref = table_refs
     rows, group = a_ref.shape[0], w_ref.shape[1]
     tables = fetch(table_hbm, table_refs, sems.at[pl.ds(2 * group, 4)])
-    for copy in weight_copies(w_hbm, w_ref, sems, 0):
-        copy.start()
+    for first in range(0, group, 2):
+        for copy in weight_copies(w_hbm, w_ref, sems, first):
+            copy.start()
     mine, core, half, job = my_place(group)
     take_rows(x_ref, 0, a_ref, a_core, core == half)
     take_rows(x_ref, rows, b_ref, b_core, core == half)
@@ -403,8 +401,8 @@
         for i in range(chunks)
     ]
     (bias_copy,) = fetch([bias_hbm], [bias_ref], sems.at[pl.ds(chunks, 1)])
-    copies[0].start()
-    copies[1].start()
+    for copy in copies[:3]:
+        copy.start()
     rows = n0_ref.shape[0]
     for k, flip in enumerate((0, 2, 1, 3)):
         for r, part in enumerate((n0_ref, n1_ref, n2_ref, n3_ref)):
@@ -414,11 +412,11 @@
                 x_ref[k * rows : (k + 1) * rows] = part[...]
 
     bias_copy.wait()
-    lifted = bias_ref[...]
+    lifted = bias_ref[...].reshape(1, -1)
     for i in range(chunks):
         copies[i].wait()
-        if i + 2 < chunks:
-            copies[i + 2].start()
+        if i + 3 < chunks:
+            copies[i + 3].start()
         part = x_ref[:, i * depth : (i + 1) * depth]
         lifted = lifted + jnp.dot(part, w_ref[i], preferred_element_type=jnp.float32)
     refined = lifted.astype(jnp.bfloat16)
@@ -434,18 +432,18 @@
     chunks = 4
     return pl.pallas_call(
         functools.partial(refine_kernel, group),
-        out_shape=pltpu.HBM((4, 2, rows, width), jnp.bfloat16),
+        out_shape=jax.ShapeDtypeStruct((4, 2, rows, width), jnp.bfloat16),
         in_specs=[smem_spec()] + [vmem_spec()] * 4 + [hbm_spec()] * 2,
         out_specs=vmem_spec(),
         scratch_shapes=[
             pltpu.VMEM((4 * rows, depth), jnp.bfloat16),
             pltpu.VMEM((chunks, depth // chunks, width), jnp.bfloat16),
-            pltpu.VMEM((1, width), jnp.float32),
+            pltpu.VMEM((width,), jnp.float32),
             pltpu.SemaphoreType.DMA((chunks + 1,)),
         ],
         compiler_params=params(14),
         cost_estimate=cost(8 * rows * depth * width, 2 * depth * width),
-    )(holder, *normed, in_hbm(weights), in_hbm(bias[None]))
+    )(holder, *normed, in_hbm(weights), in_hbm(bias))
 
 
 def choose_slots(count_ref, splits_ref, job, row, table, put):

time: 147 us -> 146 us (level)
    unnamed x21 -> x19, local copies, waits for them, and re-layouts: 10.1 us -> 10.1 us
  transfers between devices with their start and end apart: 25 -> 25, of which waited for: 12 -> 12; matrix products, arithmetic and copies ran while one was open for 7% -> 6% of each run, Pallas kernels for 25% -> 25%
where the time goes in v6:
time: 146 us; the launch traced here: 145 us
  Pallas kernels  47.5 us (33%)
  waiting for transfers between devices  31.6 us (22%)
  starting transfers between devices  31.3 us (21%)
  blocking collectives  23.1 us (16%)
  local copies, waits for them, and re-layouts  10.2 us (7%)
    all_to_all x1, blocking collectives, over_half(): lax.all_to_all(x, 'seq', split_axis=0, concat_axis=0, tiled=False, axis_i...  23.1 us
    all_to_all x2, waiting for transfers between devices, over_seq(): return lax.all_to_all(x, 'seq', split_axis=0, concat_axis=0, tiled=False)  21.8 us
    pallas_call x2, Pallas kernels, qkv_half(): pl.pallas_call(functools.partial(qkv_kernel, pieces, bool(text)), out_sha...  18.4 us
    pallas_call x2, Pallas kernels, attend_pair(): pl.pallas_call(functools.partial(attention_kernel, far), out_shape=pltpu....  11.4 us
    unnamed x19, local copies, waits for them, and re-layouts  10.1 us
    pallas_call x4, Pallas kernels, out_call(): pl.pallas_call(kernel, out_shape=tuple((jax.ShapeDtypeStruct(shape, jnp.b...  8.85 us
    all_to_all x2, starting transfers between devices, over_seq(): return lax.all_to_all(x, 'seq', split_axis=0, concat_axis=0, tiled=False)  8.16 us
    ppermute x3, starting transfers between devices, to_device(): return lax.ppermute(x, ('job', 'seq'), perm)  7.25 us
  transfers between devices with their start and end apart: 25, of which 12 were waited for; matrix products, arithmetic and copies ran while one was open for 6% of the time, Pallas kernels for 25%

profile of v6, /device:TPU:0, one launch (start us, length us, event | category | flops | bytes accessed | tf_op | source)
XLA Modules:
  0.0 144.7 jit_solution(15465183612464272628)
XLA Ops:
  1.8 3.0 %collective-permute-start = (bf16[32,4096]{1,0:T(8,128)(2,1)S(1)}, bf16[32,4096]{1,0:T(8,128)(2,1)S(1)}, u32[]{:S(2)}, u32[]{:S(2)}) collective-permute-start(bf16[32,4096]{1,0:T(8,128)(2,1)S(1)} %shard_map.158.n0_ref), channel_id=1, source_target_pairs={{0,16},{8,24},{16,0},{24,8},{1,17},{9,25},{17,1},{25,9},{2,18},{10... | collective-permute-start | bytes 786440 | tf_op jit(solution)/shard_map/ppermute | solution.py:731
  4.8 1.4 collective-permute-start.9
  6.2 8.9 %copy.19 = bf16[3072,4,3,128]{3,0,1,2:T(8,128)(2,1)} copy(bf16[3072,4,3,128]{3,1,2,0:T(4,128)(2,1)} %param.26) | data formatting | bytes 18874368 | tf_op args[11]
  15.2 1.9 %collective-permute-start.1 = (bf16[128,3072]{1,0:T(8,128)(2,1)S(1)}, bf16[128,3072]{1,0:T(8,128)(2,1)S(1)}, u32[]{:S(2)}, u32[]{:S(2)}) collective-permute-start(bf16[128,3072]{1,0:T(8,128)(2,1)S(1)} %bitcast.11), channel_id=1, source_target_pairs={{0,16},{1,17},{2,18},{3,19},{12,28},{13,29},{14,30},{15,31},{16,0}... | collective-permute-start | bytes 2359304 | tf_op jit(solution)/shard_map/ppermute | solution.py:746
  20.0 4.9 %shard_map.159 = bf16[4,2,32,768]{3,2,1,0:T(8,128)(2,1)} custom-call(s32[4]{0:T(128)S(1)} %copy-done.7, bf16[32,4096]{1,0:T(8,128)(2,1)S(1)} %shard_map.158.n0_ref, bf16[32,4096]{1,0:T(8,128)(2,1)S(1)} %collective-permute-done.2.n1_ref, bf16[32,4096]{1,0:T(8,128)(2,1)S(1)} %collective-permute-done.n2_ref, ...), custom_call_target="tpu_custom_call" | custom-call | flops 805306368 | bytes 6291456 | tf_op jit(solution)/shard_map/pallas_call | solution.py:433
  24.9 3.5 %all-to-all-start = ((bf16[4,2,32,768]{3,2,1,0:T(8,128)(2,1)}), bf16[4,2,32,768]{3,2,1,0:T(8,128)(2,1)S(1)}, u32[]{:S(2)}, u32[]{:S(2)}) async-start(bf16[4,2,32,768]{3,2,1,0:T(8,128)(2,1)} %shard_map.159), calls=%async_computation | async-start | bytes 786432 | tf_op jit(solution)/shard_map/all_to_all | solution.py:779
  28.4 3.9 %collective-permute-start.10 = (bf16[128,3072]{1,0:T(8,128)(2,1)S(1)}, bf16[128,3072]{1,0:T(8,128)(2,1)S(1)}, u32[]{:S(2)}, u32[]{:S(2)}) collective-permute-start(bf16[128,3072]{1,0:T(8,128)(2,1)S(1)} %collective-permute-done.9.refs_0_), channel_id=1, source_target_pairs={{0,16},{1,17},{2,18},{3,19},{12,28},{13,29},{14,30},{15,31},{16,0}... | collective-permute-start | bytes 2359304 | tf_op jit(solution)/shard_map/ppermute | solution.py:746
  34.7 8.1 %shard_map.160 = bf16[4,256,384]{2,1,0:T(8,128)(2,1)} custom-call(bf16[128,3072]{1,0:T(8,128)(2,1)S(1)} %bitcast.13, bf16[128,3072]{1,0:T(8,128)(2,1)S(1)} %collective-permute-done.1.refs_1_, bf16[128,3072]{1,0:T(8,128)(2,1)} %collective-permute-done.4.refs_2_, bf16[32,3072]{1,0:T(8,128)(2,1)S(1)} %collective-permute-done.5.refs_3_, ...), custom_call_target="tpu_custom_call" | custom-call | flops 2415919104 | bytes 12582912 | tf_op jit(solution)/shard_map/pallas_call | solution.py:375
  43.1 3.8 %all-to-all-start.1 = ((bf16[4,256,384]{2,1,0:T(8,128)(2,1)}), bf16[4,256,384]{2,1,0:T(8,128)(2,1)S(1)}, u32[]{:S(2)}, u32[]{:S(2)}) async-start(bf16[4,256,384]{2,1,0:T(8,128)(2,1)} %shard_map.160), calls=%async_computation.1 | async-start | bytes 1572864 | tf_op jit(solution)/shard_map/all_to_all | solution.py:750
  49.3 10.2 %shard_map.161 = bf16[4,448,384]{2,1,0:T(8,128)(2,1)} custom-call(bf16[128,3072]{1,0:T(8,128)(2,1)S(1)} %collective-permute-done.9.refs_0_, bf16[128,3072]{1,0:T(8,128)(2,1)S(1)} %collective-permute-done.10.refs_1_, bf16[128,3072]{1,0:T(8,128)(2,1)} %collective-permute-done.11.refs_2_, bf16[64,3072]{1,0:T(8,128)(2,1)S(1)} %collective-permute-done.12.refs_3_, ...), custom_call_target="tpu_custom_call" | custom-call | flops 3623878656 | bytes 14155776 | tf_op jit(solution)/shard_map/pallas_call | solution.py:375
  59.6 23.1 %all_to_all.25.second_hbm = bf16[4,448,384]{2,1,0:T(8,128)(2,1)} all-to-all(bf16[4,448,384]{2,1,0:T(8,128)(2,1)} %shard_map.161), channel_id=1, replica_groups={{0,1,2,3},{4,5,6,7},{8,9,10,11},{12,13,14,15},{16,17,18,19},{20,21,22,2..., dimensions={0} | all-to-all | bytes 2752512 | tf_op jit(solution)/shard_map/all_to_all | solution.py:750
  82.7 5.5 %shard_map.162 = bf16[8,192,128]{2,1,0:T(8,128)(2,1)} custom-call(s32[4]{0:T(128)S(1)} %copy-done.8, s32[4,8]{1,0:T(4,128)S(1)} %copy-done.6, bf16[4,256,384]{2,1,0:T(8,128)(2,1)S(1)} %all-to-all-done.1.first_hbm, bf16[4,448,384]{2,1,0:T(8,128)(2,1)} %all_to_all.25.second_hbm), custom_call_target="tpu_custom_call" | custom-call | flops 838860800 | bytes 3145728 | tf_op jit(solution)/shard_map/pallas_call | solution.py:560
  88.3 3.7 %all-to-all-start.3 = ((bf16[8,192,128]{2,1,0:T(8,128)(2,1)}), bf16[8,192,128]{2,1,0:T(8,128)(2,1)S(1)}, u32[]{:S(2)}, u32[]{:S(2)}) async-start(bf16[8,192,128]{2,1,0:T(8,128)(2,1)} %shard_map.162), calls=%async_computation.3 | async-start | bytes 786432 | tf_op jit(solution)/shard_map/all_to_all | solution.py:734
  93.2 5.9 %shard_map.163 = bf16[8,384,128]{2,1,0:T(8,128)(2,1)} custom-call(s32[4]{0:T(128)S(1)} %copy-done.8, s32[4,8]{1,0:T(4,128)S(1)} %copy-done.6, bf16[4,256,384]{2,1,0:T(8,128)(2,1)S(1)} %copy-done.4, bf16[4,448,384]{2,1,0:T(8,128)(2,1)} %all_to_all.25.second_hbm), custom_call_target="tpu_custom_call" | custom-call | flops 838860800 | bytes 3145728 | tf_op jit(solution)/shard_map/pallas_call | solution.py:560
  99.0 4.5 %all-to-all-done.3.heads_ref = bf16[8,192,128]{2,1,0:T(8,128)(2,1)S(1)} async-done(((bf16[8,192,128]{2,1,0:T(8,128)(2,1)}), bf16[8,192,128]{2,1,0:T(8,128)(2,1)S(1)}, u32[]{:S(2)}, u32[]{:S(2)}) %all-to-all-start.3) | async-done | bytes 393248 | tf_op jit(solution)/shard_map/all_to_all | solution.py:734
  103.6 1.8 %shard_map.164 = bf16[192,3072]{1,0:T(8,128)(2,1)} custom-call(bf16[8,192,128]{2,1,0:T(8,128)(2,1)S(1)} %all-to-all-done.3.heads_ref, bf16[512,3072]{1,0:T(8,128)(2,1)S(1)} %bitcast.6), custom_call_target="tpu_custom_call" | custom-call | flops 603979776 | bytes 5505024 | tf_op jit(solution)/shard_map/pallas_call | solution.py:624
  105.4 4.4 %all-to-all-start.4 = ((bf16[8,384,128]{2,1,0:T(8,128)(2,1)}), bf16[8,384,128]{2,1,0:T(8,128)(2,1)}, u32[]{:S(2)}, u32[]{:S(2)}) async-start(bf16[8,384,128]{2,1,0:T(8,128)(2,1)} %shard_map.163), calls=%async_computation.4 | async-start | bytes 1572864 | tf_op jit(solution)/shard_map/all_to_all | solution.py:734
  109.8 3.1 %shard_map.165 = bf16[192,3072]{1,0:T(8,128)(2,1)} custom-call(bf16[8,192,128]{2,1,0:T(8,128)(2,1)S(1)} %all-to-all-done.3.heads_ref, bf16[512,3072]{1,0:T(8,128)(2,1)S(1)} %bitcast.7, bf16[192,3072]{1,0:T(8,128)(2,1)} %collective-permute-done.15.refs_0_), custom_call_target="tpu_custom_call" | custom-call | flops 603979776 | bytes 5505024 | tf_op jit(solution)/shard_map/pallas_call | solution.py:624
  113.5 17.2 %all-to-all-done.4.heads_ref = bf16[8,384,128]{2,1,0:T(8,128)(2,1)} async-done(((bf16[8,384,128]{2,1,0:T(8,128)(2,1)}), bf16[8,384,128]{2,1,0:T(8,128)(2,1)}, u32[]{:S(2)}, u32[]{:S(2)}) %all-to-all-start.4) | async-done | bytes 786464 | tf_op jit(solution)/shard_map/all_to_all | solution.py:734
  130.7 2.0 %shard_map.166 = (bf16[64,3072]{1,0:T(8,128)(2,1)S(1)}, bf16[64,3072]{1,0:T(8,128)(2,1)S(1)}, bf16[64,3072]{1,0:T(8,128)(2,1)S(1)}, bf16[64,1536]{1,0:T(8,128)(2,1)S(1)}) custom-call(bf16[8,384,128]{2,1,0:T(8,128)(2,1)} %all-to-all-done.4.heads_ref, bf16[512,3072]{1,0:T(8,128)(2,1)S(1)} %bitcast.8), custom_call_target="tpu_custom_call" | custom-call | flops 603979776 | bytes 5505024 | tf_op jit(solution)/shard_map/pallas_call | solution.py:624
  133.8 2.1 %collective-permute-done.19.refs_3_ = bf16[64,1536]{1,0:T(8,128)(2,1)S(1)} collective-permute-done((bf16[64,1536]{1,0:T(8,128)(2,1)S(1)}, bf16[64,1536]{1,0:T(8,128)(2,1)S(1)}, u32[]{:S(2)}, u32[]{:S(2)}) %collective-permute-start.19) | collective-permute-done | bytes 196640 | tf_op jit(solution)/shard_map/ppermute | solution.py:728
  135.9 2.0 %shard_map.167 = (bf16[192,3072]{1,0:T(8,128)(2,1)S(1)}, bf16[64,3072]{1,0:T(8,128)(2,1)S(1)}) custom-call(bf16[8,384,128]{2,1,0:T(8,128)(2,1)} %all-to-all-done.4.heads_ref, bf16[512,3072]{1,0:T(8,128)(2,1)S(1)} %bitcast.9, bf16[64,3072]{1,0:T(8,128)(2,1)S(1)} %collective-permute-done.16.refs_0_, bf16[64,3072]{1,0:T(8,128)(2,1)S(1)} %collective-permute-done.17.refs_1_, ...), custom_call_target="tpu_custom_call" | custom-call | flops 603979776 | bytes 5505024 | tf_op jit(solution)/shard_map/pallas_call | solution.py:624
  137.9 3.7 %collective-permute-done.20.chip_hbm = bf16[192,3072]{1,0:T(8,128)(2,1)} collective-permute-done((bf16[192,3072]{1,0:T(8,128)(2,1)}, bf16[192,3072]{1,0:T(8,128)(2,1)}, u32[]{:S(2)}, u32[]{:S(2)}) %collective-permute-start.20) | collective-permute-done | bytes 1179680 | tf_op jit(solution)/shard_map/ppermute | solution.py:731
  141.6 2.9 %shard_map.168 = (bf16[1,128,3072]{2,1,0:T(8,128)(2,1)}, bf16[1,64,3072]{2,1,0:T(8,128)(2,1)}) custom-call(s32[4]{0:T(128)S(1)} %copy-done.8, s32[4,8]{1,0:T(4,128)S(1)} %copy-done.6, bf16[1,128,3072]{2,1,0:T(8,128)(2,1)S(1)} %copy-done.2, bf16[192,3072]{1,0:T(8,128)(2,1)S(1)} %get-tuple-element.40.part_ref, ...), custom_call_target="tpu_custom_call" | custom-call | flops 3538944 | bytes 5898240 | tf_op jit(solution)/shard_map/pallas_call | solution.py:683
  (59 shorter events, 11.9 us)
Async XLA Ops:
  1.8 13.4 %collective-permute-start = (bf16[32,4096]{1,0:T(8,128)(2,1)S(1)}, bf16[32,4096]{1,0:T(8,128)(2,1)S(1)}, u32[]{:S(2)}, u32[]{:S(2)}) collective-permute-start(bf16[32,4096]{1,0:T(8,128)(2,1)S(1)} %shard_map.158.n0_ref), channel_id=1, source_target_pairs={{0,16},{8,24},{16,0},{24,8},{1,17},{9,25},{17,1},{25,9},{2,18},{10... | collective-permute-start | bytes 786440 | tf_op jit(solution)/shard_map/ppermute | solution.py:731
  4.8 23.6 %collective-permute-start.9 = (bf16[128,3072]{1,0:T(8,128)(2,1)}, bf16[128,3072]{1,0:T(8,128)(2,1)S(1)}, u32[]{:S(2)}, u32[]{:S(2)}) collective-permute-start(bf16[128,3072]{1,0:T(8,128)(2,1)} %bitcast.10), channel_id=1, source_target_pairs={{4,0},{5,1},{6,2},{7,3},{8,12},{9,13},{10,14},{11,15},{20,16},{21,... | collective-permute-start | bytes 2359304 | tf_op jit(solution)/shard_map/ppermute | solution.py:746
  15.2 17.1 %collective-permute-start.1 = (bf16[128,3072]{1,0:T(8,128)(2,1)S(1)}, bf16[128,3072]{1,0:T(8,128)(2,1)S(1)}, u32[]{:S(2)}, u32[]{:S(2)}) collective-permute-start(bf16[128,3072]{1,0:T(8,128)(2,1)S(1)} %bitcast.11), channel_id=1, source_target_pairs={{0,16},{1,17},{2,18},{3,19},{12,28},{13,29},{14,30},{15,31},{16,0}... | collective-permute-start | bytes 2359304 | tf_op jit(solution)/shard_map/ppermute | solution.py:746
  17.1 2.5 %collective-permute-start.2 = (bf16[32,4096]{1,0:T(8,128)(2,1)S(1)}, bf16[32,4096]{1,0:T(8,128)(2,1)S(1)}, u32[]{:S(2)}, u32[]{:S(2)}) collective-permute-start(bf16[32,4096]{1,0:T(8,128)(2,1)S(1)} %shard_map.158.n0_ref), channel_id=1, source_target_pairs={{0,8},{8,0},{16,24},{24,16},{1,9},{9,1},{17,25},{25,17},{2,10},{10... | collective-permute-start | bytes 786440 | tf_op jit(solution)/shard_map/ppermute | solution.py:728
  18.5 1.5 %collective-permute-start.3 = (bf16[32,4096]{1,0:T(8,128)(2,1)S(1)}, bf16[32,4096]{1,0:T(8,128)(2,1)S(1)}, u32[]{:S(2)}, u32[]{:S(2)}) collective-permute-start(bf16[32,4096]{1,0:T(8,128)(2,1)S(1)} %collective-permute-done.n2_ref), channel_id=1, source_target_pairs={{0,8},{8,0},{16,24},{24,16},{1,9},{9,1},{17,25},{25,17},{2,10},{10... | collective-permute-start | bytes 786440 | tf_op jit(solution)/shard_map/ppermute | solution.py:728
  18.6 14.5 %collective-permute-start.4 = (bf16[128,3072]{1,0:T(8,128)(2,1)S(1)}, bf16[128,3072]{1,0:T(8,128)(2,1)}, u32[]{:S(2)}, u32[]{:S(2)}) collective-permute-start(bf16[128,3072]{1,0:T(8,128)(2,1)S(1)} %bitcast.12), channel_id=1, source_target_pairs={{0,8},{8,0},{16,24},{24,16},{1,9},{9,1},{17,25},{25,17},{2,10},{10... | collective-permute-start | bytes 2359304 | tf_op jit(solution)/shard_map/ppermute | solution.py:728
  24.9 18.0 %all-to-all-start = ((bf16[4,2,32,768]{3,2,1,0:T(8,128)(2,1)}), bf16[4,2,32,768]{3,2,1,0:T(8,128)(2,1)S(1)}, u32[]{:S(2)}, u32[]{:S(2)}) async-start(bf16[4,2,32,768]{3,2,1,0:T(8,128)(2,1)} %shard_map.159), calls=%async_computation | async-start | bytes 786432 | tf_op jit(solution)/shard_map/all_to_all | solution.py:779
  28.4 18.5 %collective-permute-start.10 = (bf16[128,3072]{1,0:T(8,128)(2,1)S(1)}, bf16[128,3072]{1,0:T(8,128)(2,1)S(1)}, u32[]{:S(2)}, u32[]{:S(2)}) collective-permute-start(bf16[128,3072]{1,0:T(8,128)(2,1)S(1)} %collective-permute-done.9.refs_0_), channel_id=1, source_target_pairs={{0,16},{1,17},{2,18},{3,19},{12,28},{13,29},{14,30},{15,31},{16,0}... | collective-permute-start | bytes 2359304 | tf_op jit(solution)/shard_map/ppermute | solution.py:746
  32.4 1.5 %collective-permute-start.8 = (bf16[32,3072]{1,0:T(8,128)(2,1)S(1)}, bf16[32,3072]{1,0:T(8,128)(2,1)S(1)}, u32[]{:S(2)}, u32[]{:S(2)}) collective-permute-start(bf16[32,3072]{1,0:T(8,128)(2,1)S(1)} %get-tuple-element.44), channel_id=1, source_target_pairs={{0,8},{8,0},{16,24},{24,16},{1,9},{9,1},{17,25},{25,17},{2,10},{10... | collective-permute-start | bytes 589832 | tf_op jit(solution)/shard_map/ppermute | solution.py:728
  32.4 1.7 %collective-permute-start.7 = (bf16[32,3072]{1,0:T(8,128)(2,1)S(1)}, bf16[32,3072]{1,0:T(8,128)(2,1)S(1)}, u32[]{:S(2)}, u32[]{:S(2)}) collective-permute-start(bf16[32,3072]{1,0:T(8,128)(2,1)S(1)} %get-tuple-element.45), channel_id=1, source_target_pairs={{0,8},{8,0},{16,24},{24,16},{1,9},{9,1},{17,25},{25,17},{2,10},{10... | collective-permute-start | bytes 589832 | tf_op jit(solution)/shard_map/ppermute | solution.py:728
  33.0 1.7 %collective-permute-start.5 = (bf16[32,3072]{1,0:T(8,128)(2,1)S(1)}, bf16[32,3072]{1,0:T(8,128)(2,1)S(1)}, u32[]{:S(2)}, u32[]{:S(2)}) collective-permute-start(bf16[32,3072]{1,0:T(8,128)(2,1)S(1)} %get-tuple-element.47), channel_id=1, source_target_pairs={{0,8},{8,0},{16,24},{24,16},{1,9},{9,1},{17,25},{25,17},{2,10},{10... | collective-permute-start | bytes 589832 | tf_op jit(solution)/shard_map/ppermute | solution.py:728
  33.9 13.7 %collective-permute-start.11 = (bf16[128,3072]{1,0:T(8,128)(2,1)S(1)}, bf16[128,3072]{1,0:T(8,128)(2,1)}, u32[]{:S(2)}, u32[]{:S(2)}) collective-permute-start(bf16[128,3072]{1,0:T(8,128)(2,1)S(1)} %collective-permute-done.9.refs_0_), channel_id=1, source_target_pairs={{0,8},{8,0},{16,24},{24,16},{1,9},{9,1},{17,25},{25,17},{2,10},{10... | collective-permute-start | bytes 2359304 | tf_op jit(solution)/shard_map/ppermute | solution.py:728
  42.9 4.7 %collective-permute-start.14 = (bf16[4,2,32,768]{3,2,1,0:T(8,128)(2,1)S(1)}, bf16[4,2,32,768]{3,2,1,0:T(8,128)(2,1)S(1)}, u32[]{:S(2)}, u32[]{:S(2)}) collective-permute-start(bf16[4,2,32,768]{3,2,1,0:T(8,128)(2,1)S(1)} %all-to-all-done.refs_5_), channel_id=1, source_target_pairs={{0,8},{8,0},{16,24},{24,16},{1,9},{9,1},{17,25},{25,17},{2,10},{10... | collective-permute-start | bytes 1179656 | tf_op jit(solution)/shard_map/ppermute | solution.py:728
  43.1 16.5 %all-to-all-start.1 = ((bf16[4,256,384]{2,1,0:T(8,128)(2,1)}), bf16[4,256,384]{2,1,0:T(8,128)(2,1)S(1)}, u32[]{:S(2)}, u32[]{:S(2)}) async-start(bf16[4,256,384]{2,1,0:T(8,128)(2,1)} %shard_map.160), calls=%async_computation.1 | async-start | bytes 1572864 | tf_op jit(solution)/shard_map/all_to_all | solution.py:750
  47.0 1.8 %collective-permute-start.13 = (bf16[64,3072]{1,0:T(8,128)(2,1)S(1)}, bf16[64,3072]{1,0:T(8,128)(2,1)S(1)}, u32[]{:S(2)}, u32[]{:S(2)}) collective-permute-start(bf16[64,3072]{1,0:T(8,128)(2,1)S(1)} %get-tuple-element.42), channel_id=1, source_target_pairs={{0,8},{8,0},{16,24},{24,16},{1,9},{9,1},{17,25},{25,17},{2,10},{10... | collective-permute-start | bytes 1179656 | tf_op jit(solution)/shard_map/ppermute | solution.py:728
  47.1 2.3 %collective-permute-start.12 = (bf16[64,3072]{1,0:T(8,128)(2,1)S(1)}, bf16[64,3072]{1,0:T(8,128)(2,1)S(1)}, u32[]{:S(2)}, u32[]{:S(2)}) collective-permute-start(bf16[64,3072]{1,0:T(8,128)(2,1)S(1)} %get-tuple-element.43), channel_id=1, source_target_pairs={{0,8},{8,0},{16,24},{24,16},{1,9},{9,1},{17,25},{25,17},{2,10},{10... | collective-permute-start | bytes 1179656 | tf_op jit(solution)/shard_map/ppermute | solution.py:728
  88.3 15.3 %all-to-all-start.3 = ((bf16[8,192,128]{2,1,0:T(8,128)(2,1)}), bf16[8,192,128]{2,1,0:T(8,128)(2,1)S(1)}, u32[]{:S(2)}, u32[]{:S(2)}) async-start(bf16[8,192,128]{2,1,0:T(8,128)(2,1)} %shard_map.162), calls=%async_computation.3 | async-start | bytes 786432 | tf_op jit(solution)/shard_map/all_to_all | solution.py:734
  105.4 4.4 %collective-permute-start.15 = (bf16[192,3072]{1,0:T(8,128)(2,1)}, bf16[192,3072]{1,0:T(8,128)(2,1)}, u32[]{:S(2)}, u32[]{:S(2)}) collective-permute-start(bf16[192,3072]{1,0:T(8,128)(2,1)} %shard_map.164), channel_id=1, source_target_pairs={{0,8},{8,0},{16,24},{24,16},{1,9},{9,1},{17,25},{25,17},{2,10},{10... | collective-permute-start | bytes 3538952 | tf_op jit(solution)/shard_map/ppermute | solution.py:728
  105.4 25.3 %all-to-all-start.4 = ((bf16[8,384,128]{2,1,0:T(8,128)(2,1)}), bf16[8,384,128]{2,1,0:T(8,128)(2,1)}, u32[]{:S(2)}, u32[]{:S(2)}) async-start(bf16[8,384,128]{2,1,0:T(8,128)(2,1)} %shard_map.163), calls=%async_computation.4 | async-start | bytes 1572864 | tf_op jit(solution)/shard_map/all_to_all | solution.py:734
  112.9 28.7 %collective-permute-start.20 = (bf16[192,3072]{1,0:T(8,128)(2,1)}, bf16[192,3072]{1,0:T(8,128)(2,1)}, u32[]{:S(2)}, u32[]{:S(2)}) collective-permute-start(bf16[192,3072]{1,0:T(8,128)(2,1)} %shard_map.165), channel_id=1, source_target_pairs={{0,16},{8,24},{16,0},{24,8},{1,17},{9,25},{17,1},{25,9},{2,18},{10... | collective-permute-start | bytes 3538952 | tf_op jit(solution)/shard_map/ppermute | solution.py:731
  132.7 3.2 %collective-permute-start.16 = (bf16[64,3072]{1,0:T(8,128)(2,1)S(1)}, bf16[64,3072]{1,0:T(8,128)(2,1)S(1)}, u32[]{:S(2)}, u32[]{:S(2)}) collective-permute-start(bf16[64,3072]{1,0:T(8,128)(2,1)S(1)} %get-tuple-element.36), channel_id=1, source_target_pairs={{0,8},{8,0},{16,24},{24,16},{1,9},{9,1},{17,25},{25,17},{2,10},{10... | collective-permute-start | bytes 1179656 | tf_op jit(solution)/shard_map/ppermute | solution.py:728
  132.7 3.1 %collective-permute-start.17 = (bf16[64,3072]{1,0:T(8,128)(2,1)S(1)}, bf16[64,3072]{1,0:T(8,128)(2,1)S(1)}, u32[]{:S(2)}, u32[]{:S(2)}) collective-permute-start(bf16[64,3072]{1,0:T(8,128)(2,1)S(1)} %get-tuple-element.37), channel_id=1, source_target_pairs={{0,8},{8,0},{16,24},{24,16},{1,9},{9,1},{17,25},{25,17},{2,10},{10... | collective-permute-start | bytes 1179656 | tf_op jit(solution)/shard_map/ppermute | solution.py:728
  133.2 2.6 %collective-permute-start.18 = (bf16[64,3072]{1,0:T(8,128)(2,1)S(1)}, bf16[64,3072]{1,0:T(8,128)(2,1)S(1)}, u32[]{:S(2)}, u32[]{:S(2)}) collective-permute-start(bf16[64,3072]{1,0:T(8,128)(2,1)S(1)} %get-tuple-element.38), channel_id=1, source_target_pairs={{0,8},{8,0},{16,24},{24,16},{1,9},{9,1},{17,25},{25,17},{2,10},{10... | collective-permute-start | bytes 1179656 | tf_op jit(solution)/shard_map/ppermute | solution.py:728
  133.3 2.5 %collective-permute-start.19 = (bf16[64,1536]{1,0:T(8,128)(2,1)S(1)}, bf16[64,1536]{1,0:T(8,128)(2,1)S(1)}, u32[]{:S(2)}, u32[]{:S(2)}) collective-permute-start(bf16[64,1536]{1,0:T(8,128)(2,1)S(1)} %get-tuple-element.39), channel_id=1, source_target_pairs={{0,8},{8,0},{16,24},{24,16},{1,9},{9,1},{17,25},{25,17},{2,10},{10... | collective-permute-start | bytes 589832 | tf_op jit(solution)/shard_map/ppermute | solution.py:728
  (10 other events, 129.5 us)

commit v7 on v6

--- a/solution.py
+++ b/solution.py
@@ -450,11 +450,15 @@
     shards = splits_ref.shape[1]
     slot = lax.broadcasted_iota(jnp.int32, (2 * row.shape[1] // shards, row.shape[1]), 0)
     offset = jnp.int32(0)
+    picks = []
     for s in range(shards):
         chosen = (row == slot + offset) & (slot < splits_ref[job, s]) & (row < count_ref[job])
-        chosen = jnp.where(chosen, 1.0, 0.0).astype(jnp.bfloat16)
-        put(s, jnp.dot(chosen, table, preferred_element_type=jnp.float32).astype(jnp.bfloat16))
+        picks.append(jnp.where(chosen, 1.0, 0.0).astype(jnp.bfloat16))
         offset = offset + splits_ref[job, s]
+    picked = jnp.dot(jnp.concatenate(picks, axis=0), table, preferred_element_type=jnp.float32)
+    picked = picked.astype(jnp.bfloat16)
+    for s in range(shards):
+        put(s, picked[s * slot.shape[0] : (s + 1) * slot.shape[0]])
 
 
 def attention_kernel(far, count_ref, splits_ref, first_hbm, second_hbm, *refs):

time: 146 us -> 146 us (level)
  no operation moved by 1% of the time
where the time goes in v7:
time: 146 us; the launch traced here: 145 us
  Pallas kernels  47.5 us (33%)
  waiting for transfers between devices  31.6 us (22%)
  starting transfers between devices  31.3 us (21%)
  blocking collectives  23.1 us (16%)
  local copies, waits for them, and re-layouts  10.2 us (7%)
    all_to_all x1, blocking collectives, over_half(): lax.all_to_all(x, 'seq', split_axis=0, concat_axis=0, tiled=False, axis_i...  23.1 us
    all_to_all x2, waiting for transfers between devices, over_seq(): return lax.all_to_all(x, 'seq', split_axis=0, concat_axis=0, tiled=False)  21.8 us
    pallas_call x2, Pallas kernels, qkv_half(): pl.pallas_call(functools.partial(qkv_kernel, pieces, bool(text)), out_sha...  18.4 us
    pallas_call x2, Pallas kernels, attend_pair(): pl.pallas_call(functools.partial(attention_kernel, far), out_shape=pltpu....  11.4 us
    unnamed x19, local copies, waits for them, and re-layouts  10.1 us
    pallas_call x4, Pallas kernels, out_call(): pl.pallas_call(kernel, out_shape=tuple((jax.ShapeDtypeStruct(shape, jnp.b...  8.85 us
    all_to_all x2, starting transfers between devices, over_seq(): return lax.all_to_all(x, 'seq', split_axis=0, concat_axis=0, tiled=False)  8.16 us
    ppermute x3, starting transfers between devices, to_device(): return lax.ppermute(x, ('job', 'seq'), perm)  7.25 us
  transfers between devices with their start and end apart: 25, of which 12 were waited for; matrix products, arithmetic and copies ran while one was open for 6% of the time, Pallas kernels for 25%

profile of v7, /device:TPU:0, one launch (start us, length us, event | category | flops | bytes accessed | tf_op | source)
XLA Modules:
  0.0 144.7 jit_solution(11785253196079756807)
XLA Ops:
  1.8 3.0 %collective-permute-start = (bf16[32,4096]{1,0:T(8,128)(2,1)S(1)}, bf16[32,4096]{1,0:T(8,128)(2,1)S(1)}, u32[]{:S(2)}, u32[]{:S(2)}) collective-permute-start(bf16[32,4096]{1,0:T(8,128)(2,1)S(1)} %shard_map.158.n0_ref), channel_id=1, source_target_pairs={{0,16},{8,24},{16,0},{24,8},{1,17},{9,25},{17,1},{25,9},{2,18},{10... | collective-permute-start | bytes 786440 | tf_op jit(solution)/shard_map/ppermute | solution.py:735
  4.8 1.4 collective-permute-start.9
  6.2 8.9 %copy.19 = bf16[3072,4,3,128]{3,0,1,2:T(8,128)(2,1)} copy(bf16[3072,4,3,128]{3,1,2,0:T(4,128)(2,1)} %param.26) | data formatting | bytes 18874368 | tf_op args[11]
  15.2 1.9 %collective-permute-start.1 = (bf16[128,3072]{1,0:T(8,128)(2,1)S(1)}, bf16[128,3072]{1,0:T(8,128)(2,1)S(1)}, u32[]{:S(2)}, u32[]{:S(2)}) collective-permute-start(bf16[128,3072]{1,0:T(8,128)(2,1)S(1)} %bitcast.11), channel_id=1, source_target_pairs={{0,16},{1,17},{2,18},{3,19},{12,28},{13,29},{14,30},{15,31},{16,0}... | collective-permute-start | bytes 2359304 | tf_op jit(solution)/shard_map/ppermute | solution.py:750
  20.0 4.9 %shard_map.159 = bf16[4,2,32,768]{3,2,1,0:T(8,128)(2,1)} custom-call(s32[4]{0:T(128)S(1)} %copy-done.7, bf16[32,4096]{1,0:T(8,128)(2,1)S(1)} %shard_map.158.n0_ref, bf16[32,4096]{1,0:T(8,128)(2,1)S(1)} %collective-permute-done.2.n1_ref, bf16[32,4096]{1,0:T(8,128)(2,1)S(1)} %collective-permute-done.n2_ref, ...), custom_call_target="tpu_custom_call" | custom-call | flops 805306368 | bytes 6291456 | tf_op jit(solution)/shard_map/pallas_call | solution.py:433
  24.9 3.5 %all-to-all-start = ((bf16[4,2,32,768]{3,2,1,0:T(8,128)(2,1)}), bf16[4,2,32,768]{3,2,1,0:T(8,128)(2,1)S(1)}, u32[]{:S(2)}, u32[]{:S(2)}) async-start(bf16[4,2,32,768]{3,2,1,0:T(8,128)(2,1)} %shard_map.159), calls=%async_computation | async-start | bytes 786432 | tf_op jit(solution)/shard_map/all_to_all | solution.py:783
  28.4 3.9 %collective-permute-start.10 = (bf16[128,3072]{1,0:T(8,128)(2,1)S(1)}, bf16[128,3072]{1,0:T(8,128)(2,1)S(1)}, u32[]{:S(2)}, u32[]{:S(2)}) collective-permute-start(bf16[128,3072]{1,0:T(8,128)(2,1)S(1)} %collective-permute-done.9.refs_0_), channel_id=1, source_target_pairs={{0,16},{1,17},{2,18},{3,19},{12,28},{13,29},{14,30},{15,31},{16,0}... | collective-permute-start | bytes 2359304 | tf_op jit(solution)/shard_map/ppermute | solution.py:750
  34.7 8.1 %shard_map.160 = bf16[4,256,384]{2,1,0:T(8,128)(2,1)} custom-call(bf16[128,3072]{1,0:T(8,128)(2,1)S(1)} %bitcast.13, bf16[128,3072]{1,0:T(8,128)(2,1)S(1)} %collective-permute-done.1.refs_1_, bf16[128,3072]{1,0:T(8,128)(2,1)} %collective-permute-done.4.refs_2_, bf16[32,3072]{1,0:T(8,128)(2,1)S(1)} %collective-permute-done.5.refs_3_, ...), custom_call_target="tpu_custom_call" | custom-call | flops 2415919104 | bytes 12582912 | tf_op jit(solution)/shard_map/pallas_call | solution.py:375
  43.1 3.8 %all-to-all-start.1 = ((bf16[4,256,384]{2,1,0:T(8,128)(2,1)}), bf16[4,256,384]{2,1,0:T(8,128)(2,1)S(1)}, u32[]{:S(2)}, u32[]{:S(2)}) async-start(bf16[4,256,384]{2,1,0:T(8,128)(2,1)} %shard_map.160), calls=%async_computation.1 | async-start | bytes 1572864 | tf_op jit(solution)/shard_map/all_to_all | solution.py:754
  49.3 10.2 %shard_map.161 = bf16[4,448,384]{2,1,0:T(8,128)(2,1)} custom-call(bf16[128,3072]{1,0:T(8,128)(2,1)S(1)} %collective-permute-done.9.refs_0_, bf16[128,3072]{1,0:T(8,128)(2,1)S(1)} %collective-permute-done.10.refs_1_, bf16[128,3072]{1,0:T(8,128)(2,1)} %collective-permute-done.11.refs_2_, bf16[64,3072]{1,0:T(8,128)(2,1)S(1)} %collective-permute-done.12.refs_3_, ...), custom_call_target="tpu_custom_call" | custom-call | flops 3623878656 | bytes 14155776 | tf_op jit(solution)/shard_map/pallas_call | solution.py:375
  59.6 23.1 %all_to_all.25.second_hbm = bf16[4,448,384]{2,1,0:T(8,128)(2,1)} all-to-all(bf16[4,448,384]{2,1,0:T(8,128)(2,1)} %shard_map.161), channel_id=1, replica_groups={{0,1,2,3},{4,5,6,7},{8,9,10,11},{12,13,14,15},{16,17,18,19},{20,21,22,2..., dimensions={0} | all-to-all | bytes 2752512 | tf_op jit(solution)/shard_map/all_to_all | solution.py:754
  82.7 5.6 %shard_map.162 = bf16[8,192,128]{2,1,0:T(8,128)(2,1)} custom-call(s32[4]{0:T(128)S(1)} %copy-done.8, s32[4,8]{1,0:T(4,128)S(1)} %copy-done.6, bf16[4,256,384]{2,1,0:T(8,128)(2,1)S(1)} %all-to-all-done.1.first_hbm, bf16[4,448,384]{2,1,0:T(8,128)(2,1)} %all_to_all.25.second_hbm), custom_call_target="tpu_custom_call" | custom-call | flops 838860800 | bytes 3145728 | tf_op jit(solution)/shard_map/pallas_call | solution.py:564
  88.3 3.7 %all-to-all-start.3 = ((bf16[8,192,128]{2,1,0:T(8,128)(2,1)}), bf16[8,192,128]{2,1,0:T(8,128)(2,1)S(1)}, u32[]{:S(2)}, u32[]{:S(2)}) async-start(bf16[8,192,128]{2,1,0:T(8,128)(2,1)} %shard_map.162), calls=%async_computation.3 | async-start | bytes 786432 | tf_op jit(solution)/shard_map/all_to_all | solution.py:738
  93.2 5.8 %shard_map.163 = bf16[8,384,128]{2,1,0:T(8,128)(2,1)} custom-call(s32[4]{0:T(128)S(1)} %copy-done.8, s32[4,8]{1,0:T(4,128)S(1)} %copy-done.6, bf16[4,256,384]{2,1,0:T(8,128)(2,1)S(1)} %copy-done.4, bf16[4,448,384]{2,1,0:T(8,128)(2,1)} %all_to_all.25.second_hbm), custom_call_target="tpu_custom_call" | custom-call | flops 838860800 | bytes 3145728 | tf_op jit(solution)/shard_map/pallas_call | solution.py:564
  99.0 4.6 %all-to-all-done.3.heads_ref = bf16[8,192,128]{2,1,0:T(8,128)(2,1)S(1)} async-done(((bf16[8,192,128]{2,1,0:T(8,128)(2,1)}), bf16[8,192,128]{2,1,0:T(8,128)(2,1)S(1)}, u32[]{:S(2)}, u32[]{:S(2)}) %all-to-all-start.3) | async-done | bytes 393248 | tf_op jit(solution)/shard_map/all_to_all | solution.py:738
  103.6 1.8 %shard_map.164 = bf16[192,3072]{1,0:T(8,128)(2,1)} custom-call(bf16[8,192,128]{2,1,0:T(8,128)(2,1)S(1)} %all-to-all-done.3.heads_ref, bf16[512,3072]{1,0:T(8,128)(2,1)S(1)} %bitcast.6), custom_call_target="tpu_custom_call" | custom-call | flops 603979776 | bytes 5505024 | tf_op jit(solution)/shard_map/pallas_call | solution.py:628
  105.4 4.4 %all-to-all-start.4 = ((bf16[8,384,128]{2,1,0:T(8,128)(2,1)}), bf16[8,384,128]{2,1,0:T(8,128)(2,1)}, u32[]{:S(2)}, u32[]{:S(2)}) async-start(bf16[8,384,128]{2,1,0:T(8,128)(2,1)} %shard_map.163), calls=%async_computation.4 | async-start | bytes 1572864 | tf_op jit(solution)/shard_map/all_to_all | solution.py:738
  109.9 3.1 %shard_map.165 = bf16[192,3072]{1,0:T(8,128)(2,1)} custom-call(bf16[8,192,128]{2,1,0:T(8,128)(2,1)S(1)} %all-to-all-done.3.heads_ref, bf16[512,3072]{1,0:T(8,128)(2,1)S(1)} %bitcast.7, bf16[192,3072]{1,0:T(8,128)(2,1)} %collective-permute-done.15.refs_0_), custom_call_target="tpu_custom_call" | custom-call | flops 603979776 | bytes 5505024 | tf_op jit(solution)/shard_map/pallas_call | solution.py:628
  113.5 17.2 %all-to-all-done.4.heads_ref = bf16[8,384,128]{2,1,0:T(8,128)(2,1)} async-done(((bf16[8,384,128]{2,1,0:T(8,128)(2,1)}), bf16[8,384,128]{2,1,0:T(8,128)(2,1)}, u32[]{:S(2)}, u32[]{:S(2)}) %all-to-all-start.4) | async-done | bytes 786464 | tf_op jit(solution)/shard_map/all_to_all | solution.py:738
  130.7 2.0 %shard_map.166 = (bf16[64,3072]{1,0:T(8,128)(2,1)S(1)}, bf16[64,3072]{1,0:T(8,128)(2,1)S(1)}, bf16[64,3072]{1,0:T(8,128)(2,1)S(1)}, bf16[64,1536]{1,0:T(8,128)(2,1)S(1)}) custom-call(bf16[8,384,128]{2,1,0:T(8,128)(2,1)} %all-to-all-done.4.heads_ref, bf16[512,3072]{1,0:T(8,128)(2,1)S(1)} %bitcast.8), custom_call_target="tpu_custom_call" | custom-call | flops 603979776 | bytes 5505024 | tf_op jit(solution)/shard_map/pallas_call | solution.py:628
  133.8 2.1 %collective-permute-done.19.refs_3_ = bf16[64,1536]{1,0:T(8,128)(2,1)S(1)} collective-permute-done((bf16[64,1536]{1,0:T(8,128)(2,1)S(1)}, bf16[64,1536]{1,0:T(8,128)(2,1)S(1)}, u32[]{:S(2)}, u32[]{:S(2)}) %collective-permute-start.19) | collective-permute-done | bytes 196640 | tf_op jit(solution)/shard_map/ppermute | solution.py:732
  135.9 2.0 %shard_map.167 = (bf16[192,3072]{1,0:T(8,128)(2,1)S(1)}, bf16[64,3072]{1,0:T(8,128)(2,1)S(1)}) custom-call(bf16[8,384,128]{2,1,0:T(8,128)(2,1)} %all-to-all-done.4.heads_ref, bf16[512,3072]{1,0:T(8,128)(2,1)S(1)} %bitcast.9, bf16[64,3072]{1,0:T(8,128)(2,1)S(1)} %collective-permute-done.16.refs_0_, bf16[64,3072]{1,0:T(8,128)(2,1)S(1)} %collective-permute-done.17.refs_1_, ...), custom_call_target="tpu_custom_call" | custom-call | flops 603979776 | bytes 5505024 | tf_op jit(solution)/shard_map/pallas_call | solution.py:628
  137.9 3.7 %collective-permute-done.20.chip_hbm = bf16[192,3072]{1,0:T(8,128)(2,1)} collective-permute-done((bf16[192,3072]{1,0:T(8,128)(2,1)}, bf16[192,3072]{1,0:T(8,128)(2,1)}, u32[]{:S(2)}, u32[]{:S(2)}) %collective-permute-start.20) | collective-permute-done | bytes 1179680 | tf_op jit(solution)/shard_map/ppermute | solution.py:735
  141.7 2.9 %shard_map.168 = (bf16[1,128,3072]{2,1,0:T(8,128)(2,1)}, bf16[1,64,3072]{2,1,0:T(8,128)(2,1)}) custom-call(s32[4]{0:T(128)S(1)} %copy-done.8, s32[4,8]{1,0:T(4,128)S(1)} %copy-done.6, bf16[1,128,3072]{2,1,0:T(8,128)(2,1)S(1)} %copy-done.2, bf16[192,3072]{1,0:T(8,128)(2,1)S(1)} %get-tuple-element.40.part_ref, ...), custom_call_target="tpu_custom_call" | custom-call | flops 3538944 | bytes 5898240 | tf_op jit(solution)/shard_map/pallas_call | solution.py:687
  (59 shorter events, 11.9 us)
Async XLA Ops:
  1.8 13.4 %collective-permute-start = (bf16[32,4096]{1,0:T(8,128)(2,1)S(1)}, bf16[32,4096]{1,0:T(8,128)(2,1)S(1)}, u32[]{:S(2)}, u32[]{:S(2)}) collective-permute-start(bf16[32,4096]{1,0:T(8,128)(2,1)S(1)} %shard_map.158.n0_ref), channel_id=1, source_target_pairs={{0,16},{8,24},{16,0},{24,8},{1,17},{9,25},{17,1},{25,9},{2,18},{10... | collective-permute-start | bytes 786440 | tf_op jit(solution)/shard_map/ppermute | solution.py:735
  4.8 23.6 %collective-permute-start.9 = (bf16[128,3072]{1,0:T(8,128)(2,1)}, bf16[128,3072]{1,0:T(8,128)(2,1)S(1)}, u32[]{:S(2)}, u32[]{:S(2)}) collective-permute-start(bf16[128,3072]{1,0:T(8,128)(2,1)} %bitcast.10), channel_id=1, source_target_pairs={{4,0},{5,1},{6,2},{7,3},{8,12},{9,13},{10,14},{11,15},{20,16},{21,... | collective-permute-start | bytes 2359304 | tf_op jit(solution)/shard_map/ppermute | solution.py:750
  15.2 17.1 %collective-permute-start.1 = (bf16[128,3072]{1,0:T(8,128)(2,1)S(1)}, bf16[128,3072]{1,0:T(8,128)(2,1)S(1)}, u32[]{:S(2)}, u32[]{:S(2)}) collective-permute-start(bf16[128,3072]{1,0:T(8,128)(2,1)S(1)} %bitcast.11), channel_id=1, source_target_pairs={{0,16},{1,17},{2,18},{3,19},{12,28},{13,29},{14,30},{15,31},{16,0}... | collective-permute-start | bytes 2359304 | tf_op jit(solution)/shard_map/ppermute | solution.py:750
  17.1 2.5 %collective-permute-start.2 = (bf16[32,4096]{1,0:T(8,128)(2,1)S(1)}, bf16[32,4096]{1,0:T(8,128)(2,1)S(1)}, u32[]{:S(2)}, u32[]{:S(2)}) collective-permute-start(bf16[32,4096]{1,0:T(8,128)(2,1)S(1)} %shard_map.158.n0_ref), channel_id=1, source_target_pairs={{0,8},{8,0},{16,24},{24,16},{1,9},{9,1},{17,25},{25,17},{2,10},{10... | collective-permute-start | bytes 786440 | tf_op jit(solution)/shard_map/ppermute | solution.py:732
  18.5 1.5 %collective-permute-start.3 = (bf16[32,4096]{1,0:T(8,128)(2,1)S(1)}, bf16[32,4096]{1,0:T(8,128)(2,1)S(1)}, u32[]{:S(2)}, u32[]{:S(2)}) collective-permute-start(bf16[32,4096]{1,0:T(8,128)(2,1)S(1)} %collective-permute-done.n2_ref), channel_id=1, source_target_pairs={{0,8},{8,0},{16,24},{24,16},{1,9},{9,1},{17,25},{25,17},{2,10},{10... | collective-permute-start | bytes 786440 | tf_op jit(solution)/shard_map/ppermute | solution.py:732
  18.6 14.5 %collective-permute-start.4 = (bf16[128,3072]{1,0:T(8,128)(2,1)S(1)}, bf16[128,3072]{1,0:T(8,128)(2,1)}, u32[]{:S(2)}, u32[]{:S(2)}) collective-permute-start(bf16[128,3072]{1,0:T(8,128)(2,1)S(1)} %bitcast.12), channel_id=1, source_target_pairs={{0,8},{8,0},{16,24},{24,16},{1,9},{9,1},{17,25},{25,17},{2,10},{10... | collective-permute-start | bytes 2359304 | tf_op jit(solution)/shard_map/ppermute | solution.py:732
  24.9 18.0 %all-to-all-start = ((bf16[4,2,32,768]{3,2,1,0:T(8,128)(2,1)}), bf16[4,2,32,768]{3,2,1,0:T(8,128)(2,1)S(1)}, u32[]{:S(2)}, u32[]{:S(2)}) async-start(bf16[4,2,32,768]{3,2,1,0:T(8,128)(2,1)} %shard_map.159), calls=%async_computation | async-start | bytes 786432 | tf_op jit(solution)/shard_map/all_to_all | solution.py:783
  28.4 18.5 %collective-permute-start.10 = (bf16[128,3072]{1,0:T(8,128)(2,1)S(1)}, bf16[128,3072]{1,0:T(8,128)(2,1)S(1)}, u32[]{:S(2)}, u32[]{:S(2)}) collective-permute-start(bf16[128,3072]{1,0:T(8,128)(2,1)S(1)} %collective-permute-done.9.refs_0_), channel_id=1, source_target_pairs={{0,16},{1,17},{2,18},{3,19},{12,28},{13,29},{14,30},{15,31},{16,0}... | collective-permute-start | bytes 2359304 | tf_op jit(solution)/shard_map/ppermute | solution.py:750
  32.4 1.5 %collective-permute-start.8 = (bf16[32,3072]{1,0:T(8,128)(2,1)S(1)}, bf16[32,3072]{1,0:T(8,128)(2,1)S(1)}, u32[]{:S(2)}, u32[]{:S(2)}) collective-permute-start(bf16[32,3072]{1,0:T(8,128)(2,1)S(1)} %get-tuple-element.44), channel_id=1, source_target_pairs={{0,8},{8,0},{16,24},{24,16},{1,9},{9,1},{17,25},{25,17},{2,10},{10... | collective-permute-start | bytes 589832 | tf_op jit(solution)/shard_map/ppermute | solution.py:732
  32.4 1.7 %collective-permute-start.7 = (bf16[32,3072]{1,0:T(8,128)(2,1)S(1)}, bf16[32,3072]{1,0:T(8,128)(2,1)S(1)}, u32[]{:S(2)}, u32[]{:S(2)}) collective-permute-start(bf16[32,3072]{1,0:T(8,128)(2,1)S(1)} %get-tuple-element.45), channel_id=1, source_target_pairs={{0,8},{8,0},{16,24},{24,16},{1,9},{9,1},{17,25},{25,17},{2,10},{10... | collective-permute-start | bytes 589832 | tf_op jit(solution)/shard_map/ppermute | solution.py:732
  33.0 1.7 %collective-permute-start.5 = (bf16[32,3072]{1,0:T(8,128)(2,1)S(1)}, bf16[32,3072]{1,0:T(8,128)(2,1)S(1)}, u32[]{:S(2)}, u32[]{:S(2)}) collective-permute-start(bf16[32,3072]{1,0:T(8,128)(2,1)S(1)} %get-tuple-element.47), channel_id=1, source_target_pairs={{0,8},{8,0},{16,24},{24,16},{1,9},{9,1},{17,25},{25,17},{2,10},{10... | collective-permute-start | bytes 589832 | tf_op jit(solution)/shard_map/ppermute | solution.py:732
  33.9 13.7 %collective-permute-start.11 = (bf16[128,3072]{1,0:T(8,128)(2,1)S(1)}, bf16[128,3072]{1,0:T(8,128)(2,1)}, u32[]{:S(2)}, u32[]{:S(2)}) collective-permute-start(bf16[128,3072]{1,0:T(8,128)(2,1)S(1)} %collective-permute-done.9.refs_0_), channel_id=1, source_target_pairs={{0,8},{8,0},{16,24},{24,16},{1,9},{9,1},{17,25},{25,17},{2,10},{10... | collective-permute-start | bytes 2359304 | tf_op jit(solution)/shard_map/ppermute | solution.py:732
  42.9 4.7 %collective-permute-start.14 = (bf16[4,2,32,768]{3,2,1,0:T(8,128)(2,1)S(1)}, bf16[4,2,32,768]{3,2,1,0:T(8,128)(2,1)S(1)}, u32[]{:S(2)}, u32[]{:S(2)}) collective-permute-start(bf16[4,2,32,768]{3,2,1,0:T(8,128)(2,1)S(1)} %all-to-all-done.refs_5_), channel_id=1, source_target_pairs={{0,8},{8,0},{16,24},{24,16},{1,9},{9,1},{17,25},{25,17},{2,10},{10... | collective-permute-start | bytes 1179656 | tf_op jit(solution)/shard_map/ppermute | solution.py:732
  43.1 16.5 %all-to-all-start.1 = ((bf16[4,256,384]{2,1,0:T(8,128)(2,1)}), bf16[4,256,384]{2,1,0:T(8,128)(2,1)S(1)}, u32[]{:S(2)}, u32[]{:S(2)}) async-start(bf16[4,256,384]{2,1,0:T(8,128)(2,1)} %shard_map.160), calls=%async_computation.1 | async-start | bytes 1572864 | tf_op jit(solution)/shard_map/all_to_all | solution.py:754
  47.0 1.8 %collective-permute-start.13 = (bf16[64,3072]{1,0:T(8,128)(2,1)S(1)}, bf16[64,3072]{1,0:T(8,128)(2,1)S(1)}, u32[]{:S(2)}, u32[]{:S(2)}) collective-permute-start(bf16[64,3072]{1,0:T(8,128)(2,1)S(1)} %get-tuple-element.42), channel_id=1, source_target_pairs={{0,8},{8,0},{16,24},{24,16},{1,9},{9,1},{17,25},{25,17},{2,10},{10... | collective-permute-start | bytes 1179656 | tf_op jit(solution)/shard_map/ppermute | solution.py:732
  47.1 2.3 %collective-permute-start.12 = (bf16[64,3072]{1,0:T(8,128)(2,1)S(1)}, bf16[64,3072]{1,0:T(8,128)(2,1)S(1)}, u32[]{:S(2)}, u32[]{:S(2)}) collective-permute-start(bf16[64,3072]{1,0:T(8,128)(2,1)S(1)} %get-tuple-element.43), channel_id=1, source_target_pairs={{0,8},{8,0},{16,24},{24,16},{1,9},{9,1},{17,25},{25,17},{2,10},{10... | collective-permute-start | bytes 1179656 | tf_op jit(solution)/shard_map/ppermute | solution.py:732
  88.3 15.3 %all-to-all-start.3 = ((bf16[8,192,128]{2,1,0:T(8,128)(2,1)}), bf16[8,192,128]{2,1,0:T(8,128)(2,1)S(1)}, u32[]{:S(2)}, u32[]{:S(2)}) async-start(bf16[8,192,128]{2,1,0:T(8,128)(2,1)} %shard_map.162), calls=%async_computation.3 | async-start | bytes 786432 | tf_op jit(solution)/shard_map/all_to_all | solution.py:738
  105.4 4.4 %collective-permute-start.15 = (bf16[192,3072]{1,0:T(8,128)(2,1)}, bf16[192,3072]{1,0:T(8,128)(2,1)}, u32[]{:S(2)}, u32[]{:S(2)}) collective-permute-start(bf16[192,3072]{1,0:T(8,128)(2,1)} %shard_map.164), channel_id=1, source_target_pairs={{0,8},{8,0},{16,24},{24,16},{1,9},{9,1},{17,25},{25,17},{2,10},{10... | collective-permute-start | bytes 3538952 | tf_op jit(solution)/shard_map/ppermute | solution.py:732
  105.4 25.3 %all-to-all-start.4 = ((bf16[8,384,128]{2,1,0:T(8,128)(2,1)}), bf16[8,384,128]{2,1,0:T(8,128)(2,1)}, u32[]{:S(2)}, u32[]{:S(2)}) async-start(bf16[8,384,128]{2,1,0:T(8,128)(2,1)} %shard_map.163), calls=%async_computation.4 | async-start | bytes 1572864 | tf_op jit(solution)/shard_map/all_to_all | solution.py:738
  113.0 28.7 %collective-permute-start.20 = (bf16[192,3072]{1,0:T(8,128)(2,1)}, bf16[192,3072]{1,0:T(8,128)(2,1)}, u32[]{:S(2)}, u32[]{:S(2)}) collective-permute-start(bf16[192,3072]{1,0:T(8,128)(2,1)} %shard_map.165), channel_id=1, source_target_pairs={{0,16},{8,24},{16,0},{24,8},{1,17},{9,25},{17,1},{25,9},{2,18},{10... | collective-permute-start | bytes 3538952 | tf_op jit(solution)/shard_map/ppermute | solution.py:735
  132.7 3.2 %collective-permute-start.16 = (bf16[64,3072]{1,0:T(8,128)(2,1)S(1)}, bf16[64,3072]{1,0:T(8,128)(2,1)S(1)}, u32[]{:S(2)}, u32[]{:S(2)}) collective-permute-start(bf16[64,3072]{1,0:T(8,128)(2,1)S(1)} %get-tuple-element.36), channel_id=1, source_target_pairs={{0,8},{8,0},{16,24},{24,16},{1,9},{9,1},{17,25},{25,17},{2,10},{10... | collective-permute-start | bytes 1179656 | tf_op jit(solution)/shard_map/ppermute | solution.py:732
  132.8 3.1 %collective-permute-start.17 = (bf16[64,3072]{1,0:T(8,128)(2,1)S(1)}, bf16[64,3072]{1,0:T(8,128)(2,1)S(1)}, u32[]{:S(2)}, u32[]{:S(2)}) collective-permute-start(bf16[64,3072]{1,0:T(8,128)(2,1)S(1)} %get-tuple-element.37), channel_id=1, source_target_pairs={{0,8},{8,0},{16,24},{24,16},{1,9},{9,1},{17,25},{25,17},{2,10},{10... | collective-permute-start | bytes 1179656 | tf_op jit(solution)/shard_map/ppermute | solution.py:732
  133.3 2.6 %collective-permute-start.18 = (bf16[64,3072]{1,0:T(8,128)(2,1)S(1)}, bf16[64,3072]{1,0:T(8,128)(2,1)S(1)}, u32[]{:S(2)}, u32[]{:S(2)}) collective-permute-start(bf16[64,3072]{1,0:T(8,128)(2,1)S(1)} %get-tuple-element.38), channel_id=1, source_target_pairs={{0,8},{8,0},{16,24},{24,16},{1,9},{9,1},{17,25},{25,17},{2,10},{10... | collective-permute-start | bytes 1179656 | tf_op jit(solution)/shard_map/ppermute | solution.py:732
  133.4 2.5 %collective-permute-start.19 = (bf16[64,1536]{1,0:T(8,128)(2,1)S(1)}, bf16[64,1536]{1,0:T(8,128)(2,1)S(1)}, u32[]{:S(2)}, u32[]{:S(2)}) collective-permute-start(bf16[64,1536]{1,0:T(8,128)(2,1)S(1)} %get-tuple-element.39), channel_id=1, source_target_pairs={{0,8},{8,0},{16,24},{24,16},{1,9},{9,1},{17,25},{25,17},{2,10},{10... | collective-permute-start | bytes 589832 | tf_op jit(solution)/shard_map/ppermute | solution.py:732
  (10 other events, 129.5 us)
